TPU v7x, 32 devices: a whole 2x2x4 slice. The times are simulated.
32 devices in a mesh: gz: 4 (over y, core), gx: 2 (over x), gy: 4 (over z).
Axes of the slice: x: 2, y: 2, z: 4, core: 2. Of those that a mesh axis runs over, the one named last changes fastest.
Arguments:
- initial_field: float32 [8, 256, 512], P('gz', 'gx', 'gy'), may hold values from -6 to 6
- source_term: float32 [8, 256, 512], P('gz', 'gx', 'gy'), may hold values from -48 to 48
- block_inverse: float32 [256, 512, 128], P('gx', 'gy'), may hold values from -0.1 to 0.1
Outputs:
- smoothed: float32 [8, 256, 512], P('gz', 'gx', 'gy')
All inputs are finite; a program needn't handle non-finite values.
Results may differ from a plain program's by a relative error of at most 0.00013.
Values sent between devices are 32-bit elements; how exact they have to be, the bound alone decides.
No kernel may reach another device: no remote copies, remote signals or barrier semaphores. Data moves between devices by JAX's collectives and lax.ppermute only.
A program may use at most 64 MiB of HBM per device.

v0:
```python
import jax
import jax.numpy as jnp
from jax import lax
from jax.sharding import PartitionSpec as P

exact_mode = lax.Precision.HIGHEST


def extended_2(cells, sides, width):
    for axis, dim in sides:
        count = lax.axis_size(axis)
        ends = count - 1
        head = lax.slice_in_dim(cells, 0, width, axis=dim)
        tail = lax.slice_in_dim(cells, cells.shape[dim] - width, cells.shape[dim], axis=dim)
        cells = jnp.concatenate(
            [
                lax.ppermute(tail, axis, [(i, (i + 1) % count) for i in range(ends)]),
                cells,
                lax.ppermute(head, axis, [((i + 1) % count, i) for i in range(ends)]),
            ],
            axis=dim,
        )
    return cells


def passed_along(value, axis, steps):
    count = lax.axis_size(axis)
    first, last = (max(0, -steps), min(count, count - steps))
    return lax.ppermute(value, axis, [(source, source + steps) for source in range(first, last)])


def box_sum(extended):
    row_sums = extended[:-2] + extended[1:-1] + extended[2:]
    return row_sums[:, :-2] + row_sums[:, 1:-1] + row_sums[:, 2:]


def relax_plane(under_ext, current, over_ext, source_plane, inverse_rows):
    neighbours = box_sum(under_ext) + box_sum(current) + box_sum(over_ext)
    interior = current[1:-1, 1:-1]
    residual = source_plane - (27.0 * interior - neighbours)
    return interior + jnp.einsum("xij,xj->xi", inverse_rows, residual, precision=exact_mode)


def add_rim(plane):
    return extended_2(plane, (("gx", 0), ("gy", 1)), 1)


def run_chain(initial_field, source_term, block_inverse):
    planes_dev = initial_field.shape[0]
    chain_len = lax.axis_size("gz")
    position = lax.axis_index("gz")

    def relax_here(under_ext, current, over_ext, source_plane):
        return relax_plane(under_ext, current, over_ext, source_plane, block_inverse)

    def keep_plane(under_ext, current, over_ext, source_plane):
        return current[1:-1, 1:-1]

    old_ext = extended_2(initial_field, (("gx", 1), ("gy", 2)), 1)
    over_slab = passed_along(old_ext[0], "gz", -1)
    zero_ext = jnp.zeros_like(old_ext[0])

    def forward_section(section_num, state_now):
        fwd_ext, below_keep = state_now
        active = section_num == position
        incoming = passed_along(fwd_ext[planes_dev - 1, 1:-1, 1:-1], "gz", 1)
        under_ext = add_rim(incoming)
        below_keep = jnp.where(active, under_ext, below_keep)
        planes = []
        lower_ext = under_ext
        for j in range(planes_dev):
            upper_ext = fwd_ext[j + 1] if j + 1 < planes_dev else over_slab
            fresh = lax.cond(
                active, relax_here, keep_plane, lower_ext, fwd_ext[j], upper_ext, source_term[j]
            )
            fresh_ext = jnp.where(active, add_rim(fresh), fwd_ext[j])
            planes.append(fresh_ext)
            lower_ext = fresh_ext
        return (jnp.stack(planes), below_keep)

    fwd_ext, below_keep = lax.fori_loop(0, chain_len, forward_section, (old_ext, zero_ext))

    def backward_section(section_num, bwd_ext):
        active = section_num == chain_len - 1 - position
        incoming = passed_along(bwd_ext[0, 1:-1, 1:-1], "gz", -1)
        over_ext = add_rim(incoming)
        planes = [None] * planes_dev
        upper_ext = over_ext
        for j in reversed(range(planes_dev)):
            lower_ext = fwd_ext[j - 1] if j > 0 else below_keep
            fresh = lax.cond(
                active, relax_here, keep_plane, lower_ext, bwd_ext[j], upper_ext, source_term[j]
            )
            if j > 0:
                fresh_ext = jnp.where(active, add_rim(fresh), bwd_ext[j])
            else:
                fresh_ext = jnp.where(active, jnp.pad(fresh, 1), bwd_ext[j])
            planes[j] = fresh_ext
            upper_ext = fresh_ext
        return jnp.stack(planes)

    bwd_ext = lax.fori_loop(0, chain_len, backward_section, fwd_ext)
    return bwd_ext[:, 1:-1, 1:-1]


def body(initial_field, source_term, block_inverse):
    return run_chain(initial_field, source_term, block_inverse)


def solution(mesh):
    placed = (P("gz", "gx", "gy"), P("gz", "gx", "gy"), P("gx", "gy", None))
    return jax.shard_map(
        body, mesh=mesh, in_specs=placed, out_specs=P("gz", "gx", "gy"), check_vma=False
    )
```

profile of v0, /device:TPU:0, one launch (start us, length us, event | category | flops | bytes accessed | tf_op | source)
XLA Modules:
  0.0 611.9 jit_solution(16239197521852340067)
XLA Ops:
  0.7 4.8 collective-permute-start.22
  26.9 260.1 %while.32 = (s32[]{:T(128)}, f32[2,130,130]{2,1,0:T(8,128)S(1)}, f32[130,130]{1,0:T(8,128)S(1)}, s32[]{:T(128)}, f32[2,128,128]{2,1,0:T(8,128)}, /*index=5*/f32[...) while((s32[]{:T(128)}, f32[2,130,130]{2,1,0:T(8,128)S(1)}, ...), condition=%wide.region_5.6_spmd.clone, body=%wide.region_0.5_spmd.clone.sunk | while | flops 51345488 | bytes 23155080 | solution.py:81
  26.9 4.9 collective-permute-start.9
  47.9 16.6 %conditional.12 = (f32[128,128]{1,0:T(8,128)S(1)}) conditional(s32[]{:T(128)} %convert_element_type.31, f32[130,130]{1,0:T(8,128)S(1)} %get-tuple-element.664, (f32[130,130]{1,0:T(8,128)S(1)}, f32[2,128,128]{2,1,0:T(8,128)}, f32[130,130]{1,0:T(8,128)S(1)}, f32[130,130]{1,0:T(8,128)S(1)}, f32[128,128,128]{2,1,0:T(8,128)}) %tuple.176), branch_computations={%region_1.1_spmd, %region_2.2_spmd} | conditional | flops 25462272 | bytes 10301448 | solution.py:73
  49.1 15.4 %fusion.31 = f32[128,1,128]{2,1,0:T(1,128)S(1)} fusion(f32[128,128,1]{1,2,0:T(1,128)S(1)} %bitcast.104, f32[128,128,128]{2,1,0:T(8,128)} %get-tuple-element.392), kind=kOutput, calls=%fused_computation.98 | convolution fusion | flops 25165824 | bytes 8519680 | tf_op jit(solution)/shard_map/while/body/eval_jaxpr/cond/branch_1_fun/xij,xj->xi/dot_general | solution.py:41
  73.1 4.9 collective-permute-start.17
  80.1 16.7 %conditional.13 = (f32[128,128]{1,0:T(8,128)S(1)}) conditional(s32[]{:T(128)} %convert_element_type.31, f32[130,130]{1,0:T(8,128)S(1)} %get-tuple-element.670, (f32[130,130]{1,0:T(8,128)S(1)}, f32[2,128,128]{2,1,0:T(8,128)}, pred[130,130]{1,0:T(8,128)(4,1)S(1)}, f32[130,130]{1,0:T(8,128)S(1)}, f32[130,130]{1,0:T(8,128)S(1)}, ...), branch_computations={%region_3.3_spmd, %region_4.4_spmd} | conditional | flops 25479172 | bytes 10521148 | solution.py:73
  81.3 15.4 %fusion.32 = f32[128,1,128]{2,1,0:T(1,128)S(1)} fusion(f32[128,128,1]{1,2,0:T(1,128)S(1)} %bitcast.105, f32[128,128,128]{2,1,0:T(8,128)} %get-tuple-element.399), kind=kOutput, calls=%fused_computation.99 | convolution fusion | flops 25165824 | bytes 8519680 | tf_op jit(solution)/shard_map/while/body/eval_jaxpr/cond/branch_1_fun/xij,xj->xi/dot_general | solution.py:41
  105.3 4.9 collective-permute-start.21
  123.1 4.9 collective-permute-start.13
  138.8 4.9 collective-permute-start.17
  154.4 4.9 collective-permute-start.21
  161.5 28.9 %collective-permute-start.9 = (f32[128,128]{1,0:T(8,128)S(1)}, f32[128,128]{1,0:T(8,128)S(1)}, u32[]{:S(2)}, u32[]{:S(2)}) collective-permute-start(f32[128,128]{1,0:T(8,128)S(1)} %slice_bitcast_fusion.16), channel_id=1, source_target_pairs={{0,8},{8,16},{16,24},{1,9},{9,17},{17,25},{2,10},{10,18},{18,26},{... | collective-permute-start | bytes 196616 | tf_op jit(solution)/shard_map/while/body/eval_jaxpr/ppermute | solution.py:29
  215.2 4.9 collective-permute-start.17
  230.8 4.9 collective-permute-start.21
  248.7 4.9 collective-permute-start.13
  264.3 4.9 collective-permute-start.17
  279.9 4.9 collective-permute-start.21
  287.0 324.1 %while.31 = (s32[]{:T(128)}, f32[2,130,130]{2,1,0:T(8,128)S(1)}, s32[]{:T(128)}, f32[2,128,128]{2,1,0:T(8,128)}, f32[2,130,130]{2,1,0:T(8,128)S(1)}, /*index=5*/...) while((s32[]{:T(128)}, f32[2,130,130]{2,1,0:T(8,128)S(1)}, s32[]{:T(128)}, ...), condition=%wide.region_11.12_spmd, body=%wide.region_6.11_spmd.sunk | while | flops 51244608 | bytes 22940776 | solution.py:102
  288.6 31.8 %collective-permute-done = f32[128,128]{1,0:T(8,128)S(1)} collective-permute-done((f32[128,128]{1,0:T(8,128)S(1)}, f32[128,128]{1,0:T(8,128)S(1)}, u32[]{:S(2)}, u32[]{:S(2)}) %collective-permute-start) | collective-permute-done | bytes 65568 | tf_op jit(solution)/shard_map/while/body/eval_jaxpr/ppermute | solution.py:29
  328.9 4.6 collective-permute-start.4
  344.2 4.9 collective-permute-start.8
  353.0 7.5 %collective-permute-done = f32[128,128]{1,0:T(8,128)S(1)} collective-permute-done((f32[128,128]{1,0:T(8,128)S(1)}, f32[128,128]{1,0:T(8,128)S(1)}, u32[]{:S(2)}, u32[]{:S(2)}) %collective-permute-start) | collective-permute-done | bytes 65568 | tf_op jit(solution)/shard_map/while/body/eval_jaxpr/ppermute | solution.py:29
  384.3 4.9 collective-permute-start.8
  393.1 24.9 %collective-permute-done = f32[128,128]{1,0:T(8,128)S(1)} collective-permute-done((f32[128,128]{1,0:T(8,128)S(1)}, f32[128,128]{1,0:T(8,128)S(1)}, u32[]{:S(2)}, u32[]{:S(2)}) %collective-permute-start) | collective-permute-done | bytes 65568 | tf_op jit(solution)/shard_map/while/body/eval_jaxpr/ppermute | solution.py:29
  441.8 4.9 collective-permute-start.8
  450.5 96.2 %collective-permute-done = f32[128,128]{1,0:T(8,128)S(1)} collective-permute-done((f32[128,128]{1,0:T(8,128)S(1)}, f32[128,128]{1,0:T(8,128)S(1)}, u32[]{:S(2)}, u32[]{:S(2)}) %collective-permute-start) | collective-permute-done | bytes 65568 | tf_op jit(solution)/shard_map/while/body/eval_jaxpr/ppermute | solution.py:29
  562.0 16.6 %conditional.10 = (f32[128,128]{1,0:T(8,128)S(1)}) conditional(s32[]{:T(128)} %convert_element_type.30, f32[130,130]{1,0:T(8,128)S(1)} %slice_bitcast_fusion.12, (f32[130,130]{1,0:T(8,128)S(1)}, f32[2,128,128]{2,1,0:T(8,128)}, f32[2,130,130]{2,1,0:T(8,128)S(1)}, f32[130,130]{1,0:T(8,128)S(1)}, f32[128,128,128]{2,1,0:T(8,128)}) %tuple.162), branch_computations={%region_7.7_spmd, %region_8.8_spmd} | conditional | flops 25462272 | bytes 10301448 | solution.py:91
  563.1 15.4 %fusion.33 = f32[128,1,128]{2,1,0:T(1,128)S(1)} fusion(f32[128,128,1]{1,2,0:T(1,128)S(1)} %bitcast.106, f32[128,128,128]{2,1,0:T(8,128)} %get-tuple-element.412), kind=kOutput, calls=%fused_computation.100 | convolution fusion | flops 25165824 | bytes 8519680 | tf_op jit(solution)/shard_map/while/body/eval_jaxpr/cond/branch_1_fun/xij,xj->xi/dot_general | solution.py:41
  587.2 4.9 collective-permute-start.8
  594.3 16.8 %conditional.11 = (f32[130,130]{1,0:T(8,128)S(1)}) conditional(s32[]{:T(128)} %convert_element_type.30, f32[130,130]{1,0:T(8,128)S(1)} %get-tuple-element.656, (f32[130,130]{1,0:T(8,128)S(1)}, f32[2,128,128]{2,1,0:T(8,128)}, f32[130,130]{1,0:T(8,128)S(1)}, pred[130,130]{1,0:T(8,128)(4,1)S(1)}, f32[130,130]{1,0:T(8,128)S(1)}, ...), branch_computations={%region_9.9_spmd, %region_10.10_spmd} | conditional | flops 25479172 | bytes 10654288 | solution.py:91
  595.5 15.4 %fusion.34 = f32[128,1,128]{2,1,0:T(1,128)S(1)} fusion(f32[128,128,1]{1,2,0:T(1,128)S(1)} %bitcast.107, f32[128,128,128]{2,1,0:T(8,128)} %get-tuple-element.419), kind=kOutput, calls=%fused_computation.101 | convolution fusion | flops 25165824 | bytes 8519680 | tf_op jit(solution)/shard_map/while/body/eval_jaxpr/cond/branch_1_fun/xij,xj->xi/dot_general | solution.py:41
  (338 shorter events, 277.1 us)
Async XLA Ops:
  15.5 6.9 %collective-permute-start.25 = (f32[2,130,1]{2,1,0:T(8,128)S(1)}, f32[2,130,1]{2,1,0:T(8,128)S(1)}, u32[]{:S(2)}, u32[]{:S(2)}) collective-permute-start(f32[2,130,1]{2,1,0:T(8,128)S(1)} %get-tuple-element.529), channel_id=1, source_target_pairs={{1,0},{2,1},{3,2},{5,4},{6,5},{7,6},{9,8},{10,9},{11,10},{13,12},{... | collective-permute-start | bytes 3128 | tf_op jit(solution)/shard_map/ppermute | solution.py:19
  71.8 6.6 %collective-permute-start.16 = (f32[130,1]{1,0:T(8,128)S(1)}, f32[130,1]{1,0:T(8,128)S(1)}, u32[]{:S(2)}, u32[]{:S(2)}) collective-permute-start(f32[130,1]{1,0:T(8,128)S(1)} %get-tuple-element.674), channel_id=1, source_target_pairs={{1,0},{2,1},{3,2},{5,4},{6,5},{7,6},{9,8},{10,9},{11,10},{13,12},{... | collective-permute-start | bytes 1568 | tf_op jit(solution)/shard_map/while/body/eval_jaxpr/ppermute | solution.py:19
  73.1 6.8 %collective-permute-start.17 = (f32[130,1]{1,0:T(8,128)S(1)}, f32[130,1]{1,0:T(8,128)S(1)}, u32[]{:S(2)}, u32[]{:S(2)}) collective-permute-start(f32[130,1]{1,0:T(8,128)S(1)} %get-tuple-element.676), channel_id=1, source_target_pairs={{0,1},{1,2},{2,3},{4,5},{5,6},{6,7},{8,9},{9,10},{10,11},{12,13},{... | collective-permute-start | bytes 1568 | tf_op jit(solution)/shard_map/while/body/eval_jaxpr/ppermute | solution.py:17
  104.0 6.6 %collective-permute-start.20 = (f32[130,1]{1,0:T(8,128)S(1)}, f32[130,1]{1,0:T(8,128)S(1)}, u32[]{:S(2)}, u32[]{:S(2)}) collective-permute-start(f32[130,1]{1,0:T(8,128)S(1)} %get-tuple-element.680), channel_id=1, source_target_pairs={{1,0},{2,1},{3,2},{5,4},{6,5},{7,6},{9,8},{10,9},{11,10},{13,12},{... | collective-permute-start | bytes 1568 | tf_op jit(solution)/shard_map/while/body/eval_jaxpr/ppermute | solution.py:19
  105.3 6.8 %collective-permute-start.21 = (f32[130,1]{1,0:T(8,128)S(1)}, f32[130,1]{1,0:T(8,128)S(1)}, u32[]{:S(2)}, u32[]{:S(2)}) collective-permute-start(f32[130,1]{1,0:T(8,128)S(1)} %get-tuple-element.682), channel_id=1, source_target_pairs={{0,1},{1,2},{2,3},{4,5},{5,6},{6,7},{8,9},{9,10},{10,11},{12,13},{... | collective-permute-start | bytes 1568 | tf_op jit(solution)/shard_map/while/body/eval_jaxpr/ppermute | solution.py:17
  121.8 6.6 %collective-permute-start.12 = (f32[130,1]{1,0:T(8,128)S(1)}, f32[130,1]{1,0:T(8,128)S(1)}, u32[]{:S(2)}, u32[]{:S(2)}) collective-permute-start(f32[130,1]{1,0:T(8,128)S(1)} %get-tuple-element.667), channel_id=1, source_target_pairs={{1,0},{2,1},{3,2},{5,4},{6,5},{7,6},{9,8},{10,9},{11,10},{13,12},{... | collective-permute-start | bytes 1568 | tf_op jit(solution)/shard_map/while/body/eval_jaxpr/ppermute | solution.py:19
  123.1 6.8 %collective-permute-start.13 = (f32[130,1]{1,0:T(8,128)S(1)}, f32[130,1]{1,0:T(8,128)S(1)}, u32[]{:S(2)}, u32[]{:S(2)}) collective-permute-start(f32[130,1]{1,0:T(8,128)S(1)} %get-tuple-element.668), channel_id=1, source_target_pairs={{0,1},{1,2},{2,3},{4,5},{5,6},{6,7},{8,9},{9,10},{10,11},{12,13},{... | collective-permute-start | bytes 1568 | tf_op jit(solution)/shard_map/while/body/eval_jaxpr/ppermute | solution.py:17
  137.5 6.6 %collective-permute-start.16 = (f32[130,1]{1,0:T(8,128)S(1)}, f32[130,1]{1,0:T(8,128)S(1)}, u32[]{:S(2)}, u32[]{:S(2)}) collective-permute-start(f32[130,1]{1,0:T(8,128)S(1)} %get-tuple-element.674), channel_id=1, source_target_pairs={{1,0},{2,1},{3,2},{5,4},{6,5},{7,6},{9,8},{10,9},{11,10},{13,12},{... | collective-permute-start | bytes 1568 | tf_op jit(solution)/shard_map/while/body/eval_jaxpr/ppermute | solution.py:19
  138.8 6.8 %collective-permute-start.17 = (f32[130,1]{1,0:T(8,128)S(1)}, f32[130,1]{1,0:T(8,128)S(1)}, u32[]{:S(2)}, u32[]{:S(2)}) collective-permute-start(f32[130,1]{1,0:T(8,128)S(1)} %get-tuple-element.676), channel_id=1, source_target_pairs={{0,1},{1,2},{2,3},{4,5},{5,6},{6,7},{8,9},{9,10},{10,11},{12,13},{... | collective-permute-start | bytes 1568 | tf_op jit(solution)/shard_map/while/body/eval_jaxpr/ppermute | solution.py:17
  153.1 6.6 %collective-permute-start.20 = (f32[130,1]{1,0:T(8,128)S(1)}, f32[130,1]{1,0:T(8,128)S(1)}, u32[]{:S(2)}, u32[]{:S(2)}) collective-permute-start(f32[130,1]{1,0:T(8,128)S(1)} %get-tuple-element.680), channel_id=1, source_target_pairs={{1,0},{2,1},{3,2},{5,4},{6,5},{7,6},{9,8},{10,9},{11,10},{13,12},{... | collective-permute-start | bytes 1568 | tf_op jit(solution)/shard_map/while/body/eval_jaxpr/ppermute | solution.py:19
  154.4 6.8 %collective-permute-start.21 = (f32[130,1]{1,0:T(8,128)S(1)}, f32[130,1]{1,0:T(8,128)S(1)}, u32[]{:S(2)}, u32[]{:S(2)}) collective-permute-start(f32[130,1]{1,0:T(8,128)S(1)} %get-tuple-element.682), channel_id=1, source_target_pairs={{0,1},{1,2},{2,3},{4,5},{5,6},{6,7},{8,9},{9,10},{10,11},{12,13},{... | collective-permute-start | bytes 1568 | tf_op jit(solution)/shard_map/while/body/eval_jaxpr/ppermute | solution.py:17
  161.5 29.8 %collective-permute-start.9 = (f32[128,128]{1,0:T(8,128)S(1)}, f32[128,128]{1,0:T(8,128)S(1)}, u32[]{:S(2)}, u32[]{:S(2)}) collective-permute-start(f32[128,128]{1,0:T(8,128)S(1)} %slice_bitcast_fusion.16), channel_id=1, source_target_pairs={{0,8},{8,16},{16,24},{1,9},{9,17},{17,25},{2,10},{10,18},{18,26},{... | collective-permute-start | bytes 196616 | tf_op jit(solution)/shard_map/while/body/eval_jaxpr/ppermute | solution.py:29
  213.9 6.6 %collective-permute-start.16 = (f32[130,1]{1,0:T(8,128)S(1)}, f32[130,1]{1,0:T(8,128)S(1)}, u32[]{:S(2)}, u32[]{:S(2)}) collective-permute-start(f32[130,1]{1,0:T(8,128)S(1)} %get-tuple-element.674), channel_id=1, source_target_pairs={{1,0},{2,1},{3,2},{5,4},{6,5},{7,6},{9,8},{10,9},{11,10},{13,12},{... | collective-permute-start | bytes 1568 | tf_op jit(solution)/shard_map/while/body/eval_jaxpr/ppermute | solution.py:19
  215.2 6.8 %collective-permute-start.17 = (f32[130,1]{1,0:T(8,128)S(1)}, f32[130,1]{1,0:T(8,128)S(1)}, u32[]{:S(2)}, u32[]{:S(2)}) collective-permute-start(f32[130,1]{1,0:T(8,128)S(1)} %get-tuple-element.676), channel_id=1, source_target_pairs={{0,1},{1,2},{2,3},{4,5},{5,6},{6,7},{8,9},{9,10},{10,11},{12,13},{... | collective-permute-start | bytes 1568 | tf_op jit(solution)/shard_map/while/body/eval_jaxpr/ppermute | solution.py:17
  229.5 6.6 %collective-permute-start.20 = (f32[130,1]{1,0:T(8,128)S(1)}, f32[130,1]{1,0:T(8,128)S(1)}, u32[]{:S(2)}, u32[]{:S(2)}) collective-permute-start(f32[130,1]{1,0:T(8,128)S(1)} %get-tuple-element.680), channel_id=1, source_target_pairs={{1,0},{2,1},{3,2},{5,4},{6,5},{7,6},{9,8},{10,9},{11,10},{13,12},{... | collective-permute-start | bytes 1568 | tf_op jit(solution)/shard_map/while/body/eval_jaxpr/ppermute | solution.py:19
  230.8 6.8 %collective-permute-start.21 = (f32[130,1]{1,0:T(8,128)S(1)}, f32[130,1]{1,0:T(8,128)S(1)}, u32[]{:S(2)}, u32[]{:S(2)}) collective-permute-start(f32[130,1]{1,0:T(8,128)S(1)} %get-tuple-element.682), channel_id=1, source_target_pairs={{0,1},{1,2},{2,3},{4,5},{5,6},{6,7},{8,9},{9,10},{10,11},{12,13},{... | collective-permute-start | bytes 1568 | tf_op jit(solution)/shard_map/while/body/eval_jaxpr/ppermute | solution.py:17
  247.4 6.6 %collective-permute-start.12 = (f32[130,1]{1,0:T(8,128)S(1)}, f32[130,1]{1,0:T(8,128)S(1)}, u32[]{:S(2)}, u32[]{:S(2)}) collective-permute-start(f32[130,1]{1,0:T(8,128)S(1)} %get-tuple-element.667), channel_id=1, source_target_pairs={{1,0},{2,1},{3,2},{5,4},{6,5},{7,6},{9,8},{10,9},{11,10},{13,12},{... | collective-permute-start | bytes 1568 | tf_op jit(solution)/shard_map/while/body/eval_jaxpr/ppermute | solution.py:19
  248.7 6.8 %collective-permute-start.13 = (f32[130,1]{1,0:T(8,128)S(1)}, f32[130,1]{1,0:T(8,128)S(1)}, u32[]{:S(2)}, u32[]{:S(2)}) collective-permute-start(f32[130,1]{1,0:T(8,128)S(1)} %get-tuple-element.668), channel_id=1, source_target_pairs={{0,1},{1,2},{2,3},{4,5},{5,6},{6,7},{8,9},{9,10},{10,11},{12,13},{... | collective-permute-start | bytes 1568 | tf_op jit(solution)/shard_map/while/body/eval_jaxpr/ppermute | solution.py:17
  263.0 6.6 %collective-permute-start.16 = (f32[130,1]{1,0:T(8,128)S(1)}, f32[130,1]{1,0:T(8,128)S(1)}, u32[]{:S(2)}, u32[]{:S(2)}) collective-permute-start(f32[130,1]{1,0:T(8,128)S(1)} %get-tuple-element.674), channel_id=1, source_target_pairs={{1,0},{2,1},{3,2},{5,4},{6,5},{7,6},{9,8},{10,9},{11,10},{13,12},{... | collective-permute-start | bytes 1568 | tf_op jit(solution)/shard_map/while/body/eval_jaxpr/ppermute | solution.py:19
  264.3 6.8 %collective-permute-start.17 = (f32[130,1]{1,0:T(8,128)S(1)}, f32[130,1]{1,0:T(8,128)S(1)}, u32[]{:S(2)}, u32[]{:S(2)}) collective-permute-start(f32[130,1]{1,0:T(8,128)S(1)} %get-tuple-element.676), channel_id=1, source_target_pairs={{0,1},{1,2},{2,3},{4,5},{5,6},{6,7},{8,9},{9,10},{10,11},{12,13},{... | collective-permute-start | bytes 1568 | tf_op jit(solution)/shard_map/while/body/eval_jaxpr/ppermute | solution.py:17
  278.6 6.6 %collective-permute-start.20 = (f32[130,1]{1,0:T(8,128)S(1)}, f32[130,1]{1,0:T(8,128)S(1)}, u32[]{:S(2)}, u32[]{:S(2)}) collective-permute-start(f32[130,1]{1,0:T(8,128)S(1)} %get-tuple-element.680), channel_id=1, source_target_pairs={{1,0},{2,1},{3,2},{5,4},{6,5},{7,6},{9,8},{10,9},{11,10},{13,12},{... | collective-permute-start | bytes 1568 | tf_op jit(solution)/shard_map/while/body/eval_jaxpr/ppermute | solution.py:19
  279.9 6.8 %collective-permute-start.21 = (f32[130,1]{1,0:T(8,128)S(1)}, f32[130,1]{1,0:T(8,128)S(1)}, u32[]{:S(2)}, u32[]{:S(2)}) collective-permute-start(f32[130,1]{1,0:T(8,128)S(1)} %get-tuple-element.682), channel_id=1, source_target_pairs={{0,1},{1,2},{2,3},{4,5},{5,6},{6,7},{8,9},{9,10},{10,11},{12,13},{... | collective-permute-start | bytes 1568 | tf_op jit(solution)/shard_map/while/body/eval_jaxpr/ppermute | solution.py:17
  287.3 33.1 %collective-permute-start = (f32[128,128]{1,0:T(8,128)S(1)}, f32[128,128]{1,0:T(8,128)S(1)}, u32[]{:S(2)}, u32[]{:S(2)}) collective-permute-start(f32[128,128]{1,0:T(8,128)S(1)} %slice_bitcast_fusion.13), channel_id=1, source_target_pairs={{8,0},{16,8},{24,16},{9,1},{17,9},{25,17},{10,2},{18,10},{26,18},{... | collective-permute-start | bytes 196616 | tf_op jit(solution)/shard_map/while/body/eval_jaxpr/ppermute | solution.py:29
  344.2 6.8 %collective-permute-start.8 = (f32[130,1]{1,0:T(8,128)S(1)}, f32[130,1]{1,0:T(8,128)S(1)}, u32[]{:S(2)}, u32[]{:S(2)}) collective-permute-start(f32[130,1]{1,0:T(8,128)S(1)} %get-tuple-element.654), channel_id=1, source_target_pairs={{0,1},{1,2},{2,3},{4,5},{5,6},{6,7},{8,9},{9,10},{10,11},{12,13},{... | collective-permute-start | bytes 1568 | tf_op jit(solution)/shard_map/while/body/eval_jaxpr/ppermute | solution.py:17
  351.7 8.8 %collective-permute-start = (f32[128,128]{1,0:T(8,128)S(1)}, f32[128,128]{1,0:T(8,128)S(1)}, u32[]{:S(2)}, u32[]{:S(2)}) collective-permute-start(f32[128,128]{1,0:T(8,128)S(1)} %slice_bitcast_fusion.13), channel_id=1, source_target_pairs={{8,0},{16,8},{24,16},{9,1},{17,9},{25,17},{10,2},{18,10},{26,18},{... | collective-permute-start | bytes 196616 | tf_op jit(solution)/shard_map/while/body/eval_jaxpr/ppermute | solution.py:29
  383.0 6.6 %collective-permute-start.7 = (f32[130,1]{1,0:T(8,128)S(1)}, f32[130,1]{1,0:T(8,128)S(1)}, u32[]{:S(2)}, u32[]{:S(2)}) collective-permute-start(f32[130,1]{1,0:T(8,128)S(1)} %get-tuple-element.652), channel_id=1, source_target_pairs={{1,0},{2,1},{3,2},{5,4},{6,5},{7,6},{9,8},{10,9},{11,10},{13,12},{... | collective-permute-start | bytes 1568 | tf_op jit(solution)/shard_map/while/body/eval_jaxpr/ppermute | solution.py:19
  384.3 6.8 %collective-permute-start.8 = (f32[130,1]{1,0:T(8,128)S(1)}, f32[130,1]{1,0:T(8,128)S(1)}, u32[]{:S(2)}, u32[]{:S(2)}) collective-permute-start(f32[130,1]{1,0:T(8,128)S(1)} %get-tuple-element.654), channel_id=1, source_target_pairs={{0,1},{1,2},{2,3},{4,5},{5,6},{6,7},{8,9},{9,10},{10,11},{12,13},{... | collective-permute-start | bytes 1568 | tf_op jit(solution)/shard_map/while/body/eval_jaxpr/ppermute | solution.py:17
  391.8 26.2 %collective-permute-start = (f32[128,128]{1,0:T(8,128)S(1)}, f32[128,128]{1,0:T(8,128)S(1)}, u32[]{:S(2)}, u32[]{:S(2)}) collective-permute-start(f32[128,128]{1,0:T(8,128)S(1)} %slice_bitcast_fusion.13), channel_id=1, source_target_pairs={{8,0},{16,8},{24,16},{9,1},{17,9},{25,17},{10,2},{18,10},{26,18},{... | collective-permute-start | bytes 196616 | tf_op jit(solution)/shard_map/while/body/eval_jaxpr/ppermute | solution.py:29
  440.5 6.6 %collective-permute-start.7 = (f32[130,1]{1,0:T(8,128)S(1)}, f32[130,1]{1,0:T(8,128)S(1)}, u32[]{:S(2)}, u32[]{:S(2)}) collective-permute-start(f32[130,1]{1,0:T(8,128)S(1)} %get-tuple-element.652), channel_id=1, source_target_pairs={{1,0},{2,1},{3,2},{5,4},{6,5},{7,6},{9,8},{10,9},{11,10},{13,12},{... | collective-permute-start | bytes 1568 | tf_op jit(solution)/shard_map/while/body/eval_jaxpr/ppermute | solution.py:19
  441.8 6.8 %collective-permute-start.8 = (f32[130,1]{1,0:T(8,128)S(1)}, f32[130,1]{1,0:T(8,128)S(1)}, u32[]{:S(2)}, u32[]{:S(2)}) collective-permute-start(f32[130,1]{1,0:T(8,128)S(1)} %get-tuple-element.654), channel_id=1, source_target_pairs={{0,1},{1,2},{2,3},{4,5},{5,6},{6,7},{8,9},{9,10},{10,11},{12,13},{... | collective-permute-start | bytes 1568 | tf_op jit(solution)/shard_map/while/body/eval_jaxpr/ppermute | solution.py:17
  449.2 97.5 %collective-permute-start = (f32[128,128]{1,0:T(8,128)S(1)}, f32[128,128]{1,0:T(8,128)S(1)}, u32[]{:S(2)}, u32[]{:S(2)}) collective-permute-start(f32[128,128]{1,0:T(8,128)S(1)} %slice_bitcast_fusion.13), channel_id=1, source_target_pairs={{8,0},{16,8},{24,16},{9,1},{17,9},{25,17},{10,2},{18,10},{26,18},{... | collective-permute-start | bytes 196616 | tf_op jit(solution)/shard_map/while/body/eval_jaxpr/ppermute | solution.py:29
  587.2 6.8 %collective-permute-start.8 = (f32[130,1]{1,0:T(8,128)S(1)}, f32[130,1]{1,0:T(8,128)S(1)}, u32[]{:S(2)}, u32[]{:S(2)}) collective-permute-start(f32[130,1]{1,0:T(8,128)S(1)} %get-tuple-element.654), channel_id=1, source_target_pairs={{0,1},{1,2},{2,3},{4,5},{5,6},{6,7},{8,9},{9,10},{10,11},{12,13},{... | collective-permute-start | bytes 1568 | tf_op jit(solution)/shard_map/while/body/eval_jaxpr/ppermute | solution.py:17
  (61 other events, 354.4 us)
where the time goes:
time: 615 us; the launch traced here: 612 us
  starting transfers between devices  292 us (47%)
  waiting for transfers between devices  239 us (39%)
  matrix products  61.5 us (10%)
  other arithmetic  10.7 us (2%)
    ppermute x42, starting transfers between devices, extended_2(): lax.ppermute(tail, axis, [(i, (i + 1) % count) for i in range(ends)])  195 us
    ppermute x9, waiting for transfers between devices, passed_along(): lax.ppermute(value, axis, [(source, source + steps) for source in range(f...  166 us
    dot_general x4, matrix products, relax_plane(): jnp.einsum('xij,xj->xi', inverse_rows, residual, precision=exact_mode)  61.5 us
    ppermute x42, waiting for transfers between devices, extended_2(): lax.ppermute(tail, axis, [(i, (i + 1) % count) for i in range(ends)])  58.1 us
    ppermute x42, starting transfers between devices, extended_2(): lax.ppermute(head, axis, [((i + 1) % count, i) for i in range(ends)])  54.1 us
    ppermute x9, starting transfers between devices, passed_along(): lax.ppermute(value, axis, [(source, source + steps) for source in range(f...  42.9 us
    ppermute x42, waiting for transfers between devices, extended_2(): lax.ppermute(head, axis, [((i + 1) % count, i) for i in range(ends)])  15.2 us
  transfers between devices with their start and end apart: 93, of which 72 were waited for; matrix products, arithmetic and copies ran while one was open for 0% of the time, Pallas kernels for 0%

commit v1 on v0

v1 whole, which is shorter than its diff:
```python
import functools
import math
import jax
import jax.numpy as jnp
from jax import lax
from jax.experimental import pallas as pl
from jax.experimental.pallas import tpu as pltpu
from jax.sharding import PartitionSpec as P

LANES = 128
HALF = 64
STEPS = 4
SPREAD = [(k, side, delta) for k in range(1, STEPS) for side in range(2) for delta in range(1 - k, k)]
PACK_ROWS = 8 * (-(-(STEPS + len(SPREAD)) // 8))
VMEM = pl.BlockSpec(memory_space=pltpu.VMEM)
ANY = pl.BlockSpec(memory_space=pl.ANY)
PARAMS = pltpu.CompilerParams(vmem_limit_bytes=40 * 1024 * 1024)


def low_lanes(rows):
    return lax.broadcasted_iota(jnp.int32, (rows, LANES), 1) < HALF


def swap_halves(a):
    return pltpu.roll(a, HALF, 1)


def from_line(a, delta):
    return a if delta == 0 else pltpu.roll(a, (-delta) % LANES, 1)


def sum_x(a):
    return a + pltpu.roll(a, 1, 1) + pltpu.roll(a, LANES - 1, 1)


def sum_y(a, halo=None):
    low = low_lanes(1)
    first = swap_halves(a[:8])[0:1]
    last = swap_halves(a[HALF - 8 :])[7:8]
    halo = jnp.zeros((1, LANES), jnp.float32) if halo is None else halo
    above = jnp.where(low, halo, last)
    below = jnp.where(low, first, halo)
    row = lax.broadcasted_iota(jnp.int32, a.shape, 0)
    up = jnp.where(row == 0, above, pltpu.roll(a, 1, 0))
    down = jnp.where(row == HALF - 1, below, pltpu.roll(a, HALF - 1, 0))
    return a + up + down


def spread(a):
    low = low_lanes(a.shape[0])
    swapped = swap_halves(a)
    return jnp.where(low, a, swapped), jnp.where(low, swapped, a)


def edges(a):
    return jnp.where(low_lanes(1), a[0:1], a[HALF - 1 : HALF])


def block(b_ref, j):
    return b_ref[pl.ds(pl.multiple_of(j * HALF, HALF), HALF), :]


def apply_blocks(b_ref, rhs, r_refs):
    count = len(rhs)
    for a, r_ref in zip(rhs, r_refs):
        r_ref[0:HALF, :], r_ref[HALF:LANES, :] = spread(a)
    unroll = 8 if count == 1 else 2

    def step(outer, totals):
        totals = list(totals)
        for u in range(unroll):
            j = outer * unroll + u
            rows = block(b_ref, j)
            for n in range(count):
                slot = n if count > 1 else u % 2
                totals[slot] = totals[slot] + rows * r_refs[n][pl.ds(j, 1), :]
        return tuple(totals)

    zero = jnp.zeros((HALF, LANES), jnp.float32)
    totals = lax.fori_loop(0, LANES // unroll, step, (zero,) * max(2, count))
    return [totals[0] + totals[1]] if count == 1 else list(totals)


def layout_kernel(own, axis, b_ref, ghost_ref, out_ref, window, sems):
    ghost = ghost_ref.shape[0] // LANES
    count = b_ref.shape[0] // LANES
    position = lax.axis_index(axis)
    chunk = math.gcd(own, ghost)
    size = chunk * LANES
    copies = []
    for c in range(HALF // chunk):
        start = position * own - ghost + c * chunk
        inside = jnp.logical_and(start >= 0, start < count)
        target = window.at[pl.ds(c * size, size)]
        here = jnp.clip(start, 0, count - chunk)
        beyond = jnp.clip(jnp.where(start < 0, start + ghost, start - count), 0, ghost - chunk)

        @pl.when(inside)
        def _(at=pl.multiple_of(here * LANES, LANES), target=target, c=c):
            pltpu.make_async_copy(b_ref.at[pl.ds(at, size)], target, sems.at[c]).start()

        @pl.when(jnp.logical_not(inside))
        def _(at=pl.multiple_of(beyond * LANES, LANES), target=target, c=c):
            pltpu.make_async_copy(ghost_ref.at[pl.ds(at, size)], target, sems.at[c]).start()

        copies.append(pltpu.make_async_copy(b_ref.at[pl.ds(0, size)], target, sems.at[c]))
    for copy in copies:
        copy.wait()

    def one(i, carry):
        top = window[pl.ds(i, HALF, stride=LANES), :]
        bottom = window[pl.ds(i + HALF, HALF, stride=LANES), :]
        out_ref[pl.ds(i, LANES, stride=HALF), :] = jnp.concatenate([top, bottom], axis=0).T
        return carry

    lax.fori_loop(0, HALF, one, 0)


def responses(b_ref, r_refs, pack_ref):
    low_all = low_lanes(LANES)
    edge_rows = jnp.where(
        low_all,
        b_ref[pl.ds(0, LANES, stride=HALF), :],
        b_ref[pl.ds(HALF - 1, LANES, stride=HALF), :],
    )
    firsts = [block(b_ref, 0), block(b_ref, LANES - 1)]
    shifted = [sum_y(a) for a in firsts]
    plan = [(side, delta) for side in range(2) for delta in (-1, 0, 1)]
    seconds = apply_blocks(b_ref, [from_line(shifted[side], delta) for side, delta in plan], r_refs)
    second = {key: value for key, value in zip(plan, seconds)}
    for n, (k, side, delta) in enumerate(SPREAD):
        if k == 1:
            row = edges(firsts[side])
        elif k == 2:
            row = edges(second[side, delta])
        else:
            parts = [
                from_line(second[side, delta - m], m) for m in (-1, 0, 1) if abs(delta - m) <= 1
            ]
            top, bottom = spread(sum_y(sum(parts[1:], parts[0])))
            row = jnp.sum(edge_rows[:HALF] * top + edge_rows[HALF:] * bottom, axis=0, keepdims=True)
        pack_ref[pl.ds(STEPS + n, 1), :] = row


def local_chain(steps, b_ref, rhs_ref, add_ref, state, r_refs, pack_ref, first_loc_ref):
    nz = rhs_ref.shape[0]
    if state is not None:
        pack_ref[0:1, :] = edges(state)
    for n, step in enumerate(steps[:-1]):
        z = step if step < nz else 2 * nz - 1 - step
        rhs = rhs_ref[z]
        if state is not None:
            rhs = rhs + sum_y(sum_x(state))
        (state,) = apply_blocks(b_ref, [rhs], r_refs)
        if step >= nz:
            state = state + add_ref[z]
        if n == 0:
            first_loc_ref[...] = state
        pack_ref[n + 1 : n + 2, :] = edges(state)


def gather_planes(axis, field_refs, v_ref, s_ref):
    position = lax.axis_index(axis)
    low = low_lanes(HALF)
    nz_local = field_refs[0].shape[1]
    for k, ref in enumerate(field_refs):
        base = jnp.bitwise_xor(position, k) * nz_local
        for p in range(nz_local):
            for kind, target in ((0, v_ref), (1, s_ref)):
                plane = ref[kind, p]
                turned = jnp.concatenate([plane, plane], axis=0).T
                target[base + p + 1 - kind] = jnp.where(low, turned[:HALF], turned[HALF:])


def first_kernel(axis, fields, *refs):
    field_refs = refs[:fields]
    b_ref, rhs_ref, loc_ref, pack_ref, v_ref, s_ref = refs[fields : fields + 6]
    r_refs = refs[fields + 6 :]
    nz = rhs_ref.shape[0]
    pack_ref[...] = jnp.zeros(pack_ref.shape, jnp.float32)
    responses(b_ref, r_refs, pack_ref)
    v_ref[0] = jnp.zeros((HALF, LANES), jnp.float32)
    v_ref[nz + 1] = jnp.zeros((HALF, LANES), jnp.float32)
    gather_planes(axis, field_refs, v_ref, s_ref)
    for z in range(nz):
        around = v_ref[z] + v_ref[z + 1] + v_ref[z + 2]
        rhs_ref[z] = s_ref[z] - 27.0 * v_ref[z + 1] + sum_y(sum_x(around))
        pack_ref[PACK_ROWS + z : PACK_ROWS + z + 1, :] = edges(around)
    local_chain(list(range(STEPS)), b_ref, rhs_ref, None, None, r_refs, pack_ref, loc_ref)


def halo_of(ends):
    swapped = swap_halves(ends)
    return sum_x(jnp.where(low_lanes(8), pltpu.roll(swapped, 1, 0), pltpu.roll(swapped, 7, 0)))


def lines_both(row):
    swapped = swap_halves(row)
    low = low_lanes(8)
    return jnp.where(low, row, swapped), jnp.where(low, swapped, row)


def complete_edges(first, gather, coef_ref, halo_ref, inject_ref):
    injected = []
    ends = None if first else gather[:, 0, :]
    for t in range(STEPS):
        halo = jnp.zeros((8, LANES), jnp.float32) if ends is None else halo_of(ends)
        halo_ref[t] = halo
        if first:
            halo = halo + halo_of(gather[:, PACK_ROWS + t, :])
        injected.append(lines_both(halo))
        if t == 0:
            inject_ref[0], inject_ref[1] = injected[0]
        if t < STEPS - 1:
            ends = gather[:, t + 1, :]
            for n, (k, side, delta) in enumerate(SPREAD):
                if k <= t + 1:
                    ends = ends + coef_ref[:, STEPS + n, :] * from_line(
                        injected[t + 1 - k][side], delta
                    )


def next_kernel(steps, later, first, peers, axis, ghost, *refs):
    refs = list(refs)

    def take(count):
        taken = refs[:count]
        del refs[:count]
        return taken

    packs = take(peers)
    b_ref, rhs_in, loc_in = take(3)
    coef_ref, add_in, state_in = (None, None, None) if first else take(3)
    last = steps is not None and steps[-1] == 2 * rhs_in.shape[0] - 1
    out_ref = take(1)[0] if last else None
    rhs_ref, add_ref, state_ref = take(3)
    loc_ref, pack_ref = take(2) if later else (None, None)
    coef_out = take(1)[0] if first else None
    gather, halo_ref, inject_ref, *r_refs = refs
    nz = rhs_in.shape[0]
    rows = packs[0].shape[0]
    position = lax.axis_index(axis)

    gather[...] = jnp.zeros(gather.shape, jnp.float32)
    for k in range(peers):
        gather[jnp.bitwise_xor(position, k)] = packs[k][...]
    if first:
        coef_out[...] = gather[:, :PACK_ROWS, :]
    rhs_ref[...] = rhs_in[...]
    if not first:
        add_ref[...] = add_in[...]
    complete_edges(first, gather, gather if first else coef_ref, halo_ref, inject_ref)
    own = pl.ds(position, 1)
    low = low_lanes(HALF)
    row_index = lax.broadcasted_iota(jnp.int32, (HALF, LANES), 0)
    if first:
        for z in range(nz):
            halo_ref[STEPS] = halo_of(gather[:, PACK_ROWS + z, :])
            halo = halo_ref[STEPS, own, :]
            at_edge = jnp.logical_or(
                jnp.logical_and(row_index == 0, low),
                jnp.logical_and(row_index == HALF - 1, jnp.logical_not(low)),
            )
            rhs_ref[z] = rhs_ref[z] + jnp.where(at_edge, halo, 0.0)

    state = None if first else state_in[...]
    for t, step in enumerate(steps):
        z = step if step < nz else 2 * nz - 1 - step
        if state is not None:
            around = sum_y(sum_x(state), halo_ref[t, own, :])
            if step < nz:
                rhs_ref[step - 1] = around - 27.0 * state
        if t == 0:
            left, right = inject_ref[0, own, :], inject_ref[1, own, :]
            state = loc_in[...] + block(b_ref, 0) * left + block(b_ref, LANES - 1) * right
        else:
            (state,) = apply_blocks(b_ref, [rhs_ref[z] + around], r_refs)
            if step >= nz:
                state = state + add_ref[z]
        add_ref[z] = 2.0 * state if step < nz else state
        if step == nz - 1:
            rhs_ref[z] = -27.0 * state
    state_ref[...] = state
    if later:
        pack_ref[...] = jnp.zeros(pack_ref.shape, jnp.float32)
        local_chain(later, b_ref, rhs_ref, add_ref, state, r_refs, pack_ref, loc_ref)
    if last:
        own_lines = HALF - 2 * ghost
        for z in range(nz):
            plane = add_ref[z]
            turned = jnp.concatenate([plane, swap_halves(plane)], axis=0).T
            out_ref[z] = turned[ghost : ghost + own_lines]


def local_kernel(steps, b_ref, rhs_ref, add_ref, state_ref, loc_ref, pack_ref, *r_refs):
    pack_ref[...] = jnp.zeros(pack_ref.shape, jnp.float32)
    local_chain(steps, b_ref, rhs_ref, add_ref, state_ref[...], r_refs, pack_ref, loc_ref)


def finish_kernel(axis, v_ref, *refs):
    parts, out_ref = refs[:-1], refs[-1]
    position = lax.axis_index(axis)
    lines = parts[0].shape[1]
    for k, part in enumerate(parts):
        at = pl.ds(pl.multiple_of(jnp.bitwise_xor(position, k) * lines, lines), lines)
        out_ref[:, at, :] = v_ref[:, at, :] + part[...]


def f32(*shape):
    return jax.ShapeDtypeStruct(shape, jnp.float32)


def call(kernel, ins, outs, scratch, name):
    return pl.pallas_call(
        kernel,
        out_shape=outs,
        in_specs=[VMEM] * len(ins),
        out_specs=[VMEM] * len(outs),
        scratch_shapes=scratch,
        compiler_params=PARAMS,
        name=name,
    )(*ins)


def to_peers(pieces, axis):
    count = lax.axis_size(axis)
    return [pieces[0]] + [
        lax.ppermute(pieces[k], axis, [(i, i ^ k) for i in range(count)]) for k in range(1, count)
    ]


def line_ghosts(cells, dim, width):
    count = lax.axis_size("gx")
    size = cells.shape[dim]
    head = lax.slice_in_dim(cells, 0, width, axis=dim)
    tail = lax.slice_in_dim(cells, size - width, size, axis=dim)
    if count == 2:
        at_first = lax.axis_index("gx") == 0
        other = lax.ppermute(jnp.where(at_first, tail, head), "gx", [(0, 1), (1, 0)])
        zero = jnp.zeros_like(other)
        return jnp.where(at_first, zero, other), jnp.where(at_first, other, zero)
    ups = [(i, i + 1) for i in range(count - 1)]
    downs = [(i + 1, i) for i in range(count - 1)]
    return lax.ppermute(tail, "gx", ups), lax.ppermute(head, "gx", downs)


def block_ghosts(blocks, own, width):
    groups, count = lax.axis_size("gz"), lax.axis_size("gx")
    size = blocks.shape[0]
    reach = -(-width // own)
    assert 2 * reach <= groups
    start = jnp.where(lax.axis_index("gz") < reach, size - width, 0)
    pairs = []
    for g in range(groups):
        for a in range(count - 1):
            if g < reach:
                pairs.append((g * count + a, g * count + a + 1))
            if groups - 1 - g < reach:
                pairs.append((g * count + a + 1, g * count + a))
    return lax.ppermute(lax.dynamic_slice_in_dim(blocks, start, width, 0), ("gz", "gx"), pairs)


def refresh_ghosts(planes, ghost):
    split = planes.reshape(planes.shape[0], HALF, 2, HALF)
    groups, count = lax.axis_size("gz"), lax.axis_size("gx")
    places = [g * count + x for x in range(count) for g in range(groups)]
    ups = list(zip(places[:-1], places[1:]))
    downs = list(zip(places[1:], places[:-1]))
    before = lax.ppermute(split[..., HALF - 2 * ghost : HALF - ghost], ("gz", "gx"), ups)
    after = lax.ppermute(split[..., ghost : 2 * ghost], ("gz", "gx"), downs)
    whole = jnp.concatenate([before, split[..., ghost : HALF - ghost], after], axis=-1)
    return whole.reshape(planes.shape)


def body(initial_field, source_term, block_inverse):
    groups, peers = lax.axis_size("gz"), lax.axis_size("gy")
    nz_local, lines, _ = initial_field.shape
    nz = nz_local * groups
    own = lines // groups
    ghost = (HALF - own) // 2
    assert block_inverse.shape[1:] == (LANES, LANES) and lines % groups == 0
    assert nz % STEPS == 0 and nz <= ghost and peers <= 4
    here = lax.axis_index("gz")

    rows = block_inverse.reshape(lines * LANES, LANES)
    beyond = block_ghosts(block_inverse, own, ghost).reshape(ghost * LANES, LANES)
    blocks = pl.pallas_call(
        functools.partial(layout_kernel, own, "gz"),
        out_shape=f32(LANES * HALF, LANES),
        in_specs=[ANY, ANY],
        out_specs=VMEM,
        scratch_shapes=[
            pltpu.VMEM((HALF * LANES, LANES), jnp.float32),
            pltpu.SemaphoreType.DMA((HALF // math.gcd(own, ghost),)),
        ],
        compiler_params=PARAMS,
        name="layout",
    )(rows, beyond)

    fields = jnp.stack([initial_field, source_term])
    before, after = line_ghosts(fields, 2, ghost)
    wide = jnp.concatenate([before, fields, after], axis=2)
    windows = [
        lax.dynamic_slice_in_dim(wide, jnp.bitwise_xor(here, k) * own, HALF, 2)
        for k in range(groups)
    ]
    fields_here = to_peers(windows, "gz")

    plane = pltpu.VMEM((LANES, LANES), jnp.float32)
    first_rows = PACK_ROWS + 8 * (-(-nz // 8))
    rhs, loc, pack = call(
        functools.partial(first_kernel, "gz", groups),
        [*fields_here, blocks],
        [f32(nz, HALF, LANES), f32(HALF, LANES), f32(first_rows, LANES)],
        [pltpu.VMEM((nz + 2, HALF, LANES), jnp.float32), pltpu.VMEM((nz, HALF, LANES), jnp.float32)]
        + [plane] * 6,
        "first_chain",
    )
    schedule = [list(range(a, a + STEPS)) for a in range(0, 2 * nz, STEPS)]
    coef = add = state = None
    for n, steps in enumerate(schedule):
        first = n == 0
        final = n + 1 == len(schedule)
        renew = steps[-1] == nz - 1 and 2 * nz > ghost
        later = None if final or renew else schedule[n + 1]
        packs = to_peers([pack] * peers, "gy")
        ins = [*packs, blocks, rhs, loc] + ([] if first else [coef, add, state])
        planes = f32(nz, HALF, LANES)
        outs = [f32(nz, own, LANES)] if final else []
        outs += [planes, planes, f32(HALF, LANES)]
        outs += [f32(HALF, LANES), f32(8, LANES)] if later else []
        outs += [f32(8, PACK_ROWS, LANES)] if first else []
        results = call(
            functools.partial(next_kernel, steps, later, first, peers, "gy", ghost),
            ins,
            outs,
            [
                pltpu.VMEM((8, pack.shape[0], LANES), jnp.float32),
                pltpu.VMEM((STEPS + 1, 8, LANES), jnp.float32),
                pltpu.VMEM((2, 8, LANES), jnp.float32),
                plane,
            ],
            "next_chain",
        )
        if final:
            change = results[0]
            break
        rhs, add, state = results[:3]
        if later:
            loc, pack = results[3:5]
        if first:
            coef = results[-1]
        if renew:
            renewed = refresh_ghosts(jnp.concatenate([rhs, add, state[None]]), ghost)
            rhs, add, state = renewed[:nz], renewed[nz : 2 * nz], renewed[2 * nz]
            loc, pack = call(
                functools.partial(local_kernel, schedule[n + 1]),
                [blocks, rhs, add, state],
                [f32(HALF, LANES), f32(8, LANES)],
                [plane],
                "local_chain",
            )

    sends = [
        lax.dynamic_slice_in_dim(change, jnp.bitwise_xor(here, k) * nz_local, nz_local, 0)
        for k in range(groups)
    ]
    parts = to_peers(sends, "gz")
    return call(
        functools.partial(finish_kernel, "gz"),
        [initial_field, *parts],
        [f32(*initial_field.shape)],
        [],
        "finish",
    )[0]


def solution(mesh):
    placed = (P("gz", "gx", "gy"), P("gz", "gx", "gy"), P("gx", "gy", None))
    return jax.shard_map(
        body, mesh=mesh, in_specs=placed, out_specs=P("gz", "gx", "gy"), check_vma=False
    )
```

time: 615 us -> 92.2 us (0.15)
  starting transfers between devices: 292 us -> 26.6 us
  waiting for transfers between devices: 239 us -> 23.6 us
  matrix products: 61.5 us -> 0 us
  Pallas kernels: 0 us -> 32.6 us
  other arithmetic: 10.7 us -> 1.78 us
    ppermute x93 -> x20, starting transfers between devices: 292 us -> 26.6 us  [the longest x18 21.7 us: to_peers(): lax.ppermute(pieces[k], axis, [(i, i ^ k) for i in range(count)])]
    ppermute x93 -> x20, waiting for transfers between devices: 239 us -> 23.6 us  [the longest x18 11.9 us: to_peers(): lax.ppermute(pieces[k], axis, [(i, i ^ k) for i in range(count)])]
    dot_general x4 -> x0, matrix products: 61.5 us -> none  [relax_plane(): jnp.einsum('xij,xj->xi', inverse_rows, residual, precision=exact_mode)]
    pallas_call x0 -> x7, Pallas kernels: none -> 32.6 us  [the longest x6 21.4 us: call(): pl.pallas_call(kernel, out_shape=outs, in_specs=[VMEM] * len(ins), out_sp...]
  transfers between devices with their start and end apart: 93 -> 20, of which waited for: 72 -> 11; matrix products, arithmetic and copies ran while one was open for 0% -> 2% of each run, Pallas kernels for 0% -> 12%
where the time goes in v1:
time: 92.2 us; the launch traced here: 91.8 us
  Pallas kernels  32.6 us (35%)
  starting transfers between devices  26.6 us (29%)
  waiting for transfers between devices  23.6 us (26%)
  local copies, waits for them, and re-layouts  6.93 us (8%)
  other arithmetic  1.78 us (2%)
    ppermute x18, starting transfers between devices, to_peers(): lax.ppermute(pieces[k], axis, [(i, i ^ k) for i in range(count)])  21.7 us
    pallas_call x6, Pallas kernels, call(): pl.pallas_call(kernel, out_shape=outs, in_specs=[VMEM] * len(ins), out_sp...  21.4 us
    ppermute x18, waiting for transfers between devices, to_peers(): lax.ppermute(pieces[k], axis, [(i, i ^ k) for i in range(count)])  11.9 us
    ppermute x1, waiting for transfers between devices, line_ghosts(): lax.ppermute(jnp.where(at_first, tail, head), 'gx', [(0, 1), (1, 0)])  11.7 us
    pallas_call x1, Pallas kernels, body(): pl.pallas_call(functools.partial(layout_kernel, own, 'gz'), out_shape=f32...  11.3 us
    unnamed x8, local copies, waits for them, and re-layouts  5.58 us
    ppermute x1, starting transfers between devices, block_ghosts(): lax.ppermute(lax.dynamic_slice_in_dim(blocks, start, width, 0), ('gz', 'g...  4.91 us
  transfers between devices with their start and end apart: 20, of which 11 were waited for; matrix products, arithmetic and copies ran while one was open for 2% of the time, Pallas kernels for 12%

profile of v1, /device:TPU:0, one launch (start us, length us, event | category | flops | bytes accessed | tf_op | source)
XLA Modules:
  0.0 91.8 jit_solution(1141986007277392478)
XLA Ops:
  0.0 1.3 %constant_dynamic-slice_fusion.4 = f32[16,128,128]{2,1,0:T(8,128)S(1)} fusion(f32[128,128,128]{2,1,0:T(8,128)} %param.5, s32[]{:T(128)S(6)} %select_n.53), kind=kLoop, calls=%fused_computation.9 | loop fusion | bytes 2097156 | tf_op jit(solution)/shard_map/dynamic_slice | solution.py:360
  1.3 4.9 %collective-permute-start.4 = (f32[16,128,128]{2,1,0:T(8,128)S(1)}, f32[16,128,128]{2,1,0:T(8,128)S(1)}, u32[]{:S(2)}, u32[]{:S(2)}) collective-permute-start(f32[16,128,128]{2,1,0:T(8,128)S(1)} %constant_dynamic-slice_fusion.4), channel_id=1, source_target_pairs={{0,4},{28,24},{1,5},{29,25},{2,6},{30,26},{3,7},{31,27}} | collective-permute-start | bytes 3145736 | tf_op jit(solution)/shard_map/ppermute | solution.py:360
  6.2 0.8 fusion
  7.1 11.7 %collective-permute-done = f32[2,2,16,128]{3,2,1,0:T(8,128)S(1)} collective-permute-done((f32[2,2,16,128]{3,2,1,0:T(8,128)S(1)}, f32[2,2,16,128]{3,2,1,0:T(8,128)S(1)}, u32[]{:S(2)}, u32[]{:S(2)}) %collective-permute-start) | collective-permute-done | bytes 32800 | tf_op jit(solution)/shard_map/ppermute | solution.py:339
  18.8 1.0 %pad_maximum_fusion = f32[2,2,160,128]{3,2,1,0:T(8,128)S(1)} fusion(f32[2,2,16,128]{3,2,1,0:T(8,128)S(1)} %get-tuple-element.54, f32[1,2,128,128]{3,2,1,0:T(8,128)} %bitcast.9, f32[1,2,128,128]{3,2,1,0:T(8,128)} %bitcast.6, f32[2,2,16,128]{3,2,1,0:T(8,128)S(1)} %get-tuple-element.53), kind=kLoop, calls=%fused_computation | loop fusion | flops 245760 | bytes 655360 | tf_op jit(solution)/shard_map/concatenate | solution.py:402
  19.9 1.2 %collective-permute-start.3 = (f32[2,2,64,128]{3,2,1,0:T(8,128)S(1)}, f32[2,2,64,128]{3,2,1,0:T(8,128)S(1)}, u32[]{:S(2)}, u32[]{:S(2)}) collective-permute-start(f32[2,2,64,128]{3,2,1,0:T(8,128)S(1)} %get-tuple-element.45), channel_id=1, source_target_pairs={{0,24},{8,16},{16,8},{24,0},{1,25},{9,17},{17,9},{25,1},{2,26},{10... | collective-permute-start | bytes 393224 | tf_op jit(solution)/shard_map/ppermute | solution.py:328
  21.8 3.4 %copy-done.2 = f32[128,128,128]{2,1,0:T(8,128)S(1)} copy-done((f32[128,128,128]{2,1,0:T(8,128)S(1)}, f32[128,128,128]{2,1,0:T(8,128)}, u32[]{:S(2)}) %copy-start.2) | copy-done | bytes 8388632
  25.2 11.3 %layout.1.refs_4_ = f32[8192,128]{1,0:T(8,128)S(1)} custom-call(f32[16384,128]{1,0:T(8,128)S(1)} %bitcast.4, f32[2048,128]{1,0:T(8,128)S(1)} %bitcast.7), custom_call_target="tpu_custom_call" | custom-call | tf_op jit(solution)/shard_map/layout/pallas_call | solution.py:387
  36.5 5.8 %first_chain.1 = (f32[8,64,128]{2,1,0:T(8,128)S(1)}, f32[64,128]{1,0:T(8,128)S(1)}, f32[32,128]{1,0:T(8,128)S(1)}) custom-call(f32[2,2,64,128]{3,2,1,0:T(8,128)S(1)} %get-tuple-element.48.refs_0_, f32[2,2,64,128]{3,2,1,0:T(8,128)S(1)} %collective-permute-done.1.refs_1_, f32[2,2,64,128]{3,2,1,0:T(8,128)S(1)} %collective-permute-done.2.refs_2_, ...), custom_call_target="tpu_custom_call" | custom-call | tf_op jit(solution)/shard_map/first_chain/pallas_call | solution.py:314
  42.3 3.7 %collective-permute-start.7 = (f32[32,128]{1,0:T(8,128)S(1)}, f32[32,128]{1,0:T(8,128)S(1)}, u32[]{:S(2)}, u32[]{:S(2)}) collective-permute-start(f32[32,128]{1,0:T(8,128)S(1)} %get-tuple-element.25.refs_0_), channel_id=1, source_target_pairs={{0,3},{1,2},{2,1},{3,0},{4,7},{5,6},{6,5},{7,4},{8,11},{9,10},{10,... | collective-permute-start | bytes 49160 | tf_op jit(solution)/shard_map/ppermute | solution.py:328
  45.9 0.8 collective-permute-start.5
  46.7 1.1 %collective-permute-done.7.refs_3_ = f32[32,128]{1,0:T(8,128)S(1)} collective-permute-done((f32[32,128]{1,0:T(8,128)S(1)}, f32[32,128]{1,0:T(8,128)S(1)}, u32[]{:S(2)}, u32[]{:S(2)}) %collective-permute-start.7) | collective-permute-done | bytes 16416 | tf_op jit(solution)/shard_map/ppermute | solution.py:328
  47.9 2.7 %collective-permute-done.6.refs_2_ = f32[32,128]{1,0:T(8,128)S(1)} collective-permute-done((f32[32,128]{1,0:T(8,128)S(1)}, f32[32,128]{1,0:T(8,128)S(1)}, u32[]{:S(2)}, u32[]{:S(2)}) %collective-permute-start.6) | collective-permute-done | bytes 16416 | tf_op jit(solution)/shard_map/ppermute | solution.py:328
  50.6 4.0 %next_chain.4 = (f32[8,64,128]{2,1,0:T(8,128)S(1)}, f32[8,64,128]{2,1,0:T(8,128)S(1)}, f32[64,128]{1,0:T(8,128)S(1)}, f32[64,128]{1,0:T(8,128)S(1)}, f32[8,128]{1,0:T(8,128)S(1)}, /*index=5*/f32[8,24,128]{2,1,0:T(8,128)S(1)}) custom-call(f32[32,128]{1,0:T(8,128)S(1)} %get-tuple-element.25.refs_0_, f32[32,128]{1,0:T(8,128)S(1)} %collective-permute-done.5.refs_1_, ...), custom_call_target="tpu_custom_call" | custom-call | tf_op jit(solution)/shard_map/next_chain/pallas_call | solution.py:314
  54.6 1.5 %collective-permute-start.10 = (f32[8,128]{1,0:T(8,128)S(1)}, f32[8,128]{1,0:T(8,128)S(1)}, u32[]{:S(2)}, u32[]{:S(2)}) collective-permute-start(f32[8,128]{1,0:T(8,128)S(1)} %get-tuple-element.28.refs_0_), channel_id=1, source_target_pairs={{0,3},{1,2},{2,1},{3,0},{4,7},{5,6},{6,5},{7,4},{8,11},{9,10},{10,... | collective-permute-start | bytes 12296 | tf_op jit(solution)/shard_map/ppermute | solution.py:328
  56.8 2.3 %collective-permute-start.8 = (f32[8,128]{1,0:T(8,128)S(1)}, f32[8,128]{1,0:T(8,128)S(1)}, u32[]{:S(2)}, u32[]{:S(2)}) collective-permute-start(f32[8,128]{1,0:T(8,128)S(1)} %get-tuple-element.28.refs_0_), channel_id=1, source_target_pairs={{0,1},{1,0},{2,3},{3,2},{4,5},{5,4},{6,7},{7,6},{8,9},{9,8},{10,11... | collective-permute-start | bytes 12296 | tf_op jit(solution)/shard_map/ppermute | solution.py:328
  59.0 1.0 %collective-permute-done.10.refs_3_ = f32[8,128]{1,0:T(8,128)S(1)} collective-permute-done((f32[8,128]{1,0:T(8,128)S(1)}, f32[8,128]{1,0:T(8,128)S(1)}, u32[]{:S(2)}, u32[]{:S(2)}) %collective-permute-start.10) | collective-permute-done | bytes 4128 | tf_op jit(solution)/shard_map/ppermute | solution.py:328
  60.7 3.9 %next_chain.5 = (f32[8,64,128]{2,1,0:T(8,128)S(1)}, f32[8,64,128]{2,1,0:T(8,128)S(1)}, f32[64,128]{1,0:T(8,128)S(1)}, f32[64,128]{1,0:T(8,128)S(1)}, f32[8,128]{1,0:T(8,128)S(1)}) custom-call(f32[8,128]{1,0:T(8,128)S(1)} %get-tuple-element.28.refs_0_, f32[8,128]{1,0:T(8,128)S(1)} %collective-permute-done.8.refs_1_, ...), custom_call_target="tpu_custom_call" | custom-call | tf_op jit(solution)/shard_map/next_chain/pallas_call | solution.py:314
  64.6 2.6 %collective-permute-start.13 = (f32[8,128]{1,0:T(8,128)S(1)}, f32[8,128]{1,0:T(8,128)S(1)}, u32[]{:S(2)}, u32[]{:S(2)}) collective-permute-start(f32[8,128]{1,0:T(8,128)S(1)} %get-tuple-element.34.refs_0_), channel_id=1, source_target_pairs={{0,3},{1,2},{2,1},{3,0},{4,7},{5,6},{6,5},{7,4},{8,11},{9,10},{10,... | collective-permute-start | bytes 12296 | tf_op jit(solution)/shard_map/ppermute | solution.py:328
  67.2 0.9 collective-permute-start.12
  68.1 0.9 %collective-permute-start.11 = (f32[8,128]{1,0:T(8,128)S(1)}, f32[8,128]{1,0:T(8,128)S(1)}, u32[]{:S(2)}, u32[]{:S(2)}) collective-permute-start(f32[8,128]{1,0:T(8,128)S(1)} %get-tuple-element.34.refs_0_), channel_id=1, source_target_pairs={{0,1},{1,0},{2,3},{3,2},{4,5},{5,4},{6,7},{7,6},{8,9},{9,8},{10,11... | collective-permute-start | bytes 12296 | tf_op jit(solution)/shard_map/ppermute | solution.py:328
  69.0 1.0 %collective-permute-done.13.refs_3_ = f32[8,128]{1,0:T(8,128)S(1)} collective-permute-done((f32[8,128]{1,0:T(8,128)S(1)}, f32[8,128]{1,0:T(8,128)S(1)}, u32[]{:S(2)}, u32[]{:S(2)}) %collective-permute-start.13) | collective-permute-done | bytes 4128 | tf_op jit(solution)/shard_map/ppermute | solution.py:328
  70.0 1.6 %collective-permute-done.12.refs_2_ = f32[8,128]{1,0:T(8,128)S(1)} collective-permute-done((f32[8,128]{1,0:T(8,128)S(1)}, f32[8,128]{1,0:T(8,128)S(1)}, u32[]{:S(2)}, u32[]{:S(2)}) %collective-permute-start.12) | collective-permute-done | bytes 4128 | tf_op jit(solution)/shard_map/ppermute | solution.py:328
  71.7 3.9 %next_chain.6 = (f32[8,64,128]{2,1,0:T(8,128)S(1)}, f32[8,64,128]{2,1,0:T(8,128)S(1)}, f32[64,128]{1,0:T(8,128)S(1)}, f32[64,128]{1,0:T(8,128)S(1)}, f32[8,128]{1,0:T(8,128)S(1)}) custom-call(f32[8,128]{1,0:T(8,128)S(1)} %get-tuple-element.34.refs_0_, f32[8,128]{1,0:T(8,128)S(1)} %collective-permute-done.11.refs_1_, ...), custom_call_target="tpu_custom_call" | custom-call | tf_op jit(solution)/shard_map/next_chain/pallas_call | solution.py:314
  75.6 1.5 %collective-permute-start.16 = (f32[8,128]{1,0:T(8,128)S(1)}, f32[8,128]{1,0:T(8,128)S(1)}, u32[]{:S(2)}, u32[]{:S(2)}) collective-permute-start(f32[8,128]{1,0:T(8,128)S(1)} %get-tuple-element.39.refs_0_), channel_id=1, source_target_pairs={{0,3},{1,2},{2,1},{3,0},{4,7},{5,6},{6,5},{7,4},{8,11},{9,10},{10,... | collective-permute-start | bytes 12296 | tf_op jit(solution)/shard_map/ppermute | solution.py:328
  77.1 0.9 %collective-permute-start.15 = (f32[8,128]{1,0:T(8,128)S(1)}, f32[8,128]{1,0:T(8,128)S(1)}, u32[]{:S(2)}, u32[]{:S(2)}) collective-permute-start(f32[8,128]{1,0:T(8,128)S(1)} %get-tuple-element.39.refs_0_), channel_id=1, source_target_pairs={{0,2},{1,3},{2,0},{3,1},{4,6},{5,7},{6,4},{7,5},{8,10},{9,11},{10,... | collective-permute-start | bytes 12296 | tf_op jit(solution)/shard_map/ppermute | solution.py:328
  78.1 2.0 %collective-permute-start.14 = (f32[8,128]{1,0:T(8,128)S(1)}, f32[8,128]{1,0:T(8,128)S(1)}, u32[]{:S(2)}, u32[]{:S(2)}) collective-permute-start(f32[8,128]{1,0:T(8,128)S(1)} %get-tuple-element.39.refs_0_), channel_id=1, source_target_pairs={{0,1},{1,0},{2,3},{3,2},{4,5},{5,4},{6,7},{7,6},{8,9},{9,8},{10,11... | collective-permute-start | bytes 12296 | tf_op jit(solution)/shard_map/ppermute | solution.py:328
  80.1 1.0 %collective-permute-done.16.refs_3_ = f32[8,128]{1,0:T(8,128)S(1)} collective-permute-done((f32[8,128]{1,0:T(8,128)S(1)}, f32[8,128]{1,0:T(8,128)S(1)}, u32[]{:S(2)}, u32[]{:S(2)}) %collective-permute-start.16) | collective-permute-done | bytes 4128 | tf_op jit(solution)/shard_map/ppermute | solution.py:328
  81.7 2.2 %copy-done.1 = f32[8192,128]{1,0:T(8,128)S(1)} copy-done((f32[8192,128]{1,0:T(8,128)S(1)}, f32[8192,128]{1,0:T(8,128)}, u32[]{:S(2)}) %copy-start.1) | copy-done | bytes 4194328
  83.9 3.1 %next_chain.7 = (f32[8,32,128]{2,1,0:T(8,128)S(1)}, f32[8,64,128]{2,1,0:T(8,128)}, f32[8,64,128]{2,1,0:T(8,128)}, f32[64,128]{1,0:T(8,128)}) custom-call(f32[8,128]{1,0:T(8,128)S(1)} %get-tuple-element.39.refs_0_, f32[8,128]{1,0:T(8,128)S(1)} %collective-permute-done.14.refs_1_, f32[8,128]{1,0:T(8,128)S(1)} %collective-permute-done.15.refs_2_, ...), custom_call_target="tpu_custom_call" | custom-call | tf_op jit(solution)/shard_map/next_chain/pallas_call | solution.py:314
  87.1 1.4 %collective-permute-start.18 = (f32[2,32,128]{2,1,0:T(8,128)S(1)}, f32[2,32,128]{2,1,0:T(8,128)S(1)}, u32[]{:S(2)}, u32[]{:S(2)}) collective-permute-start(f32[2,32,128]{2,1,0:T(8,128)S(1)} %get-tuple-element.50), channel_id=1, source_target_pairs={{0,16},{8,24},{16,0},{24,8},{1,17},{9,25},{17,1},{25,9},{2,18},{10... | collective-permute-start | bytes 98312 | tf_op jit(solution)/shard_map/ppermute | solution.py:328
  89.0 1.7 %collective-permute-done.19.refs_3_ = f32[2,32,128]{2,1,0:T(8,128)S(1)} collective-permute-done((f32[2,32,128]{2,1,0:T(8,128)S(1)}, f32[2,32,128]{2,1,0:T(8,128)S(1)}, u32[]{:S(2)}, u32[]{:S(2)}) %collective-permute-start.19) | collective-permute-done | bytes 32800 | tf_op jit(solution)/shard_map/ppermute | solution.py:328
  (29 shorter events, 4.3 us)
Async XLA Ops:
  1.3 20.5 %collective-permute-start.4 = (f32[16,128,128]{2,1,0:T(8,128)S(1)}, f32[16,128,128]{2,1,0:T(8,128)S(1)}, u32[]{:S(2)}, u32[]{:S(2)}) collective-permute-start(f32[16,128,128]{2,1,0:T(8,128)S(1)} %constant_dynamic-slice_fusion.4), channel_id=1, source_target_pairs={{0,4},{28,24},{1,5},{29,25},{2,6},{30,26},{3,7},{31,27}} | collective-permute-start | bytes 3145736 | tf_op jit(solution)/shard_map/ppermute | solution.py:360
  7.0 11.8 %collective-permute-start = (f32[2,2,16,128]{3,2,1,0:T(8,128)S(1)}, f32[2,2,16,128]{3,2,1,0:T(8,128)S(1)}, u32[]{:S(2)}, u32[]{:S(2)}) collective-permute-start(f32[2,2,16,128]{3,2,1,0:T(8,128)S(1)} %fusion), channel_id=1, source_target_pairs={{0,4},{4,0},{1,5},{5,1},{2,6},{6,2},{3,7},{7,3},{8,12},{12,8},{9,1... | collective-permute-start | bytes 98312 | tf_op jit(solution)/shard_map/ppermute | solution.py:339
  19.9 16.6 %collective-permute-start.3 = (f32[2,2,64,128]{3,2,1,0:T(8,128)S(1)}, f32[2,2,64,128]{3,2,1,0:T(8,128)S(1)}, u32[]{:S(2)}, u32[]{:S(2)}) collective-permute-start(f32[2,2,64,128]{3,2,1,0:T(8,128)S(1)} %get-tuple-element.45), channel_id=1, source_target_pairs={{0,24},{8,16},{16,8},{24,0},{1,25},{9,17},{17,9},{25,1},{2,26},{10... | collective-permute-start | bytes 393224 | tf_op jit(solution)/shard_map/ppermute | solution.py:328
  21.1 15.4 %collective-permute-start.2 = (f32[2,2,64,128]{3,2,1,0:T(8,128)S(1)}, f32[2,2,64,128]{3,2,1,0:T(8,128)S(1)}, u32[]{:S(2)}, u32[]{:S(2)}) collective-permute-start(f32[2,2,64,128]{3,2,1,0:T(8,128)S(1)} %get-tuple-element.46), channel_id=1, source_target_pairs={{0,16},{8,24},{16,0},{24,8},{1,17},{9,25},{17,1},{25,9},{2,18},{10... | collective-permute-start | bytes 393224 | tf_op jit(solution)/shard_map/ppermute | solution.py:328
  21.1 15.4 %collective-permute-start.1 = (f32[2,2,64,128]{3,2,1,0:T(8,128)S(1)}, f32[2,2,64,128]{3,2,1,0:T(8,128)S(1)}, u32[]{:S(2)}, u32[]{:S(2)}) collective-permute-start(f32[2,2,64,128]{3,2,1,0:T(8,128)S(1)} %get-tuple-element.47), channel_id=1, source_target_pairs={{0,8},{8,0},{16,24},{24,16},{1,9},{9,1},{17,25},{25,17},{2,10},{10... | collective-permute-start | bytes 393224 | tf_op jit(solution)/shard_map/ppermute | solution.py:328
  21.8 3.4 %copy-start.2 = (f32[128,128,128]{2,1,0:T(8,128)S(1)}, f32[128,128,128]{2,1,0:T(8,128)}, u32[]{:S(2)}) copy-start(f32[128,128,128]{2,1,0:T(8,128)} %param.5) | copy-start | bytes 25165828
  36.4 39.2 %copy-start = (f32[8192,128]{1,0:T(8,128)}, f32[8192,128]{1,0:T(8,128)S(1)}, u32[]{:S(2)}) copy-start(f32[8192,128]{1,0:T(8,128)S(1)} %layout.1.refs_4_) | copy-start | bytes 12582916
  42.3 5.6 %collective-permute-start.7 = (f32[32,128]{1,0:T(8,128)S(1)}, f32[32,128]{1,0:T(8,128)S(1)}, u32[]{:S(2)}, u32[]{:S(2)}) collective-permute-start(f32[32,128]{1,0:T(8,128)S(1)} %get-tuple-element.25.refs_0_), channel_id=1, source_target_pairs={{0,3},{1,2},{2,1},{3,0},{4,7},{5,6},{6,5},{7,4},{8,11},{9,10},{10,... | collective-permute-start | bytes 49160 | tf_op jit(solution)/shard_map/ppermute | solution.py:328
  45.9 4.6 %collective-permute-start.6 = (f32[32,128]{1,0:T(8,128)S(1)}, f32[32,128]{1,0:T(8,128)S(1)}, u32[]{:S(2)}, u32[]{:S(2)}) collective-permute-start(f32[32,128]{1,0:T(8,128)S(1)} %get-tuple-element.25.refs_0_), channel_id=1, source_target_pairs={{0,2},{1,3},{2,0},{3,1},{4,6},{5,7},{6,4},{7,5},{8,10},{9,11},{10,... | collective-permute-start | bytes 49160 | tf_op jit(solution)/shard_map/ppermute | solution.py:328
  45.9 4.6 %collective-permute-start.5 = (f32[32,128]{1,0:T(8,128)S(1)}, f32[32,128]{1,0:T(8,128)S(1)}, u32[]{:S(2)}, u32[]{:S(2)}) collective-permute-start(f32[32,128]{1,0:T(8,128)S(1)} %get-tuple-element.25.refs_0_), channel_id=1, source_target_pairs={{0,1},{1,0},{2,3},{3,2},{4,5},{5,4},{6,7},{7,6},{8,9},{9,8},{10,11... | collective-permute-start | bytes 49160 | tf_op jit(solution)/shard_map/ppermute | solution.py:328
  54.6 36.5 %copy-start.3 = (f32[2,128,128]{2,1,0:T(8,128)S(1)}, f32[2,128,128]{2,1,0:T(8,128)}, u32[]{:S(2)}) copy-start(f32[2,128,128]{2,1,0:T(8,128)} %v_ref.1) | copy-start | bytes 393220
  54.6 5.5 %collective-permute-start.10 = (f32[8,128]{1,0:T(8,128)S(1)}, f32[8,128]{1,0:T(8,128)S(1)}, u32[]{:S(2)}, u32[]{:S(2)}) collective-permute-start(f32[8,128]{1,0:T(8,128)S(1)} %get-tuple-element.28.refs_0_), channel_id=1, source_target_pairs={{0,3},{1,2},{2,1},{3,0},{4,7},{5,6},{6,5},{7,4},{8,11},{9,10},{10,... | collective-permute-start | bytes 12296 | tf_op jit(solution)/shard_map/ppermute | solution.py:328
  56.1 4.5 %collective-permute-start.9 = (f32[8,128]{1,0:T(8,128)S(1)}, f32[8,128]{1,0:T(8,128)S(1)}, u32[]{:S(2)}, u32[]{:S(2)}) collective-permute-start(f32[8,128]{1,0:T(8,128)S(1)} %get-tuple-element.28.refs_0_), channel_id=1, source_target_pairs={{0,2},{1,3},{2,0},{3,1},{4,6},{5,7},{6,4},{7,5},{8,10},{9,11},{10,... | collective-permute-start | bytes 12296 | tf_op jit(solution)/shard_map/ppermute | solution.py:328
  56.8 3.9 %collective-permute-start.8 = (f32[8,128]{1,0:T(8,128)S(1)}, f32[8,128]{1,0:T(8,128)S(1)}, u32[]{:S(2)}, u32[]{:S(2)}) collective-permute-start(f32[8,128]{1,0:T(8,128)S(1)} %get-tuple-element.28.refs_0_), channel_id=1, source_target_pairs={{0,1},{1,0},{2,3},{3,2},{4,5},{5,4},{6,7},{7,6},{8,9},{9,8},{10,11... | collective-permute-start | bytes 12296 | tf_op jit(solution)/shard_map/ppermute | solution.py:328
  64.6 5.5 %collective-permute-start.13 = (f32[8,128]{1,0:T(8,128)S(1)}, f32[8,128]{1,0:T(8,128)S(1)}, u32[]{:S(2)}, u32[]{:S(2)}) collective-permute-start(f32[8,128]{1,0:T(8,128)S(1)} %get-tuple-element.34.refs_0_), channel_id=1, source_target_pairs={{0,3},{1,2},{2,1},{3,0},{4,7},{5,6},{6,5},{7,4},{8,11},{9,10},{10,... | collective-permute-start | bytes 12296 | tf_op jit(solution)/shard_map/ppermute | solution.py:328
  67.2 4.5 %collective-permute-start.12 = (f32[8,128]{1,0:T(8,128)S(1)}, f32[8,128]{1,0:T(8,128)S(1)}, u32[]{:S(2)}, u32[]{:S(2)}) collective-permute-start(f32[8,128]{1,0:T(8,128)S(1)} %get-tuple-element.34.refs_0_), channel_id=1, source_target_pairs={{0,2},{1,3},{2,0},{3,1},{4,6},{5,7},{6,4},{7,5},{8,10},{9,11},{10,... | collective-permute-start | bytes 12296 | tf_op jit(solution)/shard_map/ppermute | solution.py:328
  68.1 3.6 %collective-permute-start.11 = (f32[8,128]{1,0:T(8,128)S(1)}, f32[8,128]{1,0:T(8,128)S(1)}, u32[]{:S(2)}, u32[]{:S(2)}) collective-permute-start(f32[8,128]{1,0:T(8,128)S(1)} %get-tuple-element.34.refs_0_), channel_id=1, source_target_pairs={{0,1},{1,0},{2,3},{3,2},{4,5},{5,4},{6,7},{7,6},{8,9},{9,8},{10,11... | collective-permute-start | bytes 12296 | tf_op jit(solution)/shard_map/ppermute | solution.py:328
  75.6 5.5 %collective-permute-start.16 = (f32[8,128]{1,0:T(8,128)S(1)}, f32[8,128]{1,0:T(8,128)S(1)}, u32[]{:S(2)}, u32[]{:S(2)}) collective-permute-start(f32[8,128]{1,0:T(8,128)S(1)} %get-tuple-element.39.refs_0_), channel_id=1, source_target_pairs={{0,3},{1,2},{2,1},{3,0},{4,7},{5,6},{6,5},{7,4},{8,11},{9,10},{10,... | collective-permute-start | bytes 12296 | tf_op jit(solution)/shard_map/ppermute | solution.py:328
  77.1 4.5 %collective-permute-start.15 = (f32[8,128]{1,0:T(8,128)S(1)}, f32[8,128]{1,0:T(8,128)S(1)}, u32[]{:S(2)}, u32[]{:S(2)}) collective-permute-start(f32[8,128]{1,0:T(8,128)S(1)} %get-tuple-element.39.refs_0_), channel_id=1, source_target_pairs={{0,2},{1,3},{2,0},{3,1},{4,6},{5,7},{6,4},{7,5},{8,10},{9,11},{10,... | collective-permute-start | bytes 12296 | tf_op jit(solution)/shard_map/ppermute | solution.py:328
  78.1 3.6 %collective-permute-start.14 = (f32[8,128]{1,0:T(8,128)S(1)}, f32[8,128]{1,0:T(8,128)S(1)}, u32[]{:S(2)}, u32[]{:S(2)}) collective-permute-start(f32[8,128]{1,0:T(8,128)S(1)} %get-tuple-element.39.refs_0_), channel_id=1, source_target_pairs={{0,1},{1,0},{2,3},{3,2},{4,5},{5,4},{6,7},{7,6},{8,9},{9,8},{10,11... | collective-permute-start | bytes 12296 | tf_op jit(solution)/shard_map/ppermute | solution.py:328
  81.7 2.2 %copy-start.1 = (f32[8192,128]{1,0:T(8,128)S(1)}, f32[8192,128]{1,0:T(8,128)}, u32[]{:S(2)}) copy-start(f32[8192,128]{1,0:T(8,128)} %copy-done) | copy-start | bytes 12582916
  87.0 3.6 %collective-permute-start.19 = (f32[2,32,128]{2,1,0:T(8,128)S(1)}, f32[2,32,128]{2,1,0:T(8,128)S(1)}, u32[]{:S(2)}, u32[]{:S(2)}) collective-permute-start(f32[2,32,128]{2,1,0:T(8,128)S(1)} %get-tuple-element.49), channel_id=1, source_target_pairs={{0,24},{8,16},{16,8},{24,0},{1,25},{9,17},{17,9},{25,1},{2,26},{10... | collective-permute-start | bytes 98312 | tf_op jit(solution)/shard_map/ppermute | solution.py:328
  87.1 4.0 %collective-permute-start.18 = (f32[2,32,128]{2,1,0:T(8,128)S(1)}, f32[2,32,128]{2,1,0:T(8,128)S(1)}, u32[]{:S(2)}, u32[]{:S(2)}) collective-permute-start(f32[2,32,128]{2,1,0:T(8,128)S(1)} %get-tuple-element.50), channel_id=1, source_target_pairs={{0,16},{8,24},{16,0},{24,8},{1,17},{9,25},{17,1},{25,9},{2,18},{10... | collective-permute-start | bytes 98312 | tf_op jit(solution)/shard_map/ppermute | solution.py:328
  88.5 2.6 %collective-permute-start.17 = (f32[2,32,128]{2,1,0:T(8,128)S(1)}, f32[2,32,128]{2,1,0:T(8,128)S(1)}, u32[]{:S(2)}, u32[]{:S(2)}) collective-permute-start(f32[2,32,128]{2,1,0:T(8,128)S(1)} %get-tuple-element.51), channel_id=1, source_target_pairs={{0,8},{8,0},{16,24},{24,16},{1,9},{9,1},{17,25},{25,17},{2,10},{10... | collective-permute-start | bytes 98312 | tf_op jit(solution)/shard_map/ppermute | solution.py:328

commit v2 on v1

--- a/solution.py
+++ b/solution.py
@@ -13,8 +13,8 @@
 SPREAD = [(k, side, delta) for k in range(1, STEPS) for side in range(2) for delta in range(1 - k, k)]
 PACK_ROWS = 8 * (-(-(STEPS + len(SPREAD)) // 8))
 VMEM = pl.BlockSpec(memory_space=pltpu.VMEM)
-ANY = pl.BlockSpec(memory_space=pl.ANY)
-PARAMS = pltpu.CompilerParams(vmem_limit_bytes=40 * 1024 * 1024)
+HBM = pl.BlockSpec(memory_space=pltpu.HBM)
+PARAMS = pltpu.CompilerParams(vmem_limit_bytes=16 * 1024 * 1024)
 
 
 def low_lanes(rows):
@@ -56,33 +56,40 @@
     return jnp.where(low_lanes(1), a[0:1], a[HALF - 1 : HALF])
 
 
-def block(b_ref, j):
-    return b_ref[pl.ds(pl.multiple_of(j * HALF, HALF), HALF), :]
-
-
-def apply_blocks(b_ref, rhs, r_refs):
-    count = len(rhs)
-    for a, r_ref in zip(rhs, r_refs):
-        r_ref[0:HALF, :], r_ref[HALF:LANES, :] = spread(a)
-    unroll = 8 if count == 1 else 2
-
-    def step(outer, totals):
-        totals = list(totals)
-        for u in range(unroll):
-            j = outer * unroll + u
-            rows = block(b_ref, j)
-            for n in range(count):
-                slot = n if count > 1 else u % 2
-                totals[slot] = totals[slot] + rows * r_refs[n][pl.ds(j, 1), :]
-        return tuple(totals)
-
-    zero = jnp.zeros((HALF, LANES), jnp.float32)
-    totals = lax.fori_loop(0, LANES // unroll, step, (zero,) * max(2, count))
-    return [totals[0] + totals[1]] if count == 1 else list(totals)
-
-
-def layout_kernel(own, axis, b_ref, ghost_ref, out_ref, window, sems):
-    ghost = ghost_ref.shape[0] // LANES
+def block_column(b_ref, j):
+    return b_ref[pl.ds(j, HALF, stride=LANES), :]
+
+
+def fold_rows(parts):
+    row = lax.broadcasted_iota(jnp.int32, (8, LANES), 0)
+    for bit in (1, 2, 4):
+        first = (row & bit) == 0
+        parts = [
+            jnp.where(first, a, b) + pltpu.roll(jnp.where(first, b, a), 8 - bit, 0)
+            for a, b in zip(parts[::2], parts[1::2])
+        ]
+    return parts[0]
+
+
+def apply_blocks(b_ref, rhs, out_ref):
+    halves = spread(rhs)
+    tiles = [half[8 * t : 8 * t + 8] for half in halves for t in range(HALF // 8)]
+    for outer in range(HALF // 8):
+        parts = []
+        for u in range(8):
+            at = (outer * 8 + u) * LANES
+            terms = [b_ref[at + 8 * t : at + 8 * t + 8, :] * tiles[t] for t in range(2)]
+            for t in range(2, len(tiles)):
+                terms[t % 2] = terms[t % 2] + b_ref[at + 8 * t : at + 8 * t + 8, :] * tiles[t]
+            parts.append(terms[0] + terms[1])
+        out_ref[outer * 8 : outer * 8 + 8, :] = fold_rows(parts)
+    return out_ref[...]
+
+
+def layout_kernel(own, ghost, axis, b_ref, *refs):
+    *ghost_refs, out_ref, ready_ref, window, sems = refs
+    ready_ref[...] = jnp.zeros(ready_ref.shape, jnp.float32)
+    ghost_ref = ghost_refs[0] if ghost_refs else b_ref
     count = b_ref.shape[0] // LANES
     position = lax.axis_index(axis)
     chunk = math.gcd(own, ghost)
@@ -107,27 +114,66 @@
     for copy in copies:
         copy.wait()
 
-    def one(i, carry):
-        top = window[pl.ds(i, HALF, stride=LANES), :]
-        bottom = window[pl.ds(i + HALF, HALF, stride=LANES), :]
-        out_ref[pl.ds(i, LANES, stride=HALF), :] = jnp.concatenate([top, bottom], axis=0).T
+    def one(outer, carry):
+        for u in range(8):
+            i = outer * 8 + u
+            top = window[pl.ds(i, HALF, stride=LANES), :]
+            bottom = window[pl.ds(i + HALF, HALF, stride=LANES), :]
+            at = pl.multiple_of(i * LANES, LANES)
+            out_ref[pl.ds(at, LANES), :] = jnp.concatenate([top, bottom], axis=0).T
         return carry
 
-    lax.fori_loop(0, HALF, one, 0)
-
-
-def responses(b_ref, r_refs, pack_ref):
+    lax.fori_loop(0, HALF // 8, one, 0)
+
+
+def patch_kernel(axis, groups, b_in, beyond, out_ref):
+    ghost = beyond.shape[0] // LANES
+    per_turn = HALF // ghost
+    unroll = 4
+    position = lax.axis_index(axis)
+    for place, at in ((0, 0), (groups - 1, HALF - ghost)):
+
+        @pl.when(position == place)
+        def _(at=at):
+            lane = lax.broadcasted_iota(jnp.int32, (LANES, LANES), 1) % HALF
+            mine = jnp.logical_and(lane >= at, lane < at + ghost)
+
+            def one(outer, carry):
+                turns = []
+                for v in range(unroll):
+                    first = (outer * unroll + v) * per_turn
+                    rows = [
+                        beyond[pl.ds(half * HALF + first + u, ghost, stride=LANES), :]
+                        for half in range(2)
+                        for u in range(per_turn)
+                    ]
+                    turns.append(jnp.concatenate(rows, axis=0).T)
+                for v in range(unroll):
+                    first = (outer * unroll + v) * per_turn
+                    for u in range(per_turn):
+                        moved = from_line(turns[v], (u * ghost - at) % LANES)
+                        here = pl.ds(pl.multiple_of((first + u) * LANES, LANES), LANES)
+                        out_ref[here, :] = jnp.where(mine, moved, b_in[here, :])
+                return carry
+
+            lax.fori_loop(0, HALF // per_turn // unroll, one, 0)
+
+
+def responses_kernel(b_ref, pack_ref, r_ref):
+    pack_ref[...] = jnp.zeros(pack_ref.shape, jnp.float32)
     low_all = low_lanes(LANES)
     edge_rows = jnp.where(
         low_all,
-        b_ref[pl.ds(0, LANES, stride=HALF), :],
-        b_ref[pl.ds(HALF - 1, LANES, stride=HALF), :],
+        b_ref[0:LANES, :],
+        b_ref[(HALF - 1) * LANES : HALF * LANES, :],
     )
-    firsts = [block(b_ref, 0), block(b_ref, LANES - 1)]
+    firsts = [block_column(b_ref, 0), block_column(b_ref, LANES - 1)]
     shifted = [sum_y(a) for a in firsts]
     plan = [(side, delta) for side in range(2) for delta in (-1, 0, 1)]
-    seconds = apply_blocks(b_ref, [from_line(shifted[side], delta) for side, delta in plan], r_refs)
-    second = {key: value for key, value in zip(plan, seconds)}
+    second = {
+        (side, delta): apply_blocks(b_ref, from_line(shifted[side], delta), r_ref)
+        for side, delta in plan
+    }
     for n, (k, side, delta) in enumerate(SPREAD):
         if k == 1:
             row = edges(firsts[side])
@@ -142,7 +188,7 @@
         pack_ref[pl.ds(STEPS + n, 1), :] = row
 
 
-def local_chain(steps, b_ref, rhs_ref, add_ref, state, r_refs, pack_ref, first_loc_ref):
+def local_chain(steps, b_ref, rhs_ref, add_ref, state, r_ref, pack_ref, first_loc_ref):
     nz = rhs_ref.shape[0]
     if state is not None:
         pack_ref[0:1, :] = edges(state)
@@ -151,7 +197,7 @@
         rhs = rhs_ref[z]
         if state is not None:
             rhs = rhs + sum_y(sum_x(state))
-        (state,) = apply_blocks(b_ref, [rhs], r_refs)
+        state = apply_blocks(b_ref, rhs, r_ref)
         if step >= nz:
             state = state + add_ref[z]
         if n == 0:
@@ -159,7 +205,7 @@
         pack_ref[n + 1 : n + 2, :] = edges(state)
 
 
-def gather_planes(axis, field_refs, v_ref, s_ref):
+def gather_planes(axis, groups, field_refs, ghost_ref, v_ref, s_ref):
     position = lax.axis_index(axis)
     low = low_lanes(HALF)
     nz_local = field_refs[0].shape[1]
@@ -168,25 +214,32 @@
         for p in range(nz_local):
             for kind, target in ((0, v_ref), (1, s_ref)):
                 plane = ref[kind, p]
+                if ghost_ref is not None:
+                    beyond = ghost_ref[(groups - 1) ^ k, kind, p]
+                    ghost = beyond.shape[0]
+                    first = jnp.where(position == 0, beyond, plane[:ghost])
+                    last = jnp.where(position == groups - 1, beyond, plane[HALF - ghost :])
+                    plane = jnp.concatenate([first, plane[ghost : HALF - ghost], last], axis=0)
                 turned = jnp.concatenate([plane, plane], axis=0).T
                 target[base + p + 1 - kind] = jnp.where(low, turned[:HALF], turned[HALF:])
 
 
-def first_kernel(axis, fields, *refs):
+def first_kernel(axis, fields, late, *refs):
     field_refs = refs[:fields]
-    b_ref, rhs_ref, loc_ref, pack_ref, v_ref, s_ref = refs[fields : fields + 6]
-    r_refs = refs[fields + 6 :]
+    ghost_ref = refs[fields] if late else None
+    refs = refs[1:] if late else refs
+    b_ref, answers_ref, rhs_ref, loc_ref, pack_ref, v_ref, s_ref, r_ref = refs[fields:]
     nz = rhs_ref.shape[0]
     pack_ref[...] = jnp.zeros(pack_ref.shape, jnp.float32)
-    responses(b_ref, r_refs, pack_ref)
+    pack_ref[:PACK_ROWS, :] = answers_ref[...]
     v_ref[0] = jnp.zeros((HALF, LANES), jnp.float32)
     v_ref[nz + 1] = jnp.zeros((HALF, LANES), jnp.float32)
-    gather_planes(axis, field_refs, v_ref, s_ref)
+    gather_planes(axis, fields, field_refs, ghost_ref, v_ref, s_ref)
     for z in range(nz):
         around = v_ref[z] + v_ref[z + 1] + v_ref[z + 2]
         rhs_ref[z] = s_ref[z] - 27.0 * v_ref[z + 1] + sum_y(sum_x(around))
         pack_ref[PACK_ROWS + z : PACK_ROWS + z + 1, :] = edges(around)
-    local_chain(list(range(STEPS)), b_ref, rhs_ref, None, None, r_refs, pack_ref, loc_ref)
+    local_chain(list(range(STEPS)), b_ref, rhs_ref, None, None, r_ref, pack_ref, loc_ref)
 
 
 def halo_of(ends):
@@ -220,6 +273,13 @@
                     )
 
 
+def ghost_pack_kernel(axis, own, ghost, *refs):
+    *window_refs, ready_ref, out_ref = refs
+    at = jnp.where(lax.axis_index(axis) == 0, ghost, own)
+    for k, ref in enumerate(window_refs):
+        out_ref[k] = ref[:, :, pl.ds(pl.multiple_of(at, 8), ghost), :]
+
+
 def next_kernel(steps, later, first, peers, axis, ghost, *refs):
     refs = list(refs)
 
@@ -236,7 +296,7 @@
     rhs_ref, add_ref, state_ref = take(3)
     loc_ref, pack_ref = take(2) if later else (None, None)
     coef_out = take(1)[0] if first else None
-    gather, halo_ref, inject_ref, *r_refs = refs
+    gather, halo_ref, inject_ref, r_ref = refs
     nz = rhs_in.shape[0]
     rows = packs[0].shape[0]
     position = lax.axis_index(axis)
@@ -272,9 +332,11 @@
                 rhs_ref[step - 1] = around - 27.0 * state
         if t == 0:
             left, right = inject_ref[0, own, :], inject_ref[1, own, :]
-            state = loc_in[...] + block(b_ref, 0) * left + block(b_ref, LANES - 1) * right
+            state = (
+                loc_in[...] + block_column(b_ref, 0) * left + block_column(b_ref, LANES - 1) * right
+            )
         else:
-            (state,) = apply_blocks(b_ref, [rhs_ref[z] + around], r_refs)
+            state = apply_blocks(b_ref, rhs_ref[z] + around, r_ref)
             if step >= nz:
                 state = state + add_ref[z]
         add_ref[z] = 2.0 * state if step < nz else state
@@ -283,7 +345,7 @@
     state_ref[...] = state
     if later:
         pack_ref[...] = jnp.zeros(pack_ref.shape, jnp.float32)
-        local_chain(later, b_ref, rhs_ref, add_ref, state, r_refs, pack_ref, loc_ref)
+        local_chain(later, b_ref, rhs_ref, add_ref, state, r_ref, pack_ref, loc_ref)
     if last:
         own_lines = HALF - 2 * ghost
         for z in range(nz):
@@ -292,9 +354,9 @@
             out_ref[z] = turned[ghost : ghost + own_lines]
 
 
-def local_kernel(steps, b_ref, rhs_ref, add_ref, state_ref, loc_ref, pack_ref, *r_refs):
+def local_kernel(steps, b_ref, rhs_ref, add_ref, state_ref, loc_ref, pack_ref, r_ref):
     pack_ref[...] = jnp.zeros(pack_ref.shape, jnp.float32)
-    local_chain(steps, b_ref, rhs_ref, add_ref, state_ref[...], r_refs, pack_ref, loc_ref)
+    local_chain(steps, b_ref, rhs_ref, add_ref, state_ref[...], r_ref, pack_ref, loc_ref)
 
 
 def finish_kernel(axis, v_ref, *refs):
@@ -322,11 +384,16 @@
     )(*ins)
 
 
+def in_hbm(a):
+    return pltpu.with_memory_space_constraint(a, pltpu.HBM)
+
+
 def to_peers(pieces, axis):
     count = lax.axis_size(axis)
-    return [pieces[0]] + [
-        lax.ppermute(pieces[k], axis, [(i, i ^ k) for i in range(count)]) for k in range(1, count)
-    ]
+    got = {0: pieces[0]}
+    for k in reversed(range(1, count)):
+        got[k] = lax.ppermute(pieces[k], axis, [(i, i ^ k) for i in range(count)])
+    return [got[k] for k in range(count)]
 
 
 def line_ghosts(cells, dim, width):
@@ -349,15 +416,30 @@
     size = blocks.shape[0]
     reach = -(-width // own)
     assert 2 * reach <= groups
-    start = jnp.where(lax.axis_index("gz") < reach, size - width, 0)
+    shift = reach if 4 * reach <= groups else 0
+    start = jnp.where(lax.axis_index("gz") < groups // 2, size - width, 0)
     pairs = []
-    for g in range(groups):
+    for g in range(reach):
         for a in range(count - 1):
-            if g < reach:
-                pairs.append((g * count + a, g * count + a + 1))
-            if groups - 1 - g < reach:
-                pairs.append((g * count + a + 1, g * count + a))
+            pairs.append(((g + shift) * count + a, g * count + a + 1))
+            pairs.append(((groups - 1 - g - shift) * count + a + 1, (groups - 1 - g) * count + a))
     return lax.ppermute(lax.dynamic_slice_in_dim(blocks, start, width, 0), ("gz", "gx"), pairs)
+
+
+def window_ghosts(windows, ready, own, ghost):
+    groups, count = lax.axis_size("gz"), lax.axis_size("gx")
+    nz_local = windows[0].shape[1]
+    (lines,) = call(
+        functools.partial(ghost_pack_kernel, "gz", own, ghost),
+        [*windows, ready],
+        [f32(groups, 2, nz_local, ghost, LANES)],
+        [],
+        "ghost_pack",
+    )
+    end = (groups - 1) * count
+    pairs = [(end + a, a + 1) for a in range(count - 1)]
+    pairs += [(a + 1, end + a) for a in range(count - 1)]
+    return lax.ppermute(lines, ("gz", "gx"), pairs)
 
 
 def refresh_ghosts(planes, ghost):
@@ -382,38 +464,59 @@
     assert nz % STEPS == 0 and nz <= ghost and peers <= 4
     here = lax.axis_index("gz")
 
+    fields = jnp.stack([initial_field, source_term])
     rows = block_inverse.reshape(lines * LANES, LANES)
     beyond = block_ghosts(block_inverse, own, ghost).reshape(ghost * LANES, LANES)
-    blocks = pl.pallas_call(
-        functools.partial(layout_kernel, own, "gz"),
-        out_shape=f32(LANES * HALF, LANES),
-        in_specs=[ANY, ANY],
-        out_specs=VMEM,
+    late = own == 2 * ghost
+    turned = LANES * HALF * LANES * 4
+    blocks, ready = pl.pallas_call(
+        functools.partial(layout_kernel, own, ghost, "gz"),
+        out_shape=[f32(LANES * HALF, LANES), f32(8, LANES)],
+        in_specs=[HBM] * (1 if late else 2),
+        out_specs=[VMEM, VMEM],
         scratch_shapes=[
             pltpu.VMEM((HALF * LANES, LANES), jnp.float32),
             pltpu.SemaphoreType.DMA((HALF // math.gcd(own, ghost),)),
         ],
         compiler_params=PARAMS,
+        cost_estimate=pl.CostEstimate(flops=0, bytes_accessed=4 * turned, transcendentals=0),
         name="layout",
-    )(rows, beyond)
-
-    fields = jnp.stack([initial_field, source_term])
-    before, after = line_ghosts(fields, 2, ghost)
-    wide = jnp.concatenate([before, fields, after], axis=2)
+    )(*[in_hbm(a) for a in ([rows] if late else [rows, beyond])])
+    if late:
+        wide = jnp.pad(fields, ((0, 0), (0, 0), (ghost, ghost), (0, 0)))
+    else:
+        before, after = line_ghosts(fields, 2, ghost)
+        wide = jnp.concatenate([before, fields, after], axis=2)
     windows = [
         lax.dynamic_slice_in_dim(wide, jnp.bitwise_xor(here, k) * own, HALF, 2)
         for k in range(groups)
     ]
     fields_here = to_peers(windows, "gz")
-
-    plane = pltpu.VMEM((LANES, LANES), jnp.float32)
+    ghosts_here = []
+    if late:
+        ghosts_here = [window_ghosts(fields_here, ready, own, ghost)]
+        blocks = pl.pallas_call(
+            functools.partial(patch_kernel, "gz", groups),
+            out_shape=f32(LANES * HALF, LANES),
+            in_specs=[VMEM, VMEM],
+            out_specs=VMEM,
+            input_output_aliases={0: 0},
+            compiler_params=PARAMS,
+            name="patch",
+        )(blocks, beyond)
+
+
+    plane = pltpu.VMEM((HALF, LANES), jnp.float32)
+    (answers,) = call(
+        responses_kernel, [blocks], [f32(PACK_ROWS, LANES)], [plane], "responses"
+    )
     first_rows = PACK_ROWS + 8 * (-(-nz // 8))
     rhs, loc, pack = call(
-        functools.partial(first_kernel, "gz", groups),
-        [*fields_here, blocks],
+        functools.partial(first_kernel, "gz", groups, late),
+        [*fields_here, *ghosts_here, blocks, answers],
         [f32(nz, HALF, LANES), f32(HALF, LANES), f32(first_rows, LANES)],
         [pltpu.VMEM((nz + 2, HALF, LANES), jnp.float32), pltpu.VMEM((nz, HALF, LANES), jnp.float32)]
-        + [plane] * 6,
+        + [plane],
         "first_chain",
     )
     schedule = [list(range(a, a + STEPS)) for a in range(0, 2 * nz, STEPS)]

time: 92.2 us -> 69.8 us (0.76)
  the two profiles are of different devices: /device:TPU:0 before, /device:TPU:11 now
where the time goes in v2:
time: 69.8 us; the launch traced here: 69.6 us
  starting transfers between devices  32.8 us (47%)
  Pallas kernels  21 us (30%)
  waiting for transfers between devices  11 us (16%)
  local copies, waits for them, and re-layouts  3.55 us (5%)
  other arithmetic  1 us (1%)
    ppermute x18, starting transfers between devices, to_peers(): got[k] = lax.ppermute(pieces[k], axis, [(i, i ^ k) for i in range(count)])  31.4 us
    pallas_call x8, Pallas kernels, call(): pl.pallas_call(kernel, out_shape=outs, in_specs=[VMEM] * len(ins), out_sp...  16 us
    ppermute x18, waiting for transfers between devices, to_peers(): got[k] = lax.ppermute(pieces[k], axis, [(i, i ^ k) for i in range(count)])  11 us
    pallas_call x1, Pallas kernels, body(): pl.pallas_call(functools.partial(layout_kernel, own, ghost, 'gz'), out_sh...  5.04 us
    unnamed x6, local copies, waits for them, and re-layouts  2.2 us
  transfers between devices with their start and end apart: 20, of which 10 were waited for; matrix products, arithmetic and copies ran while one was open for 2% of the time, Pallas kernels for 10%

profile of v2, /device:TPU:11, one launch (start us, length us, event | category | flops | bytes accessed | tf_op | source)
XLA Modules:
  0.0 69.6 jit_solution(15220495634032311446)
XLA Ops:
  0.0 1.3 %constant_dynamic-slice_fusion.4 = f32[16,128,128]{2,1,0:T(8,128)S(1)} fusion(f32[128,128,128]{2,1,0:T(8,128)} %param.5, s32[]{:T(128)S(6)} %select_n.33), kind=kLoop, calls=%fused_computation.8 | loop fusion | bytes 2097156 | tf_op jit(solution)/shard_map/dynamic_slice | solution.py:426
  1.3 0.7 %collective-permute-start.4 = (f32[16,128,128]{2,1,0:T(8,128)S(1)}, f32[16,128,128]{2,1,0:T(8,128)S(1)}, u32[]{:S(2)}, u32[]{:S(2)}) collective-permute-start(f32[16,128,128]{2,1,0:T(8,128)S(1)} %constant_dynamic-slice_fusion.4), channel_id=1, source_target_pairs={{8,4},{20,24},{9,5},{21,25},{10,6},{22,26},{11,7},{23,27}} | collective-permute-start | bytes 3145736 | tf_op jit(solution)/shard_map/ppermute | solution.py:426
  2.1 1.0 %select_maximum_fusion = f32[2,2,160,128]{3,2,1,0:T(8,128)S(1)} fusion(f32[1,2,128,128]{3,2,1,0:T(8,128)} %bitcast.7, f32[1,2,128,128]{3,2,1,0:T(8,128)} %bitcast.5), kind=kLoop, calls=%fused_computation.2 | loop fusion | flops 491520 | bytes 589824 | tf_op jit(solution)/shard_map/stack | solution.py:467
  3.1 3.1 %collective-permute-start.2 = (f32[2,2,64,128]{3,2,1,0:T(8,128)S(1)}, f32[2,2,64,128]{3,2,1,0:T(8,128)S(1)}, u32[]{:S(2)}, u32[]{:S(2)}) collective-permute-start(f32[2,2,64,128]{3,2,1,0:T(8,128)S(1)} %get-tuple-element.49), channel_id=1, source_target_pairs={{0,24},{8,16},{16,8},{24,0},{1,25},{9,17},{17,9},{25,1},{2,26},{10... | collective-permute-start | bytes 393224 | tf_op jit(solution)/shard_map/ppermute | solution.py:395
  6.7 5.0 %layout.1 = (f32[8192,128]{1,0:T(8,128)S(1)}, f32[8,128]{1,0:T(8,128)S(1)}) custom-call(f32[16384,128]{1,0:T(8,128)} %bitcast.6), custom_call_target="tpu_custom_call" | custom-call | bytes 16777216 | tf_op jit(solution)/shard_map/layout/pallas_call | solution.py:472
  12.0 0.7 collective-permute-start.3
  12.7 2.2 %responses.1.refs_6_ = f32[24,128]{1,0:T(8,128)S(1)} custom-call(f32[8192,128]{1,0:T(8,128)S(1)} %patch.1.b_ref.refs_5_.refs_4_), custom_call_target="tpu_custom_call" | custom-call | tf_op jit(solution)/shard_map/responses/pallas_call | solution.py:376
  14.9 1.6 %first_chain.1 = (f32[8,64,128]{2,1,0:T(8,128)S(1)}, f32[64,128]{1,0:T(8,128)S(1)}, f32[32,128]{1,0:T(8,128)S(1)}) custom-call(f32[2,2,64,128]{3,2,1,0:T(8,128)S(1)} %get-tuple-element.52.refs_0_, f32[2,2,64,128]{3,2,1,0:T(8,128)S(1)} %collective-permute-done.refs_1_, f32[2,2,64,128]{3,2,1,0:T(8,128)S(1)} %collective-permute-done.1.refs_2_, ...), custom_call_target="tpu_custom_call" | custom-call | tf_op jit(solution)/shard_map/first_chain/pallas_call | solution.py:376
  16.4 1.4 %collective-permute-start.7 = (f32[32,128]{1,0:T(8,128)S(1)}, f32[32,128]{1,0:T(8,128)S(1)}, u32[]{:S(2)}, u32[]{:S(2)}) collective-permute-start(f32[32,128]{1,0:T(8,128)S(1)} %get-tuple-element.29.refs_0_), channel_id=1, source_target_pairs={{0,3},{1,2},{2,1},{3,0},{4,7},{5,6},{6,5},{7,4},{8,11},{9,10},{10,... | collective-permute-start | bytes 49160 | tf_op jit(solution)/shard_map/ppermute | solution.py:395
  17.8 1.1 %collective-permute-start.6 = (f32[32,128]{1,0:T(8,128)S(1)}, f32[32,128]{1,0:T(8,128)S(1)}, u32[]{:S(2)}, u32[]{:S(2)}) collective-permute-start(f32[32,128]{1,0:T(8,128)S(1)} %get-tuple-element.29.refs_0_), channel_id=1, source_target_pairs={{0,2},{1,3},{2,0},{3,1},{4,6},{5,7},{6,4},{7,5},{8,10},{9,11},{10,... | collective-permute-start | bytes 49160 | tf_op jit(solution)/shard_map/ppermute | solution.py:395
  18.9 1.1 %collective-permute-start.5 = (f32[32,128]{1,0:T(8,128)S(1)}, f32[32,128]{1,0:T(8,128)S(1)}, u32[]{:S(2)}, u32[]{:S(2)}) collective-permute-start(f32[32,128]{1,0:T(8,128)S(1)} %get-tuple-element.29.refs_0_), channel_id=1, source_target_pairs={{0,1},{1,0},{2,3},{3,2},{4,5},{5,4},{6,7},{7,6},{8,9},{9,8},{10,11... | collective-permute-start | bytes 49160 | tf_op jit(solution)/shard_map/ppermute | solution.py:395
  20.0 1.3 %collective-permute-done.6.refs_2_ = f32[32,128]{1,0:T(8,128)S(1)} collective-permute-done((f32[32,128]{1,0:T(8,128)S(1)}, f32[32,128]{1,0:T(8,128)S(1)}, u32[]{:S(2)}, u32[]{:S(2)}) %collective-permute-start.6) | collective-permute-done | bytes 16416 | tf_op jit(solution)/shard_map/ppermute | solution.py:395
  21.5 3.2 %next_chain.4 = (f32[8,64,128]{2,1,0:T(8,128)S(1)}, f32[8,64,128]{2,1,0:T(8,128)S(1)}, f32[64,128]{1,0:T(8,128)S(1)}, f32[64,128]{1,0:T(8,128)S(1)}, f32[8,128]{1,0:T(8,128)S(1)}, /*index=5*/f32[8,24,128]{2,1,0:T(8,128)S(1)}) custom-call(f32[32,128]{1,0:T(8,128)S(1)} %get-tuple-element.29.refs_0_, f32[32,128]{1,0:T(8,128)S(1)} %collective-permute-done.5.refs_1_, ...), custom_call_target="tpu_custom_call" | custom-call | tf_op jit(solution)/shard_map/next_chain/pallas_call | solution.py:376
  24.7 2.4 %collective-permute-start.10 = (f32[8,128]{1,0:T(8,128)S(1)}, f32[8,128]{1,0:T(8,128)S(1)}, u32[]{:S(2)}, u32[]{:S(2)}) collective-permute-start(f32[8,128]{1,0:T(8,128)S(1)} %get-tuple-element.32.refs_0_), channel_id=1, source_target_pairs={{0,3},{1,2},{2,1},{3,0},{4,7},{5,6},{6,5},{7,4},{8,11},{9,10},{10,... | collective-permute-start | bytes 12296 | tf_op jit(solution)/shard_map/ppermute | solution.py:395
  27.0 1.8 %collective-permute-start.9 = (f32[8,128]{1,0:T(8,128)S(1)}, f32[8,128]{1,0:T(8,128)S(1)}, u32[]{:S(2)}, u32[]{:S(2)}) collective-permute-start(f32[8,128]{1,0:T(8,128)S(1)} %get-tuple-element.32.refs_0_), channel_id=1, source_target_pairs={{0,2},{1,3},{2,0},{3,1},{4,6},{5,7},{6,4},{7,5},{8,10},{9,11},{10,... | collective-permute-start | bytes 12296 | tf_op jit(solution)/shard_map/ppermute | solution.py:395
  28.8 1.5 %collective-permute-done.9.refs_2_ = f32[8,128]{1,0:T(8,128)S(1)} collective-permute-done((f32[8,128]{1,0:T(8,128)S(1)}, f32[8,128]{1,0:T(8,128)S(1)}, u32[]{:S(2)}, u32[]{:S(2)}) %collective-permute-start.9) | collective-permute-done | bytes 4128 | tf_op jit(solution)/shard_map/ppermute | solution.py:395
  30.4 0.9 %collective-permute-done.8.refs_1_ = f32[8,128]{1,0:T(8,128)S(1)} collective-permute-done((f32[8,128]{1,0:T(8,128)S(1)}, f32[8,128]{1,0:T(8,128)S(1)}, u32[]{:S(2)}, u32[]{:S(2)}) %collective-permute-start.8) | collective-permute-done | bytes 4128 | tf_op jit(solution)/shard_map/ppermute | solution.py:395
  31.3 3.1 %next_chain.5 = (f32[8,64,128]{2,1,0:T(8,128)S(1)}, f32[8,64,128]{2,1,0:T(8,128)S(1)}, f32[64,128]{1,0:T(8,128)S(1)}, f32[64,128]{1,0:T(8,128)S(1)}, f32[8,128]{1,0:T(8,128)S(1)}) custom-call(f32[8,128]{1,0:T(8,128)S(1)} %get-tuple-element.32.refs_0_, f32[8,128]{1,0:T(8,128)S(1)} %collective-permute-done.8.refs_1_, ...), custom_call_target="tpu_custom_call" | custom-call | tf_op jit(solution)/shard_map/next_chain/pallas_call | solution.py:376
  34.7 2.2 %collective-permute-start.12 = (f32[8,128]{1,0:T(8,128)S(1)}, f32[8,128]{1,0:T(8,128)S(1)}, u32[]{:S(2)}, u32[]{:S(2)}) collective-permute-start(f32[8,128]{1,0:T(8,128)S(1)} %get-tuple-element.38.refs_0_), channel_id=1, source_target_pairs={{0,2},{1,3},{2,0},{3,1},{4,6},{5,7},{6,4},{7,5},{8,10},{9,11},{10,... | collective-permute-start | bytes 12296 | tf_op jit(solution)/shard_map/ppermute | solution.py:395
  37.1 1.0 %collective-permute-done.12.refs_2_ = f32[8,128]{1,0:T(8,128)S(1)} collective-permute-done((f32[8,128]{1,0:T(8,128)S(1)}, f32[8,128]{1,0:T(8,128)S(1)}, u32[]{:S(2)}, u32[]{:S(2)}) %collective-permute-start.12) | collective-permute-done | bytes 4128 | tf_op jit(solution)/shard_map/ppermute | solution.py:395
  38.1 1.3 %collective-permute-done.11.refs_1_ = f32[8,128]{1,0:T(8,128)S(1)} collective-permute-done((f32[8,128]{1,0:T(8,128)S(1)}, f32[8,128]{1,0:T(8,128)S(1)}, u32[]{:S(2)}, u32[]{:S(2)}) %collective-permute-start.11) | collective-permute-done | bytes 4128 | tf_op jit(solution)/shard_map/ppermute | solution.py:395
  39.4 2.7 %next_chain.6 = (f32[8,64,128]{2,1,0:T(8,128)S(1)}, f32[8,64,128]{2,1,0:T(8,128)S(1)}, f32[64,128]{1,0:T(8,128)S(1)}, f32[64,128]{1,0:T(8,128)S(1)}, f32[8,128]{1,0:T(8,128)S(1)}) custom-call(f32[8,128]{1,0:T(8,128)S(1)} %get-tuple-element.38.refs_0_, f32[8,128]{1,0:T(8,128)S(1)} %collective-permute-done.11.refs_1_, ...), custom_call_target="tpu_custom_call" | custom-call | tf_op jit(solution)/shard_map/next_chain/pallas_call | solution.py:376
  42.2 0.8 %collective-permute-start.16 = (f32[8,128]{1,0:T(8,128)S(1)}, f32[8,128]{1,0:T(8,128)S(1)}, u32[]{:S(2)}, u32[]{:S(2)}) collective-permute-start(f32[8,128]{1,0:T(8,128)S(1)} %get-tuple-element.43.refs_0_), channel_id=1, source_target_pairs={{0,3},{1,2},{2,1},{3,0},{4,7},{5,6},{6,5},{7,4},{8,11},{9,10},{10,... | collective-permute-start | bytes 12296 | tf_op jit(solution)/shard_map/ppermute | solution.py:395
  43.0 2.1 %collective-permute-start.15 = (f32[8,128]{1,0:T(8,128)S(1)}, f32[8,128]{1,0:T(8,128)S(1)}, u32[]{:S(2)}, u32[]{:S(2)}) collective-permute-start(f32[8,128]{1,0:T(8,128)S(1)} %get-tuple-element.43.refs_0_), channel_id=1, source_target_pairs={{0,2},{1,3},{2,0},{3,1},{4,6},{5,7},{6,4},{7,5},{8,10},{9,11},{10,... | collective-permute-start | bytes 12296 | tf_op jit(solution)/shard_map/ppermute | solution.py:395
  45.1 1.3 %collective-permute-done.15.refs_2_ = f32[8,128]{1,0:T(8,128)S(1)} collective-permute-done((f32[8,128]{1,0:T(8,128)S(1)}, f32[8,128]{1,0:T(8,128)S(1)}, u32[]{:S(2)}, u32[]{:S(2)}) %collective-permute-start.15) | collective-permute-done | bytes 4128 | tf_op jit(solution)/shard_map/ppermute | solution.py:395
  46.3 1.2 %collective-permute-done.14.refs_1_ = f32[8,128]{1,0:T(8,128)S(1)} collective-permute-done((f32[8,128]{1,0:T(8,128)S(1)}, f32[8,128]{1,0:T(8,128)S(1)}, u32[]{:S(2)}, u32[]{:S(2)}) %collective-permute-start.14) | collective-permute-done | bytes 4128 | tf_op jit(solution)/shard_map/ppermute | solution.py:395
  47.5 2.2 %copy-done.1 = f32[8192,128]{1,0:T(8,128)S(1)} copy-done((f32[8192,128]{1,0:T(8,128)S(1)}, f32[8192,128]{1,0:T(8,128)}, u32[]{:S(2)}) %copy-start.1) | copy-done | bytes 4194328
  49.7 2.6 %next_chain.7 = (f32[8,32,128]{2,1,0:T(8,128)S(1)}, f32[8,64,128]{2,1,0:T(8,128)}, f32[8,64,128]{2,1,0:T(8,128)}, f32[64,128]{1,0:T(8,128)}) custom-call(f32[8,128]{1,0:T(8,128)S(1)} %get-tuple-element.43.refs_0_, f32[8,128]{1,0:T(8,128)S(1)} %collective-permute-done.14.refs_1_, f32[8,128]{1,0:T(8,128)S(1)} %collective-permute-done.15.refs_2_, ...), custom_call_target="tpu_custom_call" | custom-call | tf_op jit(solution)/shard_map/next_chain/pallas_call | solution.py:376
  52.3 10.6 %collective-permute-start.19 = (f32[2,32,128]{2,1,0:T(8,128)S(1)}, f32[2,32,128]{2,1,0:T(8,128)S(1)}, u32[]{:S(2)}, u32[]{:S(2)}) collective-permute-start(f32[2,32,128]{2,1,0:T(8,128)S(1)} %get-tuple-element.53), channel_id=1, source_target_pairs={{0,24},{8,16},{16,8},{24,0},{1,25},{9,17},{17,9},{25,1},{2,26},{10... | collective-permute-start | bytes 98312 | tf_op jit(solution)/shard_map/ppermute | solution.py:395
  62.9 3.9 %collective-permute-start.18 = (f32[2,32,128]{2,1,0:T(8,128)S(1)}, f32[2,32,128]{2,1,0:T(8,128)S(1)}, u32[]{:S(2)}, u32[]{:S(2)}) collective-permute-start(f32[2,32,128]{2,1,0:T(8,128)S(1)} %get-tuple-element.54), channel_id=1, source_target_pairs={{0,16},{8,24},{16,0},{24,8},{1,17},{9,25},{17,1},{25,9},{2,18},{10... | collective-permute-start | bytes 98312 | tf_op jit(solution)/shard_map/ppermute | solution.py:395
  66.9 2.0 %collective-permute-done.18.refs_2_ = f32[2,32,128]{2,1,0:T(8,128)S(1)} collective-permute-done((f32[2,32,128]{2,1,0:T(8,128)S(1)}, f32[2,32,128]{2,1,0:T(8,128)S(1)}, u32[]{:S(2)}, u32[]{:S(2)}) %collective-permute-start.18) | collective-permute-done | bytes 32800 | tf_op jit(solution)/shard_map/ppermute | solution.py:395
  68.9 0.7 finish.1
  (28 shorter events, 1.5 us)
Async XLA Ops:
  1.3 11.3 %collective-permute-start.4 = (f32[16,128,128]{2,1,0:T(8,128)S(1)}, f32[16,128,128]{2,1,0:T(8,128)S(1)}, u32[]{:S(2)}, u32[]{:S(2)}) collective-permute-start(f32[16,128,128]{2,1,0:T(8,128)S(1)} %constant_dynamic-slice_fusion.4), channel_id=1, source_target_pairs={{8,4},{20,24},{9,5},{21,25},{10,6},{22,26},{11,7},{23,27}} | collective-permute-start | bytes 3145736 | tf_op jit(solution)/shard_map/ppermute | solution.py:426
  3.1 8.6 %collective-permute-start.2 = (f32[2,2,64,128]{3,2,1,0:T(8,128)S(1)}, f32[2,2,64,128]{3,2,1,0:T(8,128)S(1)}, u32[]{:S(2)}, u32[]{:S(2)}) collective-permute-start(f32[2,2,64,128]{3,2,1,0:T(8,128)S(1)} %get-tuple-element.49), channel_id=1, source_target_pairs={{0,24},{8,16},{16,8},{24,0},{1,25},{9,17},{17,9},{25,1},{2,26},{10... | collective-permute-start | bytes 393224 | tf_op jit(solution)/shard_map/ppermute | solution.py:395
  6.2 5.7 %collective-permute-start.1 = (f32[2,2,64,128]{3,2,1,0:T(8,128)S(1)}, f32[2,2,64,128]{3,2,1,0:T(8,128)S(1)}, u32[]{:S(2)}, u32[]{:S(2)}) collective-permute-start(f32[2,2,64,128]{3,2,1,0:T(8,128)S(1)} %get-tuple-element.50), channel_id=1, source_target_pairs={{0,16},{8,24},{16,0},{24,8},{1,17},{9,25},{17,1},{25,9},{2,18},{10... | collective-permute-start | bytes 393224 | tf_op jit(solution)/shard_map/ppermute | solution.py:395
  6.2 5.7 %collective-permute-start = (f32[2,2,64,128]{3,2,1,0:T(8,128)S(1)}, f32[2,2,64,128]{3,2,1,0:T(8,128)S(1)}, u32[]{:S(2)}, u32[]{:S(2)}) collective-permute-start(f32[2,2,64,128]{3,2,1,0:T(8,128)S(1)} %get-tuple-element.51), channel_id=1, source_target_pairs={{0,8},{8,0},{16,24},{24,16},{1,9},{9,1},{17,25},{25,17},{2,10},{10... | collective-permute-start | bytes 393224 | tf_op jit(solution)/shard_map/ppermute | solution.py:395
  12.0 2.9 %collective-permute-start.3 = (f32[4,2,2,16,128]{4,3,2,1,0:T(8,128)S(1)}, f32[4,2,2,16,128]{4,3,2,1,0:T(8,128)S(1)}, u32[]{:S(2)}, u32[]{:S(2)}) collective-permute-start(f32[4,2,2,16,128]{4,3,2,1,0:T(8,128)S(1)} %ghost_pack.1), channel_id=1, source_target_pairs={{24,4},{4,24},{25,5},{5,25},{26,6},{6,26},{27,7},{7,27}} | collective-permute-start | bytes 393224 | tf_op jit(solution)/shard_map/ppermute | solution.py:442
  12.7 26.8 %copy-start = (f32[8192,128]{1,0:T(8,128)}, f32[8192,128]{1,0:T(8,128)S(1)}, u32[]{:S(2)}) copy-start(f32[8192,128]{1,0:T(8,128)S(1)} %patch.1.b_ref.refs_5_.refs_4_) | copy-start | bytes 12582916
  16.4 3.6 %collective-permute-start.7 = (f32[32,128]{1,0:T(8,128)S(1)}, f32[32,128]{1,0:T(8,128)S(1)}, u32[]{:S(2)}, u32[]{:S(2)}) collective-permute-start(f32[32,128]{1,0:T(8,128)S(1)} %get-tuple-element.29.refs_0_), channel_id=1, source_target_pairs={{0,3},{1,2},{2,1},{3,0},{4,7},{5,6},{6,5},{7,4},{8,11},{9,10},{10,... | collective-permute-start | bytes 49160 | tf_op jit(solution)/shard_map/ppermute | solution.py:395
  17.8 3.5 %collective-permute-start.6 = (f32[32,128]{1,0:T(8,128)S(1)}, f32[32,128]{1,0:T(8,128)S(1)}, u32[]{:S(2)}, u32[]{:S(2)}) collective-permute-start(f32[32,128]{1,0:T(8,128)S(1)} %get-tuple-element.29.refs_0_), channel_id=1, source_target_pairs={{0,2},{1,3},{2,0},{3,1},{4,6},{5,7},{6,4},{7,5},{8,10},{9,11},{10,... | collective-permute-start | bytes 49160 | tf_op jit(solution)/shard_map/ppermute | solution.py:395
  18.9 2.6 %collective-permute-start.5 = (f32[32,128]{1,0:T(8,128)S(1)}, f32[32,128]{1,0:T(8,128)S(1)}, u32[]{:S(2)}, u32[]{:S(2)}) collective-permute-start(f32[32,128]{1,0:T(8,128)S(1)} %get-tuple-element.29.refs_0_), channel_id=1, source_target_pairs={{0,1},{1,0},{2,3},{3,2},{4,5},{5,4},{6,7},{7,6},{8,9},{9,8},{10,11... | collective-permute-start | bytes 49160 | tf_op jit(solution)/shard_map/ppermute | solution.py:395
  24.6 44.2 %copy-start.2 = (f32[2,128,128]{2,1,0:T(8,128)S(1)}, f32[2,128,128]{2,1,0:T(8,128)}, u32[]{:S(2)}) copy-start(f32[2,128,128]{2,1,0:T(8,128)} %v_ref.1) | copy-start | bytes 393220
  24.7 4.2 %collective-permute-start.10 = (f32[8,128]{1,0:T(8,128)S(1)}, f32[8,128]{1,0:T(8,128)S(1)}, u32[]{:S(2)}, u32[]{:S(2)}) collective-permute-start(f32[8,128]{1,0:T(8,128)S(1)} %get-tuple-element.32.refs_0_), channel_id=1, source_target_pairs={{0,3},{1,2},{2,1},{3,0},{4,7},{5,6},{6,5},{7,4},{8,11},{9,10},{10,... | collective-permute-start | bytes 12296 | tf_op jit(solution)/shard_map/ppermute | solution.py:395
  27.0 3.4 %collective-permute-start.9 = (f32[8,128]{1,0:T(8,128)S(1)}, f32[8,128]{1,0:T(8,128)S(1)}, u32[]{:S(2)}, u32[]{:S(2)}) collective-permute-start(f32[8,128]{1,0:T(8,128)S(1)} %get-tuple-element.32.refs_0_), channel_id=1, source_target_pairs={{0,2},{1,3},{2,0},{3,1},{4,6},{5,7},{6,4},{7,5},{8,10},{9,11},{10,... | collective-permute-start | bytes 12296 | tf_op jit(solution)/shard_map/ppermute | solution.py:395
  28.8 2.5 %collective-permute-start.8 = (f32[8,128]{1,0:T(8,128)S(1)}, f32[8,128]{1,0:T(8,128)S(1)}, u32[]{:S(2)}, u32[]{:S(2)}) collective-permute-start(f32[8,128]{1,0:T(8,128)S(1)} %get-tuple-element.32.refs_0_), channel_id=1, source_target_pairs={{0,1},{1,0},{2,3},{3,2},{4,5},{5,4},{6,7},{7,6},{8,9},{9,8},{10,11... | collective-permute-start | bytes 12296 | tf_op jit(solution)/shard_map/ppermute | solution.py:395
  34.4 2.7 %collective-permute-start.13 = (f32[8,128]{1,0:T(8,128)S(1)}, f32[8,128]{1,0:T(8,128)S(1)}, u32[]{:S(2)}, u32[]{:S(2)}) collective-permute-start(f32[8,128]{1,0:T(8,128)S(1)} %get-tuple-element.38.refs_0_), channel_id=1, source_target_pairs={{0,3},{1,2},{2,1},{3,0},{4,7},{5,6},{6,5},{7,4},{8,11},{9,10},{10,... | collective-permute-start | bytes 12296 | tf_op jit(solution)/shard_map/ppermute | solution.py:395
  34.7 3.4 %collective-permute-start.12 = (f32[8,128]{1,0:T(8,128)S(1)}, f32[8,128]{1,0:T(8,128)S(1)}, u32[]{:S(2)}, u32[]{:S(2)}) collective-permute-start(f32[8,128]{1,0:T(8,128)S(1)} %get-tuple-element.38.refs_0_), channel_id=1, source_target_pairs={{0,2},{1,3},{2,0},{3,1},{4,6},{5,7},{6,4},{7,5},{8,10},{9,11},{10,... | collective-permute-start | bytes 12296 | tf_op jit(solution)/shard_map/ppermute | solution.py:395
  37.0 2.5 %collective-permute-start.11 = (f32[8,128]{1,0:T(8,128)S(1)}, f32[8,128]{1,0:T(8,128)S(1)}, u32[]{:S(2)}, u32[]{:S(2)}) collective-permute-start(f32[8,128]{1,0:T(8,128)S(1)} %get-tuple-element.38.refs_0_), channel_id=1, source_target_pairs={{0,1},{1,0},{2,3},{3,2},{4,5},{5,4},{6,7},{7,6},{8,9},{9,8},{10,11... | collective-permute-start | bytes 12296 | tf_op jit(solution)/shard_map/ppermute | solution.py:395
  42.2 2.9 %collective-permute-start.16 = (f32[8,128]{1,0:T(8,128)S(1)}, f32[8,128]{1,0:T(8,128)S(1)}, u32[]{:S(2)}, u32[]{:S(2)}) collective-permute-start(f32[8,128]{1,0:T(8,128)S(1)} %get-tuple-element.43.refs_0_), channel_id=1, source_target_pairs={{0,3},{1,2},{2,1},{3,0},{4,7},{5,6},{6,5},{7,4},{8,11},{9,10},{10,... | collective-permute-start | bytes 12296 | tf_op jit(solution)/shard_map/ppermute | solution.py:395
  43.0 3.4 %collective-permute-start.15 = (f32[8,128]{1,0:T(8,128)S(1)}, f32[8,128]{1,0:T(8,128)S(1)}, u32[]{:S(2)}, u32[]{:S(2)}) collective-permute-start(f32[8,128]{1,0:T(8,128)S(1)} %get-tuple-element.43.refs_0_), channel_id=1, source_target_pairs={{0,2},{1,3},{2,0},{3,1},{4,6},{5,7},{6,4},{7,5},{8,10},{9,11},{10,... | collective-permute-start | bytes 12296 | tf_op jit(solution)/shard_map/ppermute | solution.py:395
  45.1 2.5 %collective-permute-start.14 = (f32[8,128]{1,0:T(8,128)S(1)}, f32[8,128]{1,0:T(8,128)S(1)}, u32[]{:S(2)}, u32[]{:S(2)}) collective-permute-start(f32[8,128]{1,0:T(8,128)S(1)} %get-tuple-element.43.refs_0_), channel_id=1, source_target_pairs={{0,1},{1,0},{2,3},{3,2},{4,5},{5,4},{6,7},{7,6},{8,9},{9,8},{10,11... | collective-permute-start | bytes 12296 | tf_op jit(solution)/shard_map/ppermute | solution.py:395
  47.5 2.2 %copy-start.1 = (f32[8192,128]{1,0:T(8,128)S(1)}, f32[8192,128]{1,0:T(8,128)}, u32[]{:S(2)}) copy-start(f32[8192,128]{1,0:T(8,128)} %copy-done) | copy-start | bytes 12582916
  52.3 14.6 %collective-permute-start.19 = (f32[2,32,128]{2,1,0:T(8,128)S(1)}, f32[2,32,128]{2,1,0:T(8,128)S(1)}, u32[]{:S(2)}, u32[]{:S(2)}) collective-permute-start(f32[2,32,128]{2,1,0:T(8,128)S(1)} %get-tuple-element.53), channel_id=1, source_target_pairs={{0,24},{8,16},{16,8},{24,0},{1,25},{9,17},{17,9},{25,1},{2,26},{10... | collective-permute-start | bytes 98312 | tf_op jit(solution)/shard_map/ppermute | solution.py:395
  62.9 6.0 %collective-permute-start.18 = (f32[2,32,128]{2,1,0:T(8,128)S(1)}, f32[2,32,128]{2,1,0:T(8,128)S(1)}, u32[]{:S(2)}, u32[]{:S(2)}) collective-permute-start(f32[2,32,128]{2,1,0:T(8,128)S(1)} %get-tuple-element.54), channel_id=1, source_target_pairs={{0,16},{8,24},{16,0},{24,8},{1,17},{9,25},{17,1},{25,9},{2,18},{10... | collective-permute-start | bytes 98312 | tf_op jit(solution)/shard_map/ppermute | solution.py:395
  66.8 2.0 %collective-permute-start.17 = (f32[2,32,128]{2,1,0:T(8,128)S(1)}, f32[2,32,128]{2,1,0:T(8,128)S(1)}, u32[]{:S(2)}, u32[]{:S(2)}) collective-permute-start(f32[2,32,128]{2,1,0:T(8,128)S(1)} %get-tuple-element.55), channel_id=1, source_target_pairs={{0,8},{8,0},{16,24},{24,16},{1,9},{9,1},{17,25},{25,17},{2,10},{10... | collective-permute-start | bytes 98312 | tf_op jit(solution)/shard_map/ppermute | solution.py:395

commit v3 on v2

--- a/solution.py
+++ b/solution.py
@@ -11,6 +11,7 @@
 HALF = 64
 STEPS = 4
 SPREAD = [(k, side, delta) for k in range(1, STEPS) for side in range(2) for delta in range(1 - k, k)]
+PLANES = sum(k <= 2 for k, _, _ in SPREAD)
 PACK_ROWS = 8 * (-(-(STEPS + len(SPREAD)) // 8))
 VMEM = pl.BlockSpec(memory_space=pltpu.VMEM)
 HBM = pl.BlockSpec(memory_space=pltpu.HBM)
@@ -72,18 +73,32 @@
 
 
 def apply_blocks(b_ref, rhs, out_ref):
-    halves = spread(rhs)
-    tiles = [half[8 * t : 8 * t + 8] for half in halves for t in range(HALF // 8)]
-    for outer in range(HALF // 8):
+    tiles = [half[8 * t : 8 * t + 8] for half in spread(rhs) for t in range(HALF // 8)]
+
+    def rows(outer, carry):
         parts = []
         for u in range(8):
             at = (outer * 8 + u) * LANES
-            terms = [b_ref[at + 8 * t : at + 8 * t + 8, :] * tiles[t] for t in range(2)]
+            terms = [b_ref[pl.ds(at + 8 * t, 8), :] * tiles[t] for t in range(2)]
             for t in range(2, len(tiles)):
-                terms[t % 2] = terms[t % 2] + b_ref[at + 8 * t : at + 8 * t + 8, :] * tiles[t]
+                terms[t % 2] = terms[t % 2] + b_ref[pl.ds(at + 8 * t, 8), :] * tiles[t]
             parts.append(terms[0] + terms[1])
-        out_ref[outer * 8 : outer * 8 + 8, :] = fold_rows(parts)
+        out_ref[pl.ds(outer * 8, 8), :] = fold_rows(parts)
+        return carry
+
+    lax.fori_loop(0, HALF // 8, rows, 0, unroll=True)
     return out_ref[...]
+
+
+def edge_rows(b_ref):
+    return jnp.where(
+        low_lanes(LANES), b_ref[0:LANES, :], b_ref[(HALF - 1) * LANES : HALF * LANES, :]
+    )
+
+
+def apply_edges(rows, rhs):
+    top, bottom = spread(rhs)
+    return jnp.sum(rows[:HALF] * top + rows[HALF:] * bottom, axis=0, keepdims=True)
 
 
 def layout_kernel(own, ghost, axis, b_ref, *refs):
@@ -124,6 +139,45 @@
         return carry
 
     lax.fori_loop(0, HALF // 8, one, 0)
+
+
+def tail_kernel(axis, groups, b_ref, tail_ref, sems):
+    ghost = tail_ref.shape[0]
+    start = jnp.where(lax.axis_index(axis) < groups // 2, b_ref.shape[0] - ghost, 0)
+    part = ghost // 4
+    copies = [
+        pltpu.make_async_copy(
+            b_ref.at[pl.ds(start + n * part, part)], tail_ref.at[pl.ds(n * part, part)], sems.at[n]
+        )
+        for n in range(4)
+    ]
+    for copy in copies:
+        copy.start()
+    for copy in copies:
+        copy.wait()
+
+
+def pack_kernel(axis, own, ghost, v_ref, s_ref, *refs):
+    *window_refs, sems = refs
+    position = lax.axis_index(axis)
+    last = v_ref.shape[1] - ghost
+    copies = []
+    for k, window_ref in enumerate(window_refs):
+        peer = jnp.bitwise_xor(position, k)
+        for c in range(HALF // ghost):
+            at = pl.multiple_of(jnp.clip(peer * own - ghost + c * ghost, 0, last), ghost)
+            for kind, ref in enumerate((v_ref, s_ref)):
+                copies.append(
+                    pltpu.make_async_copy(
+                        ref.at[:, pl.ds(at, ghost), :],
+                        window_ref.at[kind, :, pl.ds(c * ghost, ghost), :],
+                        sems.at[len(copies)],
+                    )
+                )
+    for copy in copies:
+        copy.start()
+    for copy in copies:
+        copy.wait()
 
 
 def patch_kernel(axis, groups, b_in, beyond, out_ref):
@@ -159,50 +213,67 @@
             lax.fori_loop(0, HALF // per_turn // unroll, one, 0)
 
 
-def responses_kernel(b_ref, pack_ref, r_ref):
+def responses_kernel(b_ref, pack_ref, plane_ref, r_ref, many_ref):
     pack_ref[...] = jnp.zeros(pack_ref.shape, jnp.float32)
-    low_all = low_lanes(LANES)
-    edge_rows = jnp.where(
-        low_all,
-        b_ref[0:LANES, :],
-        b_ref[(HALF - 1) * LANES : HALF * LANES, :],
-    )
     firsts = [block_column(b_ref, 0), block_column(b_ref, LANES - 1)]
-    shifted = [sum_y(a) for a in firsts]
-    plan = [(side, delta) for side in range(2) for delta in (-1, 0, 1)]
-    second = {
-        (side, delta): apply_blocks(b_ref, from_line(shifted[side], delta), r_ref)
-        for side, delta in plan
-    }
+    for side, first in enumerate(firsts):
+        many_ref[side] = first
+        shifted = sum_y(first)
+        for n, (k, at_side, delta) in enumerate(SPREAD):
+            if k == 2 and at_side == side:
+                many_ref[n] = from_line(shifted, delta)
+
+    def product(n, carry):
+        many_ref[n] = apply_blocks(b_ref, many_ref[n], r_ref)
+        return carry
+
+    lax.fori_loop(2, PLANES, product, 0, unroll=True)
+    second = {SPREAD[n][1:]: many_ref[n] for n in range(2, PLANES)}
+    rows = edge_rows(b_ref)
     for n, (k, side, delta) in enumerate(SPREAD):
-        if k == 1:
-            row = edges(firsts[side])
-        elif k == 2:
-            row = edges(second[side, delta])
+        if k <= 2:
+            row = edges(many_ref[n])
         else:
             parts = [
                 from_line(second[side, delta - m], m) for m in (-1, 0, 1) if abs(delta - m) <= 1
             ]
-            top, bottom = spread(sum_y(sum(parts[1:], parts[0])))
-            row = jnp.sum(edge_rows[:HALF] * top + edge_rows[HALF:] * bottom, axis=0, keepdims=True)
+            row = apply_edges(rows, sum_y(sum(parts[1:], parts[0])))
         pack_ref[pl.ds(STEPS + n, 1), :] = row
-
-
-def local_chain(steps, b_ref, rhs_ref, add_ref, state, r_ref, pack_ref, first_loc_ref):
-    nz = rhs_ref.shape[0]
-    if state is not None:
+    plane_ref[...] = many_ref[...]
+
+
+def planes_of(steps, nz):
+    return (steps[0], 1) if steps[0] < nz else (2 * nz - 1 - steps[0], -1)
+
+
+def local_chain(steps, b_ref, rhs_ref, add_ref, state, r_ref, pack_ref, loc_ref):
+    first, move = planes_of(steps, rhs_ref.shape[0])
+    if state is None:
+        state = jnp.zeros((HALF, LANES), jnp.float32)
+    else:
         pack_ref[0:1, :] = edges(state)
-    for n, step in enumerate(steps[:-1]):
-        z = step if step < nz else 2 * nz - 1 - step
-        rhs = rhs_ref[z]
-        if state is not None:
-            rhs = rhs + sum_y(sum_x(state))
-        state = apply_blocks(b_ref, rhs, r_ref)
-        if step >= nz:
+    ahead = len(steps) - 2
+
+    def transition(n, state):
+        z = first + move * n
+        state = apply_blocks(b_ref, rhs_ref[z] + sum_y(sum_x(state)), r_ref)
+        if move < 0:
             state = state + add_ref[z]
-        if n == 0:
-            first_loc_ref[...] = state
-        pack_ref[n + 1 : n + 2, :] = edges(state)
+        loc_ref[n] = state
+        pack_ref[pl.ds(n + 1, 1), :] = edges(state)
+        return state
+
+    state = lax.fori_loop(0, ahead, transition, state, unroll=True)
+    z = first + move * ahead
+    row = apply_edges(edge_rows(b_ref), rhs_ref[z] + sum_y(sum_x(state)))
+    pack_ref[ahead + 1 : ahead + 2, :] = row + edges(add_ref[z]) if move < 0 else row
+
+
+def copy_pack(pack_refs):
+    first = pack_refs[0][...]
+    for ref in pack_refs[1:]:
+        ref[: first.shape[0], :] = first
+        ref[first.shape[0] :, :] = jnp.zeros((ref.shape[0] - first.shape[0], LANES), jnp.float32)
 
 
 def gather_planes(axis, groups, field_refs, ghost_ref, v_ref, s_ref):
@@ -228,7 +299,8 @@
     field_refs = refs[:fields]
     ghost_ref = refs[fields] if late else None
     refs = refs[1:] if late else refs
-    b_ref, answers_ref, rhs_ref, loc_ref, pack_ref, v_ref, s_ref, r_ref = refs[fields:]
+    b_ref, answers_ref, rhs_ref, loc_ref, *pack_refs, v_ref, s_ref, r_ref = refs[fields:]
+    pack_ref = pack_refs[0]
     nz = rhs_ref.shape[0]
     pack_ref[...] = jnp.zeros(pack_ref.shape, jnp.float32)
     pack_ref[:PACK_ROWS, :] = answers_ref[...]
@@ -240,37 +312,51 @@
         rhs_ref[z] = s_ref[z] - 27.0 * v_ref[z + 1] + sum_y(sum_x(around))
         pack_ref[PACK_ROWS + z : PACK_ROWS + z + 1, :] = edges(around)
     local_chain(list(range(STEPS)), b_ref, rhs_ref, None, None, r_ref, pack_ref, loc_ref)
-
-
-def halo_of(ends):
-    swapped = swap_halves(ends)
-    return sum_x(jnp.where(low_lanes(8), pltpu.roll(swapped, 1, 0), pltpu.roll(swapped, 7, 0)))
-
-
-def lines_both(row):
-    swapped = swap_halves(row)
+    copy_pack(pack_refs)
+
+
+def beside(ends, swapped):
     low = low_lanes(8)
-    return jnp.where(low, row, swapped), jnp.where(low, swapped, row)
+    left = pltpu.roll(jnp.where(low, swapped, ends), 1, 0)
+    right = pltpu.roll(jnp.where(low, ends, swapped), 7, 0)
+    return left, right
 
 
 def complete_edges(first, gather, coef_ref, halo_ref, inject_ref):
-    injected = []
-    ends = None if first else gather[:, 0, :]
+    low = low_lanes(8)
+    known = [gather[:, t, :] for t in range(STEPS)]
+    totals = [(row, swap_halves(row)) for row in known]
     for t in range(STEPS):
-        halo = jnp.zeros((8, LANES), jnp.float32) if ends is None else halo_of(ends)
-        halo_ref[t] = halo
+        halo = None if first and t == 0 else beside(*totals[t])
+        if halo is None:
+            halo_ref[t] = jnp.zeros((8, LANES), jnp.float32)
+        else:
+            halo_ref[t] = sum_x(jnp.where(low, *halo))
         if first:
-            halo = halo + halo_of(gather[:, PACK_ROWS + t, :])
-        injected.append(lines_both(halo))
-        if t == 0:
-            inject_ref[0], inject_ref[1] = injected[0]
-        if t < STEPS - 1:
-            ends = gather[:, t + 1, :]
-            for n, (k, side, delta) in enumerate(SPREAD):
-                if k <= t + 1:
-                    ends = ends + coef_ref[:, STEPS + n, :] * from_line(
-                        injected[t + 1 - k][side], delta
-                    )
+            row = gather[:, PACK_ROWS + t, :]
+            start = beside(row, swap_halves(row))
+            halo = start if halo is None else [x + y for x, y in zip(halo, start)]
+        reach = STEPS - 1 - t
+        width = max(reach - 1, 1 if t == 0 else 0)
+        if reach < 1:
+            break
+        summed = []
+        for cells in halo:
+            moved = {m: from_line(cells, m) for m in range(-width - 1, width + 2)}
+            summed.append(
+                {m: moved[m - 1] + moved[m] + moved[m + 1] for m in range(-width, width + 1)}
+            )
+        for n, (k, side, delta) in enumerate(SPREAD):
+            if k <= reach:
+                coef = coef_ref[:, STEPS + n, :]
+                ends, swapped = totals[t + k]
+                totals[t + k] = (
+                    ends + coef * summed[side][delta],
+                    swapped + swap_halves(coef) * summed[side][delta],
+                )
+        if t < 2:
+            for n, (k, side, delta) in enumerate(SPREAD[: PLANES if t == 0 else 2]):
+                inject_ref[t * PLANES + n] = summed[side][delta]
 
 
 def ghost_pack_kernel(axis, own, ghost, *refs):
@@ -289,63 +375,79 @@
         return taken
 
     packs = take(peers)
-    b_ref, rhs_in, loc_in = take(3)
+    b_ref, plane_ref, rhs_in, loc_in = take(4)
     coef_ref, add_in, state_in = (None, None, None) if first else take(3)
     last = steps is not None and steps[-1] == 2 * rhs_in.shape[0] - 1
     out_ref = take(1)[0] if last else None
     rhs_ref, add_ref, state_ref = take(3)
-    loc_ref, pack_ref = take(2) if later else (None, None)
+    loc_ref, *pack_refs = take(peers) if later else (None,)
     coef_out = take(1)[0] if first else None
     gather, halo_ref, inject_ref, r_ref = refs
     nz = rhs_in.shape[0]
-    rows = packs[0].shape[0]
     position = lax.axis_index(axis)
 
     gather[...] = jnp.zeros(gather.shape, jnp.float32)
     for k in range(peers):
-        gather[jnp.bitwise_xor(position, k)] = packs[k][...]
+        gather[jnp.bitwise_xor(position, k)] = packs[k][: gather.shape[1], :]
     if first:
         coef_out[...] = gather[:, :PACK_ROWS, :]
-    rhs_ref[...] = rhs_in[...]
-    if not first:
-        add_ref[...] = add_in[...]
     complete_edges(first, gather, gather if first else coef_ref, halo_ref, inject_ref)
     own = pl.ds(position, 1)
     low = low_lanes(HALF)
     row_index = lax.broadcasted_iota(jnp.int32, (HALF, LANES), 0)
     if first:
         for z in range(nz):
-            halo_ref[STEPS] = halo_of(gather[:, PACK_ROWS + z, :])
-            halo = halo_ref[STEPS, own, :]
+            row = gather[:, PACK_ROWS + z, :]
+            left, right = beside(row, swap_halves(row))
+            halo_ref[STEPS + z] = sum_x(jnp.where(low_lanes(8), left, right))
+            halo = halo_ref[STEPS + z, own, :]
             at_edge = jnp.logical_or(
                 jnp.logical_and(row_index == 0, low),
                 jnp.logical_and(row_index == HALF - 1, jnp.logical_not(low)),
             )
             rhs_ref[z] = rhs_ref[z] + jnp.where(at_edge, halo, 0.0)
 
-    state = None if first else state_in[...]
-    for t, step in enumerate(steps):
-        z = step if step < nz else 2 * nz - 1 - step
-        if state is not None:
-            around = sum_y(sum_x(state), halo_ref[t, own, :])
-            if step < nz:
-                rhs_ref[step - 1] = around - 27.0 * state
-        if t == 0:
-            left, right = inject_ref[0, own, :], inject_ref[1, own, :]
-            state = (
-                loc_in[...] + block_column(b_ref, 0) * left + block_column(b_ref, LANES - 1) * right
-            )
-        else:
-            state = apply_blocks(b_ref, rhs_ref[z] + around, r_ref)
-            if step >= nz:
-                state = state + add_ref[z]
-        add_ref[z] = 2.0 * state if step < nz else state
-        if step == nz - 1:
-            rhs_ref[z] = -27.0 * state
+    first_plane, move = planes_of(steps, nz)
+
+    def keep(z, state):
+        add_ref[z] = 2.0 * state if move > 0 else state
+
+    if not first:
+        state = state_in[...]
+        if move > 0:
+            around = sum_y(sum_x(state), halo_ref[0, own, :])
+            rhs_ref[first_plane - 1] = around - 27.0 * state
+    state = loc_in[0]
+    for n in range(2):
+        state = state + plane_ref[n] * inject_ref[n, own, :]
+    keep(first_plane, state)
+    if move > 0:
+        rhs_ref[first_plane] = sum_y(sum_x(state), halo_ref[1, own, :]) - 27.0 * state
+    state = loc_in[1]
+    for n in range(PLANES):
+        state = state + plane_ref[n] * inject_ref[n if n >= 2 else PLANES + n, own, :]
+    keep(first_plane + move, state)
+
+    def transition(t, state):
+        z = first_plane + move * t
+        around = sum_y(sum_x(state), halo_ref[t, own, :])
+        if move > 0:
+            rhs_ref[z - 1] = around - 27.0 * state
+        state = apply_blocks(b_ref, rhs_ref[z] + around, r_ref)
+        if move < 0:
+            state = state + add_ref[z]
+        keep(z, state)
+        return state
+
+    state = lax.fori_loop(2, STEPS, transition, state, unroll=True)
+    if steps[-1] == nz - 1:
+        rhs_ref[nz - 1] = -27.0 * state
     state_ref[...] = state
     if later:
+        pack_ref = pack_refs[0]
         pack_ref[...] = jnp.zeros(pack_ref.shape, jnp.float32)
         local_chain(later, b_ref, rhs_ref, add_ref, state, r_ref, pack_ref, loc_ref)
+        copy_pack(pack_refs)
     if last:
         own_lines = HALF - 2 * ghost
         for z in range(nz):
@@ -354,9 +456,11 @@
             out_ref[z] = turned[ghost : ghost + own_lines]
 
 
-def local_kernel(steps, b_ref, rhs_ref, add_ref, state_ref, loc_ref, pack_ref, r_ref):
-    pack_ref[...] = jnp.zeros(pack_ref.shape, jnp.float32)
-    local_chain(steps, b_ref, rhs_ref, add_ref, state_ref[...], r_ref, pack_ref, loc_ref)
+def local_kernel(steps, b_ref, rhs_ref, add_ref, state_ref, loc_ref, *refs):
+    *pack_refs, r_ref = refs
+    pack_refs[0][...] = jnp.zeros(pack_refs[0].shape, jnp.float32)
+    local_chain(steps, b_ref, rhs_ref, add_ref, state_ref[...], r_ref, pack_refs[0], loc_ref)
+    copy_pack(pack_refs)
 
 
 def finish_kernel(axis, v_ref, *refs):
@@ -372,14 +476,18 @@
     return jax.ShapeDtypeStruct(shape, jnp.float32)
 
 
-def call(kernel, ins, outs, scratch, name):
+SMALL = pltpu.CompilerParams(vmem_limit_bytes=16 * 1024 * 1024)
+
+
+def call(kernel, ins, outs, scratch, name, aliases=None):
     return pl.pallas_call(
         kernel,
         out_shape=outs,
         in_specs=[VMEM] * len(ins),
         out_specs=[VMEM] * len(outs),
         scratch_shapes=scratch,
-        compiler_params=PARAMS,
+        input_output_aliases=aliases or {},
+        compiler_params=SMALL,
         name=name,
     )(*ins)
 
@@ -411,19 +519,23 @@
     return lax.ppermute(tail, "gx", ups), lax.ppermute(head, "gx", downs)
 
 
-def block_ghosts(blocks, own, width):
+def block_tail(blocks, width):
+    groups, size = lax.axis_size("gz"), blocks.shape[0]
+    start = jnp.where(lax.axis_index("gz") < groups // 2, size - width, 0)
+    return lax.dynamic_slice_in_dim(blocks, start, width, 0)
+
+
+def block_ghosts(tail, own):
     groups, count = lax.axis_size("gz"), lax.axis_size("gx")
-    size = blocks.shape[0]
-    reach = -(-width // own)
+    reach = -(-tail.shape[0] // own)
     assert 2 * reach <= groups
     shift = reach if 4 * reach <= groups else 0
-    start = jnp.where(lax.axis_index("gz") < groups // 2, size - width, 0)
     pairs = []
     for g in range(reach):
         for a in range(count - 1):
             pairs.append(((g + shift) * count + a, g * count + a + 1))
             pairs.append(((groups - 1 - g - shift) * count + a + 1, (groups - 1 - g) * count + a))
-    return lax.ppermute(lax.dynamic_slice_in_dim(blocks, start, width, 0), ("gz", "gx"), pairs)
+    return lax.ppermute(tail, ("gz", "gx"), pairs)
 
 
 def window_ghosts(windows, ready, own, ghost):
@@ -464,10 +576,38 @@
     assert nz % STEPS == 0 and nz <= ghost and peers <= 4
     here = lax.axis_index("gz")
 
-    fields = jnp.stack([initial_field, source_term])
+    late = own == 2 * ghost
     rows = block_inverse.reshape(lines * LANES, LANES)
-    beyond = block_ghosts(block_inverse, own, ghost).reshape(ghost * LANES, LANES)
-    late = own == 2 * ghost
+    if late:
+        chunks = HALF // ghost
+        tail = pl.pallas_call(
+            functools.partial(tail_kernel, "gz", groups),
+            out_shape=f32(ghost, LANES, LANES),
+            in_specs=[HBM],
+            out_specs=HBM,
+            scratch_shapes=[pltpu.SemaphoreType.DMA((4,))],
+            compiler_params=PARAMS,
+            name="tail",
+        )(in_hbm(block_inverse))
+        windows = pl.pallas_call(
+            functools.partial(pack_kernel, "gz", own, ghost),
+            out_shape=[f32(2, nz_local, HALF, LANES)] * groups,
+            in_specs=[HBM] * 2,
+            out_specs=[VMEM] * groups,
+            scratch_shapes=[pltpu.SemaphoreType.DMA((2 * groups * chunks,))],
+            compiler_params=PARAMS,
+            name="pack",
+        )(in_hbm(initial_field), in_hbm(source_term))
+    else:
+        tail = block_tail(block_inverse, ghost)
+        fields = jnp.stack([initial_field, source_term])
+        before, after = line_ghosts(fields, 2, ghost)
+        wide = jnp.concatenate([before, fields, after], axis=2)
+        windows = [
+            lax.dynamic_slice_in_dim(wide, jnp.bitwise_xor(here, k) * own, HALF, 2)
+            for k in range(groups)
+        ]
+    beyond = block_ghosts(tail, own).reshape(ghost * LANES, LANES)
     turned = LANES * HALF * LANES * 4
     blocks, ready = pl.pallas_call(
         functools.partial(layout_kernel, own, ghost, "gz"),
@@ -482,15 +622,6 @@
         cost_estimate=pl.CostEstimate(flops=0, bytes_accessed=4 * turned, transcendentals=0),
         name="layout",
     )(*[in_hbm(a) for a in ([rows] if late else [rows, beyond])])
-    if late:
-        wide = jnp.pad(fields, ((0, 0), (0, 0), (ghost, ghost), (0, 0)))
-    else:
-        before, after = line_ghosts(fields, 2, ghost)
-        wide = jnp.concatenate([before, fields, after], axis=2)
-    windows = [
-        lax.dynamic_slice_in_dim(wide, jnp.bitwise_xor(here, k) * own, HALF, 2)
-        for k in range(groups)
-    ]
     fields_here = to_peers(windows, "gz")
     ghosts_here = []
     if late:
@@ -507,14 +638,19 @@
 
 
     plane = pltpu.VMEM((HALF, LANES), jnp.float32)
-    (answers,) = call(
-        responses_kernel, [blocks], [f32(PACK_ROWS, LANES)], [plane], "responses"
+    answers, effects = call(
+        responses_kernel,
+        [blocks],
+        [f32(PACK_ROWS, LANES), f32(PLANES, HALF, LANES)],
+        [plane, pltpu.VMEM((PLANES, HALF, LANES), jnp.float32)],
+        "responses",
     )
     first_rows = PACK_ROWS + 8 * (-(-nz // 8))
-    rhs, loc, pack = call(
+    rhs, loc, *packs = call(
         functools.partial(first_kernel, "gz", groups, late),
         [*fields_here, *ghosts_here, blocks, answers],
-        [f32(nz, HALF, LANES), f32(HALF, LANES), f32(first_rows, LANES)],
+        [f32(nz, HALF, LANES), f32(2, HALF, LANES)]
+        + [f32(first_rows + 8 * k, LANES) for k in range(peers - 1)],
         [pltpu.VMEM((nz + 2, HALF, LANES), jnp.float32), pltpu.VMEM((nz, HALF, LANES), jnp.float32)]
         + [plane],
         "first_chain",
@@ -526,40 +662,46 @@
         final = n + 1 == len(schedule)
         renew = steps[-1] == nz - 1 and 2 * nz > ghost
         later = None if final or renew else schedule[n + 1]
-        packs = to_peers([pack] * peers, "gy")
-        ins = [*packs, blocks, rhs, loc] + ([] if first else [coef, add, state])
+        packs = to_peers([packs[0], *packs], "gy")
+        ins = [*packs, blocks, effects, rhs, loc] + ([] if first else [coef, add, state])
         planes = f32(nz, HALF, LANES)
         outs = [f32(nz, own, LANES)] if final else []
         outs += [planes, planes, f32(HALF, LANES)]
-        outs += [f32(HALF, LANES), f32(8, LANES)] if later else []
+        if later:
+            outs += [f32(2, HALF, LANES)] + [f32(8 * k, LANES) for k in range(1, peers)]
         outs += [f32(8, PACK_ROWS, LANES)] if first else []
+        at_rhs = 1 if final else 0
+        aliases = {peers + 2: at_rhs}
+        if not first:
+            aliases[peers + 5] = at_rhs + 1
         results = call(
             functools.partial(next_kernel, steps, later, first, peers, "gy", ghost),
             ins,
             outs,
             [
-                pltpu.VMEM((8, pack.shape[0], LANES), jnp.float32),
-                pltpu.VMEM((STEPS + 1, 8, LANES), jnp.float32),
-                pltpu.VMEM((2, 8, LANES), jnp.float32),
+                pltpu.VMEM((8, first_rows if first else 8, LANES), jnp.float32),
+                pltpu.VMEM((STEPS + nz, 8, LANES), jnp.float32),
+                pltpu.VMEM((PLANES + 2, 8, LANES), jnp.float32),
                 plane,
             ],
             "next_chain",
+            aliases,
         )
         if final:
             change = results[0]
             break
         rhs, add, state = results[:3]
         if later:
-            loc, pack = results[3:5]
+            loc, *packs = results[3 : 3 + peers]
         if first:
             coef = results[-1]
         if renew:
             renewed = refresh_ghosts(jnp.concatenate([rhs, add, state[None]]), ghost)
             rhs, add, state = renewed[:nz], renewed[nz : 2 * nz], renewed[2 * nz]
-            loc, pack = call(
+            loc, *packs = call(
                 functools.partial(local_kernel, schedule[n + 1]),
                 [blocks, rhs, add, state],
-                [f32(HALF, LANES), f32(8, LANES)],
+                [f32(2, HALF, LANES)] + [f32(8 * k, LANES) for k in range(1, peers)],
                 [plane],
                 "local_chain",
             )

time: 69.8 us -> 68 us (0.974)
  waiting for transfers between devices: 11 us -> 12.5 us
  local copies, waits for them, and re-layouts: 3.55 us -> 2.21 us
  starting transfers between devices: 32.8 us -> 31.6 us
  other arithmetic: 1 us -> 0 us
    pallas_call x0 -> x2, Pallas kernels: none -> 2.52 us  [the longest x1 1.3 us: body(): pl.pallas_call(functools.partial(pack_kernel, 'gz', own, ghost), out_shap...]
    pallas_call x8, Pallas kernels: 16 us -> 13.7 us  [call(): pl.pallas_call(kernel, out_shape=outs, in_specs=[VMEM] * len(ins), out_sp...]
    ppermute x18, waiting for transfers between devices: 11 us -> 12.5 us  [to_peers(): got[k] = lax.ppermute(pieces[k], axis, [(i, i ^ k) for i in range(count)])]
    dynamic_slice x2 -> x0, local copies, waits for them, and re-layouts: 1.34 us -> none  [the longest x1 1.29 us: block_ghosts(): lax.dynamic_slice_in_dim(blocks, start, width, 0)]
    ppermute x18, starting transfers between devices: 31.4 us -> 30.2 us  [to_peers(): got[k] = lax.ppermute(pieces[k], axis, [(i, i ^ k) for i in range(count)])]
    another operation x1 -> x0, other arithmetic: 1 us -> none  [body(): fields = jnp.stack([initial_field, source_term])]
  transfers between devices with their start and end apart: 20 -> 20, of which waited for: 10 -> 7; matrix products, arithmetic and copies ran while one was open for 2% -> 0% of each run, Pallas kernels for 10% -> 13%
where the time goes in v3:
time: 68 us; the launch traced here: 67.7 us
  starting transfers between devices  31.6 us (46%)
  Pallas kernels  21.3 us (31%)
  waiting for transfers between devices  12.5 us (18%)
  local copies, waits for them, and re-layouts  2.21 us (3%)
    ppermute x18, starting transfers between devices, to_peers(): got[k] = lax.ppermute(pieces[k], axis, [(i, i ^ k) for i in range(count)])  30.2 us
    pallas_call x8, Pallas kernels, call(): pl.pallas_call(kernel, out_shape=outs, in_specs=[VMEM] * len(ins), out_sp...  13.7 us
    ppermute x18, waiting for transfers between devices, to_peers(): got[k] = lax.ppermute(pieces[k], axis, [(i, i ^ k) for i in range(count)])  12.5 us
    pallas_call x1, Pallas kernels, body(): pl.pallas_call(functools.partial(layout_kernel, own, ghost, 'gz'), out_sh...  5.04 us
    unnamed x6, local copies, waits for them, and re-layouts  2.2 us
  transfers between devices with their start and end apart: 20, of which 7 were waited for; matrix products, arithmetic and copies ran while one was open for 0% of the time, Pallas kernels for 13%

profile of v3, /device:TPU:11, one launch (start us, length us, event | category | flops | bytes accessed | tf_op | source)
XLA Modules:
  0.0 67.7 jit_solution(8992695709926045250)
XLA Ops:
  0.0 1.2 %tail.1 = f32[16,128,128]{2,1,0:T(8,128)S(1)} custom-call(f32[128,128,128]{2,1,0:T(8,128)} %b_ref.1), custom_call_target="tpu_custom_call" | custom-call | tf_op jit(solution)/shard_map/tail/pallas_call | solution.py:583
  1.2 0.7 %collective-permute-start.4 = (f32[16,128,128]{2,1,0:T(8,128)S(1)}, f32[16,128,128]{2,1,0:T(8,128)S(1)}, u32[]{:S(2)}, u32[]{:S(2)}) collective-permute-start(f32[16,128,128]{2,1,0:T(8,128)S(1)} %tail.1), channel_id=1, source_target_pairs={{8,4},{20,24},{9,5},{21,25},{10,6},{22,26},{11,7},{23,27}} | collective-permute-start | bytes 3145736 | tf_op jit(solution)/shard_map/ppermute | solution.py:538
  2.0 1.3 %pack.1 = (f32[2,2,64,128]{3,2,1,0:T(8,128)S(1)}, f32[2,2,64,128]{3,2,1,0:T(8,128)S(1)}, f32[2,2,64,128]{3,2,1,0:T(8,128)S(1)}, f32[2,2,64,128]{3,2,1,0:T(8,128)S(1)}) custom-call(f32[2,128,128]{2,1,0:T(8,128)} %v_ref.3, f32[2,128,128]{2,1,0:T(8,128)} %s_ref.1), custom_call_target="tpu_custom_call" | custom-call | tf_op jit(solution)/shard_map/pack/pallas_call | solution.py:592
  3.3 1.3 %collective-permute-start = (f32[2,2,64,128]{3,2,1,0:T(8,128)S(1)}, f32[2,2,64,128]{3,2,1,0:T(8,128)S(1)}, u32[]{:S(2)}, u32[]{:S(2)}) collective-permute-start(f32[2,2,64,128]{3,2,1,0:T(8,128)S(1)} %get-tuple-element.42), channel_id=1, source_target_pairs={{0,8},{8,0},{16,24},{24,16},{1,9},{9,1},{17,25},{25,17},{2,10},{10... | collective-permute-start | bytes 393224 | tf_op jit(solution)/shard_map/ppermute | solution.py:503
  4.6 1.9 %collective-permute-start.1 = (f32[2,2,64,128]{3,2,1,0:T(8,128)S(1)}, f32[2,2,64,128]{3,2,1,0:T(8,128)S(1)}, u32[]{:S(2)}, u32[]{:S(2)}) collective-permute-start(f32[2,2,64,128]{3,2,1,0:T(8,128)S(1)} %get-tuple-element.43), channel_id=1, source_target_pairs={{0,16},{8,24},{16,0},{24,8},{1,17},{9,25},{17,1},{25,9},{2,18},{10... | collective-permute-start | bytes 393224 | tf_op jit(solution)/shard_map/ppermute | solution.py:503
  6.5 5.0 %layout.1 = (f32[8192,128]{1,0:T(8,128)S(1)}, f32[8,128]{1,0:T(8,128)S(1)}) custom-call(f32[16384,128]{1,0:T(8,128)} %bitcast.3), custom_call_target="tpu_custom_call" | custom-call | bytes 16777216 | tf_op jit(solution)/shard_map/layout/pallas_call | solution.py:612
  11.6 1.7 %collective-permute-done.2.refs_3_ = f32[2,2,64,128]{3,2,1,0:T(8,128)S(1)} collective-permute-done((f32[2,2,64,128]{3,2,1,0:T(8,128)S(1)}, f32[2,2,64,128]{3,2,1,0:T(8,128)S(1)}, u32[]{:S(2)}, u32[]{:S(2)}) %collective-permute-start.2) | collective-permute-done | bytes 131104 | tf_op jit(solution)/shard_map/ppermute | solution.py:503
  13.3 0.7 collective-permute-start.3
  14.1 2.3 %responses.1 = (f32[24,128]{1,0:T(8,128)S(1)}, f32[8,64,128]{2,1,0:T(8,128)S(1)}) custom-call(f32[8192,128]{1,0:T(8,128)S(1)} %patch.1.b_ref.refs_5_.refs_4_), custom_call_target="tpu_custom_call" | custom-call | tf_op jit(solution)/shard_map/responses/pallas_call | solution.py:483
  16.4 1.5 %first_chain.1 = (f32[8,64,128]{2,1,0:T(8,128)S(1)}, f32[2,64,128]{2,1,0:T(8,128)S(1)}, f32[32,128]{1,0:T(8,128)S(1)}, f32[40,128]{1,0:T(8,128)S(1)}, f32[48,128]{1,0:T(8,128)S(1)}) custom-call(f32[2,2,64,128]{3,2,1,0:T(8,128)S(1)} %get-tuple-element.41.refs_0_, f32[2,2,64,128]{3,2,1,0:T(8,128)S(1)} %collective-permute-done.refs_1_, ...), custom_call_target="tpu_custom_call" | custom-call | tf_op jit(solution)/shard_map/first_chain/pallas_call | solution.py:483
  17.9 1.4 %collective-permute-start.7 = (f32[48,128]{1,0:T(8,128)S(1)}, f32[48,128]{1,0:T(8,128)S(1)}, u32[]{:S(2)}, u32[]{:S(2)}) collective-permute-start(f32[48,128]{1,0:T(8,128)S(1)} %get-tuple-element.50), channel_id=1, source_target_pairs={{0,3},{1,2},{2,1},{3,0},{4,7},{5,6},{6,5},{7,4},{8,11},{9,10},{10,... | collective-permute-start | bytes 73736 | tf_op jit(solution)/shard_map/ppermute | solution.py:503
  19.3 1.1 %collective-permute-start.6 = (f32[40,128]{1,0:T(8,128)S(1)}, f32[40,128]{1,0:T(8,128)S(1)}, u32[]{:S(2)}, u32[]{:S(2)}) collective-permute-start(f32[40,128]{1,0:T(8,128)S(1)} %get-tuple-element.49), channel_id=1, source_target_pairs={{0,2},{1,3},{2,0},{3,1},{4,6},{5,7},{6,4},{7,5},{8,10},{9,11},{10,... | collective-permute-start | bytes 61448 | tf_op jit(solution)/shard_map/ppermute | solution.py:503
  20.3 1.1 %collective-permute-start.5 = (f32[32,128]{1,0:T(8,128)S(1)}, f32[32,128]{1,0:T(8,128)S(1)}, u32[]{:S(2)}, u32[]{:S(2)}) collective-permute-start(f32[32,128]{1,0:T(8,128)S(1)} %get-tuple-element.48.refs_0_), channel_id=1, source_target_pairs={{0,1},{1,0},{2,3},{3,2},{4,5},{5,4},{6,7},{7,6},{8,9},{9,8},{10,11... | collective-permute-start | bytes 49160 | tf_op jit(solution)/shard_map/ppermute | solution.py:503
  21.5 1.6 %collective-permute-done.5.refs_1_ = f32[32,128]{1,0:T(8,128)S(1)} collective-permute-done((f32[32,128]{1,0:T(8,128)S(1)}, f32[32,128]{1,0:T(8,128)S(1)}, u32[]{:S(2)}, u32[]{:S(2)}) %collective-permute-start.5) | collective-permute-done | bytes 16416 | tf_op jit(solution)/shard_map/ppermute | solution.py:503
  23.1 2.3 %next_chain.4 = (f32[8,64,128]{2,1,0:T(8,128)S(1)}, f32[8,64,128]{2,1,0:T(8,128)S(1)}, f32[64,128]{1,0:T(8,128)S(1)}, f32[2,64,128]{2,1,0:T(8,128)S(1)}, f32[8,1...) custom-call(f32[32,128]{1,0:T(8,128)S(1)} %get-tuple-element.48.refs, ...), custom_call_target="tpu_custom_call", output_to_operand_aliasing={{0}: (6, {})} | custom-call | tf_op jit(solution)/shard_map/next_chain/pallas_call | solution.py:483
  25.4 2.2 %collective-permute-start.10 = (f32[24,128]{1,0:T(8,128)S(1)}, f32[24,128]{1,0:T(8,128)S(1)}, u32[]{:S(2)}, u32[]{:S(2)}) collective-permute-start(f32[24,128]{1,0:T(8,128)S(1)} %get-tuple-element.56), channel_id=1, source_target_pairs={{0,3},{1,2},{2,1},{3,0},{4,7},{5,6},{6,5},{7,4},{8,11},{9,10},{10,... | collective-permute-start | bytes 36872 | tf_op jit(solution)/shard_map/ppermute | solution.py:503
  27.6 1.8 %collective-permute-start.9 = (f32[16,128]{1,0:T(8,128)S(1)}, f32[16,128]{1,0:T(8,128)S(1)}, u32[]{:S(2)}, u32[]{:S(2)}) collective-permute-start(f32[16,128]{1,0:T(8,128)S(1)} %get-tuple-element.55), channel_id=1, source_target_pairs={{0,2},{1,3},{2,0},{3,1},{4,6},{5,7},{6,4},{7,5},{8,10},{9,11},{10,... | collective-permute-start | bytes 24584 | tf_op jit(solution)/shard_map/ppermute | solution.py:503
  29.4 2.5 %collective-permute-done.8.refs_1_ = f32[8,128]{1,0:T(8,128)S(1)} collective-permute-done((f32[8,128]{1,0:T(8,128)S(1)}, f32[8,128]{1,0:T(8,128)S(1)}, u32[]{:S(2)}, u32[]{:S(2)}) %collective-permute-start.8) | collective-permute-done | bytes 4128 | tf_op jit(solution)/shard_map/ppermute | solution.py:503
  31.9 2.7 %next_chain.5 = (f32[8,64,128]{2,1,0:T(8,128)S(1)}, f32[8,64,128]{2,1,0:T(8,128)S(1)}, f32[64,128]{1,0:T(8,128)S(1)}, f32[2,64,128]{2,1,0:T(8,128)S(1)}, f32[8,1...) custom-call(f32[8,128]{1,0:T(8,128)S(1)} %get-tuple-element.54.refs_, ...), custom_call_target="tpu_custom_call", output_to_operand_aliasing={{0}: (6, {}), {1}: (9, {})} | custom-call | tf_op jit(solution)/shard_map/next_chain/pallas_call | solution.py:483
  35.0 1.8 %collective-permute-start.12 = (f32[16,128]{1,0:T(8,128)S(1)}, f32[16,128]{1,0:T(8,128)S(1)}, u32[]{:S(2)}, u32[]{:S(2)}) collective-permute-start(f32[16,128]{1,0:T(8,128)S(1)} %get-tuple-element.63), channel_id=1, source_target_pairs={{0,2},{1,3},{2,0},{3,1},{4,6},{5,7},{6,4},{7,5},{8,10},{9,11},{10,... | collective-permute-start | bytes 24584 | tf_op jit(solution)/shard_map/ppermute | solution.py:503
  37.3 2.1 %collective-permute-done.11.refs_1_ = f32[8,128]{1,0:T(8,128)S(1)} collective-permute-done((f32[8,128]{1,0:T(8,128)S(1)}, f32[8,128]{1,0:T(8,128)S(1)}, u32[]{:S(2)}, u32[]{:S(2)}) %collective-permute-start.11) | collective-permute-done | bytes 4128 | tf_op jit(solution)/shard_map/ppermute | solution.py:503
  39.5 2.3 %next_chain.6 = (f32[8,64,128]{2,1,0:T(8,128)S(1)}, f32[8,64,128]{2,1,0:T(8,128)S(1)}, f32[64,128]{1,0:T(8,128)S(1)}, f32[2,64,128]{2,1,0:T(8,128)S(1)}, f32[8,1...) custom-call(f32[8,128]{1,0:T(8,128)S(1)} %get-tuple-element.62.refs_, ...), custom_call_target="tpu_custom_call", output_to_operand_aliasing={{0}: (6, {}), {1}: (9, {})} | custom-call | tf_op jit(solution)/shard_map/next_chain/pallas_call | solution.py:483
  41.8 1.2 %collective-permute-start.16 = (f32[24,128]{1,0:T(8,128)S(1)}, f32[24,128]{1,0:T(8,128)S(1)}, u32[]{:S(2)}, u32[]{:S(2)}) collective-permute-start(f32[24,128]{1,0:T(8,128)S(1)} %get-tuple-element.71), channel_id=1, source_target_pairs={{0,3},{1,2},{2,1},{3,0},{4,7},{5,6},{6,5},{7,4},{8,11},{9,10},{10,... | collective-permute-start | bytes 36872 | tf_op jit(solution)/shard_map/ppermute | solution.py:503
  43.0 1.7 %collective-permute-start.15 = (f32[16,128]{1,0:T(8,128)S(1)}, f32[16,128]{1,0:T(8,128)S(1)}, u32[]{:S(2)}, u32[]{:S(2)}) collective-permute-start(f32[16,128]{1,0:T(8,128)S(1)} %get-tuple-element.70), channel_id=1, source_target_pairs={{0,2},{1,3},{2,0},{3,1},{4,6},{5,7},{6,4},{7,5},{8,10},{9,11},{10,... | collective-permute-start | bytes 24584 | tf_op jit(solution)/shard_map/ppermute | solution.py:503
  44.7 2.5 %collective-permute-done.14.refs_1_ = f32[8,128]{1,0:T(8,128)S(1)} collective-permute-done((f32[8,128]{1,0:T(8,128)S(1)}, f32[8,128]{1,0:T(8,128)S(1)}, u32[]{:S(2)}, u32[]{:S(2)}) %collective-permute-start.14) | collective-permute-done | bytes 4128 | tf_op jit(solution)/shard_map/ppermute | solution.py:503
  47.1 2.2 %copy-done.1 = f32[8192,128]{1,0:T(8,128)S(1)} copy-done((f32[8192,128]{1,0:T(8,128)S(1)}, f32[8192,128]{1,0:T(8,128)}, u32[]{:S(2)}) %copy-start.1) | copy-done | bytes 4194328
  49.3 1.9 %next_chain.7 = (f32[8,32,128]{2,1,0:T(8,128)S(1)}, f32[8,64,128]{2,1,0:T(8,128)S(1)}, f32[8,64,128]{2,1,0:T(8,128)S(1)}, f32[64,128]{1,0:T(8,128)}) custom-call(f32[8,128]{1,0:T(8,128)S(1)} %get-tuple-element.69.refs_0_, f32[8,128]{1,0:T(8,128)S(1)} %collective-permute-done.14.refs_1_, ...), custom_call_target="tpu_custom_call", output_to_operand_aliasing={{1}: (6, {}), {2}: (9, {})} | custom-call | tf_op jit(solution)/shard_map/next_chain/pallas_call | solution.py:483
  51.3 12.0 %collective-permute-start.17 = (f32[2,32,128]{2,1,0:T(8,128)S(1)}, f32[2,32,128]{2,1,0:T(8,128)S(1)}, u32[]{:S(2)}, u32[]{:S(2)}) collective-permute-start(f32[2,32,128]{2,1,0:T(8,128)S(1)} %get-tuple-element.79), channel_id=1, source_target_pairs={{0,8},{8,0},{16,24},{24,16},{1,9},{9,1},{17,25},{25,17},{2,10},{10... | collective-permute-start | bytes 98312 | tf_op jit(solution)/shard_map/ppermute | solution.py:503
  63.2 1.7 %collective-permute-start.19 = (f32[2,32,128]{2,1,0:T(8,128)S(1)}, f32[2,32,128]{2,1,0:T(8,128)S(1)}, u32[]{:S(2)}, u32[]{:S(2)}) collective-permute-start(f32[2,32,128]{2,1,0:T(8,128)S(1)} %get-tuple-element.77), channel_id=1, source_target_pairs={{0,24},{8,16},{16,8},{24,0},{1,25},{9,17},{17,9},{25,1},{2,26},{10... | collective-permute-start | bytes 98312 | tf_op jit(solution)/shard_map/ppermute | solution.py:503
  64.9 1.1 %collective-permute-done.18.refs_2_ = f32[2,32,128]{2,1,0:T(8,128)S(1)} collective-permute-done((f32[2,32,128]{2,1,0:T(8,128)S(1)}, f32[2,32,128]{2,1,0:T(8,128)S(1)}, u32[]{:S(2)}, u32[]{:S(2)}) %collective-permute-start.18) | collective-permute-done | bytes 32800 | tf_op jit(solution)/shard_map/ppermute | solution.py:503
  66.0 1.1 %collective-permute-done.19.refs_3_ = f32[2,32,128]{2,1,0:T(8,128)S(1)} collective-permute-done((f32[2,32,128]{2,1,0:T(8,128)S(1)}, f32[2,32,128]{2,1,0:T(8,128)S(1)}, u32[]{:S(2)}, u32[]{:S(2)}) %collective-permute-start.19) | collective-permute-done | bytes 32800 | tf_op jit(solution)/shard_map/ppermute | solution.py:503
  67.1 0.7 finish.1
  (27 shorter events, 1.0 us)
Async XLA Ops:
  1.2 12.8 %collective-permute-start.4 = (f32[16,128,128]{2,1,0:T(8,128)S(1)}, f32[16,128,128]{2,1,0:T(8,128)S(1)}, u32[]{:S(2)}, u32[]{:S(2)}) collective-permute-start(f32[16,128,128]{2,1,0:T(8,128)S(1)} %tail.1), channel_id=1, source_target_pairs={{8,4},{20,24},{9,5},{21,25},{10,6},{22,26},{11,7},{23,27}} | collective-permute-start | bytes 3145736 | tf_op jit(solution)/shard_map/ppermute | solution.py:538
  3.3 8.3 %collective-permute-start = (f32[2,2,64,128]{3,2,1,0:T(8,128)S(1)}, f32[2,2,64,128]{3,2,1,0:T(8,128)S(1)}, u32[]{:S(2)}, u32[]{:S(2)}) collective-permute-start(f32[2,2,64,128]{3,2,1,0:T(8,128)S(1)} %get-tuple-element.42), channel_id=1, source_target_pairs={{0,8},{8,0},{16,24},{24,16},{1,9},{9,1},{17,25},{25,17},{2,10},{10... | collective-permute-start | bytes 393224 | tf_op jit(solution)/shard_map/ppermute | solution.py:503
  4.6 7.0 %collective-permute-start.1 = (f32[2,2,64,128]{3,2,1,0:T(8,128)S(1)}, f32[2,2,64,128]{3,2,1,0:T(8,128)S(1)}, u32[]{:S(2)}, u32[]{:S(2)}) collective-permute-start(f32[2,2,64,128]{3,2,1,0:T(8,128)S(1)} %get-tuple-element.43), channel_id=1, source_target_pairs={{0,16},{8,24},{16,0},{24,8},{1,17},{9,25},{17,1},{25,9},{2,18},{10... | collective-permute-start | bytes 393224 | tf_op jit(solution)/shard_map/ppermute | solution.py:503
  6.5 6.8 %collective-permute-start.2 = (f32[2,2,64,128]{3,2,1,0:T(8,128)S(1)}, f32[2,2,64,128]{3,2,1,0:T(8,128)S(1)}, u32[]{:S(2)}, u32[]{:S(2)}) collective-permute-start(f32[2,2,64,128]{3,2,1,0:T(8,128)S(1)} %get-tuple-element.44), channel_id=1, source_target_pairs={{0,24},{8,16},{16,8},{24,0},{1,25},{9,17},{17,9},{25,1},{2,26},{10... | collective-permute-start | bytes 393224 | tf_op jit(solution)/shard_map/ppermute | solution.py:503
  13.3 3.0 %collective-permute-start.3 = (f32[4,2,2,16,128]{4,3,2,1,0:T(8,128)S(1)}, f32[4,2,2,16,128]{4,3,2,1,0:T(8,128)S(1)}, u32[]{:S(2)}, u32[]{:S(2)}) collective-permute-start(f32[4,2,2,16,128]{4,3,2,1,0:T(8,128)S(1)} %ghost_pack.1), channel_id=1, source_target_pairs={{24,4},{4,24},{25,5},{5,25},{26,6},{6,26},{27,7},{7,27}} | collective-permute-start | bytes 393224 | tf_op jit(solution)/shard_map/ppermute | solution.py:554
  14.1 25.4 %copy-start = (f32[8192,128]{1,0:T(8,128)}, f32[8192,128]{1,0:T(8,128)S(1)}, u32[]{:S(2)}) copy-start(f32[8192,128]{1,0:T(8,128)S(1)} %patch.1.b_ref.refs_5_.refs_4_) | copy-start | bytes 12582916
  17.9 5.2 %collective-permute-start.7 = (f32[48,128]{1,0:T(8,128)S(1)}, f32[48,128]{1,0:T(8,128)S(1)}, u32[]{:S(2)}, u32[]{:S(2)}) collective-permute-start(f32[48,128]{1,0:T(8,128)S(1)} %get-tuple-element.50), channel_id=1, source_target_pairs={{0,3},{1,2},{2,1},{3,0},{4,7},{5,6},{6,5},{7,4},{8,11},{9,10},{10,... | collective-permute-start | bytes 73736 | tf_op jit(solution)/shard_map/ppermute | solution.py:503
  19.3 3.8 %collective-permute-start.6 = (f32[40,128]{1,0:T(8,128)S(1)}, f32[40,128]{1,0:T(8,128)S(1)}, u32[]{:S(2)}, u32[]{:S(2)}) collective-permute-start(f32[40,128]{1,0:T(8,128)S(1)} %get-tuple-element.49), channel_id=1, source_target_pairs={{0,2},{1,3},{2,0},{3,1},{4,6},{5,7},{6,4},{7,5},{8,10},{9,11},{10,... | collective-permute-start | bytes 61448 | tf_op jit(solution)/shard_map/ppermute | solution.py:503
  20.3 2.7 %collective-permute-start.5 = (f32[32,128]{1,0:T(8,128)S(1)}, f32[32,128]{1,0:T(8,128)S(1)}, u32[]{:S(2)}, u32[]{:S(2)}) collective-permute-start(f32[32,128]{1,0:T(8,128)S(1)} %get-tuple-element.48.refs_0_), channel_id=1, source_target_pairs={{0,1},{1,0},{2,3},{3,2},{4,5},{5,4},{6,7},{7,6},{8,9},{9,8},{10,11... | collective-permute-start | bytes 49160 | tf_op jit(solution)/shard_map/ppermute | solution.py:503
  25.4 6.5 %collective-permute-start.10 = (f32[24,128]{1,0:T(8,128)S(1)}, f32[24,128]{1,0:T(8,128)S(1)}, u32[]{:S(2)}, u32[]{:S(2)}) collective-permute-start(f32[24,128]{1,0:T(8,128)S(1)} %get-tuple-element.56), channel_id=1, source_target_pairs={{0,3},{1,2},{2,1},{3,0},{4,7},{5,6},{6,5},{7,4},{8,11},{9,10},{10,... | collective-permute-start | bytes 36872 | tf_op jit(solution)/shard_map/ppermute | solution.py:503
  27.6 4.3 %collective-permute-start.9 = (f32[16,128]{1,0:T(8,128)S(1)}, f32[16,128]{1,0:T(8,128)S(1)}, u32[]{:S(2)}, u32[]{:S(2)}) collective-permute-start(f32[16,128]{1,0:T(8,128)S(1)} %get-tuple-element.55), channel_id=1, source_target_pairs={{0,2},{1,3},{2,0},{3,1},{4,6},{5,7},{6,4},{7,5},{8,10},{9,11},{10,... | collective-permute-start | bytes 24584 | tf_op jit(solution)/shard_map/ppermute | solution.py:503
  29.4 2.5 %collective-permute-start.8 = (f32[8,128]{1,0:T(8,128)S(1)}, f32[8,128]{1,0:T(8,128)S(1)}, u32[]{:S(2)}, u32[]{:S(2)}) collective-permute-start(f32[8,128]{1,0:T(8,128)S(1)} %get-tuple-element.54.refs_0_), channel_id=1, source_target_pairs={{0,1},{1,0},{2,3},{3,2},{4,5},{5,4},{6,7},{7,6},{8,9},{9,8},{10,11... | collective-permute-start | bytes 12296 | tf_op jit(solution)/shard_map/ppermute | solution.py:503
  34.6 4.8 %collective-permute-start.13 = (f32[24,128]{1,0:T(8,128)S(1)}, f32[24,128]{1,0:T(8,128)S(1)}, u32[]{:S(2)}, u32[]{:S(2)}) collective-permute-start(f32[24,128]{1,0:T(8,128)S(1)} %get-tuple-element.64), channel_id=1, source_target_pairs={{0,3},{1,2},{2,1},{3,0},{4,7},{5,6},{6,5},{7,4},{8,11},{9,10},{10,... | collective-permute-start | bytes 36872 | tf_op jit(solution)/shard_map/ppermute | solution.py:503
  35.0 4.4 %collective-permute-start.12 = (f32[16,128]{1,0:T(8,128)S(1)}, f32[16,128]{1,0:T(8,128)S(1)}, u32[]{:S(2)}, u32[]{:S(2)}) collective-permute-start(f32[16,128]{1,0:T(8,128)S(1)} %get-tuple-element.63), channel_id=1, source_target_pairs={{0,2},{1,3},{2,0},{3,1},{4,6},{5,7},{6,4},{7,5},{8,10},{9,11},{10,... | collective-permute-start | bytes 24584 | tf_op jit(solution)/shard_map/ppermute | solution.py:503
  36.8 2.6 %collective-permute-start.11 = (f32[8,128]{1,0:T(8,128)S(1)}, f32[8,128]{1,0:T(8,128)S(1)}, u32[]{:S(2)}, u32[]{:S(2)}) collective-permute-start(f32[8,128]{1,0:T(8,128)S(1)} %get-tuple-element.62.refs_0_), channel_id=1, source_target_pairs={{0,1},{1,0},{2,3},{3,2},{4,5},{5,4},{6,7},{7,6},{8,9},{9,8},{10,11... | collective-permute-start | bytes 12296 | tf_op jit(solution)/shard_map/ppermute | solution.py:503
  39.5 27.6 %copy-start.2 = (f32[2,128,128]{2,1,0:T(8,128)S(1)}, f32[2,128,128]{2,1,0:T(8,128)}, u32[]{:S(2)}) copy-start(f32[2,128,128]{2,1,0:T(8,128)} %v_ref.3) | copy-start | bytes 393220
  41.8 5.4 %collective-permute-start.16 = (f32[24,128]{1,0:T(8,128)S(1)}, f32[24,128]{1,0:T(8,128)S(1)}, u32[]{:S(2)}, u32[]{:S(2)}) collective-permute-start(f32[24,128]{1,0:T(8,128)S(1)} %get-tuple-element.71), channel_id=1, source_target_pairs={{0,3},{1,2},{2,1},{3,0},{4,7},{5,6},{6,5},{7,4},{8,11},{9,10},{10,... | collective-permute-start | bytes 36872 | tf_op jit(solution)/shard_map/ppermute | solution.py:503
  43.0 4.2 %collective-permute-start.15 = (f32[16,128]{1,0:T(8,128)S(1)}, f32[16,128]{1,0:T(8,128)S(1)}, u32[]{:S(2)}, u32[]{:S(2)}) collective-permute-start(f32[16,128]{1,0:T(8,128)S(1)} %get-tuple-element.70), channel_id=1, source_target_pairs={{0,2},{1,3},{2,0},{3,1},{4,6},{5,7},{6,4},{7,5},{8,10},{9,11},{10,... | collective-permute-start | bytes 24584 | tf_op jit(solution)/shard_map/ppermute | solution.py:503
  44.7 2.5 %collective-permute-start.14 = (f32[8,128]{1,0:T(8,128)S(1)}, f32[8,128]{1,0:T(8,128)S(1)}, u32[]{:S(2)}, u32[]{:S(2)}) collective-permute-start(f32[8,128]{1,0:T(8,128)S(1)} %get-tuple-element.69.refs_0_), channel_id=1, source_target_pairs={{0,1},{1,0},{2,3},{3,2},{4,5},{5,4},{6,7},{7,6},{8,9},{9,8},{10,11... | collective-permute-start | bytes 12296 | tf_op jit(solution)/shard_map/ppermute | solution.py:503
  47.1 2.2 %copy-start.1 = (f32[8192,128]{1,0:T(8,128)S(1)}, f32[8192,128]{1,0:T(8,128)}, u32[]{:S(2)}) copy-start(f32[8192,128]{1,0:T(8,128)} %copy-done) | copy-start | bytes 12582916
  51.3 13.7 %collective-permute-start.17 = (f32[2,32,128]{2,1,0:T(8,128)S(1)}, f32[2,32,128]{2,1,0:T(8,128)S(1)}, u32[]{:S(2)}, u32[]{:S(2)}) collective-permute-start(f32[2,32,128]{2,1,0:T(8,128)S(1)} %get-tuple-element.79), channel_id=1, source_target_pairs={{0,8},{8,0},{16,24},{24,16},{1,9},{9,1},{17,25},{25,17},{2,10},{10... | collective-permute-start | bytes 98312 | tf_op jit(solution)/shard_map/ppermute | solution.py:503
  63.2 2.8 %collective-permute-start.18 = (f32[2,32,128]{2,1,0:T(8,128)S(1)}, f32[2,32,128]{2,1,0:T(8,128)S(1)}, u32[]{:S(2)}, u32[]{:S(2)}) collective-permute-start(f32[2,32,128]{2,1,0:T(8,128)S(1)} %get-tuple-element.78), channel_id=1, source_target_pairs={{0,16},{8,24},{16,0},{24,8},{1,17},{9,25},{17,1},{25,9},{2,18},{10... | collective-permute-start | bytes 98312 | tf_op jit(solution)/shard_map/ppermute | solution.py:503
  63.2 3.8 %collective-permute-start.19 = (f32[2,32,128]{2,1,0:T(8,128)S(1)}, f32[2,32,128]{2,1,0:T(8,128)S(1)}, u32[]{:S(2)}, u32[]{:S(2)}) collective-permute-start(f32[2,32,128]{2,1,0:T(8,128)S(1)} %get-tuple-element.77), channel_id=1, source_target_pairs={{0,24},{8,16},{16,8},{24,0},{1,25},{9,17},{17,9},{25,1},{2,26},{10... | collective-permute-start | bytes 98312 | tf_op jit(solution)/shard_map/ppermute | solution.py:503

commit v4 on v3

--- a/solution.py
+++ b/solution.py
@@ -16,6 +16,12 @@
 VMEM = pl.BlockSpec(memory_space=pltpu.VMEM)
 HBM = pl.BlockSpec(memory_space=pltpu.HBM)
 PARAMS = pltpu.CompilerParams(vmem_limit_bytes=16 * 1024 * 1024)
+
+
+def window_of(device):
+    if isinstance(device, int):
+        return device ^ 1 if device < 2 else device
+    return jnp.where(device < 2, jnp.bitwise_xor(device, 1), device)
 
 
 def low_lanes(rows):
@@ -72,10 +78,12 @@
     return parts[0]
 
 
-def apply_blocks(b_ref, rhs, out_ref):
+def apply_blocks(b_ref, rhs, out_ref, arrival=None):
     tiles = [half[8 * t : 8 * t + 8] for half in spread(rhs) for t in range(HALF // 8)]
 
     def rows(outer, carry):
+        if arrival is not None:
+            arrival(outer)
         parts = []
         for u in range(8):
             at = (outer * 8 + u) * LANES
@@ -106,7 +114,7 @@
     ready_ref[...] = jnp.zeros(ready_ref.shape, jnp.float32)
     ghost_ref = ghost_refs[0] if ghost_refs else b_ref
     count = b_ref.shape[0] // LANES
-    position = lax.axis_index(axis)
+    position = window_of(lax.axis_index(axis))
     chunk = math.gcd(own, ghost)
     size = chunk * LANES
     copies = []
@@ -163,7 +171,7 @@
     last = v_ref.shape[1] - ghost
     copies = []
     for k, window_ref in enumerate(window_refs):
-        peer = jnp.bitwise_xor(position, k)
+        peer = window_of(jnp.bitwise_xor(position, k))
         for c in range(HALF // ghost):
             at = pl.multiple_of(jnp.clip(peer * own - ghost + c * ghost, 0, last), ghost)
             for kind, ref in enumerate((v_ref, s_ref)):
@@ -184,7 +192,7 @@
     ghost = beyond.shape[0] // LANES
     per_turn = HALF // ghost
     unroll = 4
-    position = lax.axis_index(axis)
+    position = window_of(lax.axis_index(axis))
     for place, at in ((0, 0), (groups - 1, HALF - ghost)):
 
         @pl.when(position == place)
@@ -278,6 +286,8 @@
 
 def gather_planes(axis, groups, field_refs, ghost_ref, v_ref, s_ref):
     position = lax.axis_index(axis)
+    window = window_of(position)
+    senders = window_of(0) ^ window_of(groups - 1)
     low = low_lanes(HALF)
     nz_local = field_refs[0].shape[1]
     for k, ref in enumerate(field_refs):
@@ -286,10 +296,10 @@
             for kind, target in ((0, v_ref), (1, s_ref)):
                 plane = ref[kind, p]
                 if ghost_ref is not None:
-                    beyond = ghost_ref[(groups - 1) ^ k, kind, p]
+                    beyond = ghost_ref[senders ^ k, kind, p]
                     ghost = beyond.shape[0]
-                    first = jnp.where(position == 0, beyond, plane[:ghost])
-                    last = jnp.where(position == groups - 1, beyond, plane[HALF - ghost :])
+                    first = jnp.where(window == 0, beyond, plane[:ghost])
+                    last = jnp.where(window == groups - 1, beyond, plane[HALF - ghost :])
                     plane = jnp.concatenate([first, plane[ghost : HALF - ghost], last], axis=0)
                 turned = jnp.concatenate([plane, plane], axis=0).T
                 target[base + p + 1 - kind] = jnp.where(low, turned[:HALF], turned[HALF:])
@@ -361,7 +371,7 @@
 
 def ghost_pack_kernel(axis, own, ghost, *refs):
     *window_refs, ready_ref, out_ref = refs
-    at = jnp.where(lax.axis_index(axis) == 0, ghost, own)
+    at = jnp.where(window_of(lax.axis_index(axis)) == 0, ghost, own)
     for k, ref in enumerate(window_refs):
         out_ref[k] = ref[:, :, pl.ds(pl.multiple_of(at, 8), ghost), :]
 
@@ -378,13 +388,33 @@
     b_ref, plane_ref, rhs_in, loc_in = take(4)
     coef_ref, add_in, state_in = (None, None, None) if first else take(3)
     last = steps is not None and steps[-1] == 2 * rhs_in.shape[0] - 1
-    out_ref = take(1)[0] if last else None
-    rhs_ref, add_ref, state_ref = take(3)
+    if last:
+        (out_ref,) = take(1)
+        rhs_ref, state_ref, add_ref = rhs_in, None, refs.pop()
+        add_ref[...] = add_in[...]
+    else:
+        rhs_ref, add_ref, state_ref = take(3)
     loc_ref, *pack_refs = take(peers) if later else (None,)
     coef_out = take(1)[0] if first else None
-    gather, halo_ref, inject_ref, r_ref = refs
+    gather, halo_ref, inject_ref, r_ref, *own_copy = refs
     nz = rhs_in.shape[0]
     position = lax.axis_index(axis)
+    arrival = None
+    if last:
+        b_hbm, (b_ref, sems) = b_ref, own_copy
+        size = 8 * LANES
+        copies = [
+            pltpu.make_async_copy(
+                b_hbm.at[pl.ds(n * size, size)], b_ref.at[pl.ds(n * size, size)], sems.at[n]
+            )
+            for n in range(HALF // 8)
+        ]
+        for copy in copies:
+            copy.start()
+
+        def arrival(n):
+            at = pl.ds(n * size, size)
+            pltpu.make_async_copy(b_hbm.at[at], b_ref.at[at], sems.at[n]).wait()
 
     gather[...] = jnp.zeros(gather.shape, jnp.float32)
     for k in range(peers):
@@ -428,21 +458,19 @@
         state = state + plane_ref[n] * inject_ref[n if n >= 2 else PLANES + n, own, :]
     keep(first_plane + move, state)
 
-    def transition(t, state):
+    for t in range(2, STEPS):
         z = first_plane + move * t
         around = sum_y(sum_x(state), halo_ref[t, own, :])
         if move > 0:
             rhs_ref[z - 1] = around - 27.0 * state
-        state = apply_blocks(b_ref, rhs_ref[z] + around, r_ref)
+        state = apply_blocks(b_ref, rhs_ref[z] + around, r_ref, arrival if t == 2 else None)
         if move < 0:
             state = state + add_ref[z]
         keep(z, state)
-        return state
-
-    state = lax.fori_loop(2, STEPS, transition, state, unroll=True)
     if steps[-1] == nz - 1:
         rhs_ref[nz - 1] = -27.0 * state
-    state_ref[...] = state
+    if not last:
+        state_ref[...] = state
     if later:
         pack_ref = pack_refs[0]
         pack_ref[...] = jnp.zeros(pack_ref.shape, jnp.float32)
@@ -468,7 +496,7 @@
     position = lax.axis_index(axis)
     lines = parts[0].shape[1]
     for k, part in enumerate(parts):
-        at = pl.ds(pl.multiple_of(jnp.bitwise_xor(position, k) * lines, lines), lines)
+        at = pl.ds(pl.multiple_of(window_of(jnp.bitwise_xor(position, k)) * lines, lines), lines)
         out_ref[:, at, :] = v_ref[:, at, :] + part[...]
 
 
@@ -479,17 +507,17 @@
 SMALL = pltpu.CompilerParams(vmem_limit_bytes=16 * 1024 * 1024)
 
 
-def call(kernel, ins, outs, scratch, name, aliases=None):
+def call(kernel, ins, outs, scratch, name, aliases=None, hbm=()):
     return pl.pallas_call(
         kernel,
         out_shape=outs,
-        in_specs=[VMEM] * len(ins),
+        in_specs=[HBM if n in hbm else VMEM for n in range(len(ins))],
         out_specs=[VMEM] * len(outs),
         scratch_shapes=scratch,
         input_output_aliases=aliases or {},
         compiler_params=SMALL,
         name=name,
-    )(*ins)
+    )(*[in_hbm(x) if n in hbm else x for n, x in enumerate(ins)])
 
 
 def in_hbm(a):
@@ -529,12 +557,12 @@
     groups, count = lax.axis_size("gz"), lax.axis_size("gx")
     reach = -(-tail.shape[0] // own)
     assert 2 * reach <= groups
-    shift = reach if 4 * reach <= groups else 0
     pairs = []
-    for g in range(reach):
+    for strip in range(reach):
+        low, high = window_of(strip), window_of(groups - 1 - strip)
         for a in range(count - 1):
-            pairs.append(((g + shift) * count + a, g * count + a + 1))
-            pairs.append(((groups - 1 - g - shift) * count + a + 1, (groups - 1 - g) * count + a))
+            pairs.append((low * count + a, low * count + a + 1))
+            pairs.append((high * count + a + 1, high * count + a))
     return lax.ppermute(tail, ("gz", "gx"), pairs)
 
 
@@ -548,16 +576,16 @@
         [],
         "ghost_pack",
     )
-    end = (groups - 1) * count
-    pairs = [(end + a, a + 1) for a in range(count - 1)]
-    pairs += [(a + 1, end + a) for a in range(count - 1)]
+    low, high = window_of(0) * count, window_of(groups - 1) * count
+    pairs = [(high + a, low + a + 1) for a in range(count - 1)]
+    pairs += [(low + a + 1, high + a) for a in range(count - 1)]
     return lax.ppermute(lines, ("gz", "gx"), pairs)
 
 
 def refresh_ghosts(planes, ghost):
     split = planes.reshape(planes.shape[0], HALF, 2, HALF)
     groups, count = lax.axis_size("gz"), lax.axis_size("gx")
-    places = [g * count + x for x in range(count) for g in range(groups)]
+    places = [window_of(w) * count + x for x in range(count) for w in range(groups)]
     ups = list(zip(places[:-1], places[1:]))
     downs = list(zip(places[1:], places[:-1]))
     before = lax.ppermute(split[..., HALF - 2 * ghost : HALF - ghost], ("gz", "gx"), ups)
@@ -584,7 +612,7 @@
             functools.partial(tail_kernel, "gz", groups),
             out_shape=f32(ghost, LANES, LANES),
             in_specs=[HBM],
-            out_specs=HBM,
+            out_specs=VMEM,
             scratch_shapes=[pltpu.SemaphoreType.DMA((4,))],
             compiler_params=PARAMS,
             name="tail",
@@ -604,7 +632,7 @@
         before, after = line_ghosts(fields, 2, ghost)
         wide = jnp.concatenate([before, fields, after], axis=2)
         windows = [
-            lax.dynamic_slice_in_dim(wide, jnp.bitwise_xor(here, k) * own, HALF, 2)
+            lax.dynamic_slice_in_dim(wide, window_of(jnp.bitwise_xor(here, k)) * own, HALF, 2)
             for k in range(groups)
         ]
     beyond = block_ghosts(tail, own).reshape(ghost * LANES, LANES)
@@ -665,15 +693,13 @@
         packs = to_peers([packs[0], *packs], "gy")
         ins = [*packs, blocks, effects, rhs, loc] + ([] if first else [coef, add, state])
         planes = f32(nz, HALF, LANES)
-        outs = [f32(nz, own, LANES)] if final else []
-        outs += [planes, planes, f32(HALF, LANES)]
+        outs = [f32(nz, own, LANES)] if final else [planes, planes, f32(HALF, LANES)]
         if later:
             outs += [f32(2, HALF, LANES)] + [f32(8 * k, LANES) for k in range(1, peers)]
         outs += [f32(8, PACK_ROWS, LANES)] if first else []
-        at_rhs = 1 if final else 0
-        aliases = {peers + 2: at_rhs}
-        if not first:
-            aliases[peers + 5] = at_rhs + 1
+        aliases = {} if final else {peers + 2: 0}
+        if not first and not final:
+            aliases[peers + 5] = 1
         results = call(
             functools.partial(next_kernel, steps, later, first, peers, "gy", ghost),
             ins,
@@ -683,9 +709,19 @@
                 pltpu.VMEM((STEPS + nz, 8, LANES), jnp.float32),
                 pltpu.VMEM((PLANES + 2, 8, LANES), jnp.float32),
                 plane,
-            ],
+            ]
+            + (
+                [
+                    pltpu.VMEM((LANES * HALF, LANES), jnp.float32),
+                    pltpu.SemaphoreType.DMA((HALF // 8,)),
+                    pltpu.VMEM((nz, HALF, LANES), jnp.float32),
+                ]
+                if final
+                else []
+            ),
             "next_chain",
             aliases,
+            (peers,) if final else (),
         )
         if final:
             change = results[0]

time: 68 us -> 62.6 us (0.921)
  the two profiles are of different devices: /device:TPU:11 before, /device:TPU:0 now
where the time goes in v4:
time: 62.6 us; the launch traced here: 62.4 us
  starting transfers between devices  26.4 us (42%)
  Pallas kernels  22.4 us (36%)
  waiting for transfers between devices  13.4 us (21%)
    ppermute x18, starting transfers between devices, to_peers(): got[k] = lax.ppermute(pieces[k], axis, [(i, i ^ k) for i in range(count)])  25 us
    pallas_call x8, Pallas kernels, call(): pl.pallas_call(kernel, out_shape=outs, in_specs=[HBM if n in hbm else VME...  14.8 us
    ppermute x18, waiting for transfers between devices, to_peers(): got[k] = lax.ppermute(pieces[k], axis, [(i, i ^ k) for i in range(count)])  13.4 us
    pallas_call x1, Pallas kernels, body(): pl.pallas_call(functools.partial(layout_kernel, own, ghost, 'gz'), out_sh...  5.04 us
    pallas_call x1, Pallas kernels, body(): pl.pallas_call(functools.partial(pack_kernel, 'gz', own, ghost), out_shap...  1.3 us
  transfers between devices with their start and end apart: 20, of which 8 were waited for; matrix products, arithmetic and copies ran while one was open for 0% of the time, Pallas kernels for 14%

profile of v4, /device:TPU:0, one launch (start us, length us, event | category | flops | bytes accessed | tf_op | source)
XLA Modules:
  0.0 62.4 jit_solution(17944473407668055825)
XLA Ops:
  0.0 1.2 %tail.1 = f32[16,128,128]{2,1,0:T(8,128)S(1)} custom-call(f32[128,128,128]{2,1,0:T(8,128)} %b_ref.1), custom_call_target="tpu_custom_call" | custom-call | tf_op jit(solution)/shard_map/tail/pallas_call | solution.py:611
  1.2 0.7 %collective-permute-start.4 = (f32[16,128,128]{2,1,0:T(8,128)S(1)}, f32[16,128,128]{2,1,0:T(8,128)S(1)}, u32[]{:S(2)}, u32[]{:S(2)}) collective-permute-start(f32[16,128,128]{2,1,0:T(8,128)S(1)} %tail.1), channel_id=1, source_target_pairs={{8,12},{28,24},{9,13},{29,25},{10,14},{30,26},{11,15},{31,27}} | collective-permute-start | bytes 3145736 | tf_op jit(solution)/shard_map/ppermute | solution.py:566
  2.0 1.3 %pack.1 = (f32[2,2,64,128]{3,2,1,0:T(8,128)S(1)}, f32[2,2,64,128]{3,2,1,0:T(8,128)S(1)}, f32[2,2,64,128]{3,2,1,0:T(8,128)S(1)}, f32[2,2,64,128]{3,2,1,0:T(8,128)S(1)}) custom-call(f32[2,128,128]{2,1,0:T(8,128)} %v_ref.3, f32[2,128,128]{2,1,0:T(8,128)} %s_ref.1), custom_call_target="tpu_custom_call" | custom-call | tf_op jit(solution)/shard_map/pack/pallas_call | solution.py:620
  3.3 3.8 %collective-permute-start = (f32[2,2,64,128]{3,2,1,0:T(8,128)S(1)}, f32[2,2,64,128]{3,2,1,0:T(8,128)S(1)}, u32[]{:S(2)}, u32[]{:S(2)}) collective-permute-start(f32[2,2,64,128]{3,2,1,0:T(8,128)S(1)} %get-tuple-element.41), channel_id=1, source_target_pairs={{0,8},{8,0},{16,24},{24,16},{1,9},{9,1},{17,25},{25,17},{2,10},{10... | collective-permute-start | bytes 393224 | tf_op jit(solution)/shard_map/ppermute | solution.py:531
  7.1 1.4 %collective-permute-start.2 = (f32[2,2,64,128]{3,2,1,0:T(8,128)S(1)}, f32[2,2,64,128]{3,2,1,0:T(8,128)S(1)}, u32[]{:S(2)}, u32[]{:S(2)}) collective-permute-start(f32[2,2,64,128]{3,2,1,0:T(8,128)S(1)} %get-tuple-element.43), channel_id=1, source_target_pairs={{0,24},{8,16},{16,8},{24,0},{1,25},{9,17},{17,9},{25,1},{2,26},{10... | collective-permute-start | bytes 393224 | tf_op jit(solution)/shard_map/ppermute | solution.py:531
  8.5 5.0 %layout.1 = (f32[8192,128]{1,0:T(8,128)S(1)}, f32[8,128]{1,0:T(8,128)S(1)}) custom-call(f32[16384,128]{1,0:T(8,128)} %bitcast.3), custom_call_target="tpu_custom_call" | custom-call | bytes 16777216 | tf_op jit(solution)/shard_map/layout/pallas_call | solution.py:640
  13.6 0.9 %collective-permute-done.2.refs_3_ = f32[2,2,64,128]{3,2,1,0:T(8,128)S(1)} collective-permute-done((f32[2,2,64,128]{3,2,1,0:T(8,128)S(1)}, f32[2,2,64,128]{3,2,1,0:T(8,128)S(1)}, u32[]{:S(2)}, u32[]{:S(2)}) %collective-permute-start.2) | collective-permute-done | bytes 131104 | tf_op jit(solution)/shard_map/ppermute | solution.py:531
  15.2 2.3 %responses.1 = (f32[24,128]{1,0:T(8,128)S(1)}, f32[8,64,128]{2,1,0:T(8,128)S(1)}) custom-call(f32[8192,128]{1,0:T(8,128)S(1)} %patch.1.b_ref.refs_5_.refs_4_), custom_call_target="tpu_custom_call" | custom-call | tf_op jit(solution)/shard_map/responses/pallas_call | solution.py:511
  17.5 1.5 %first_chain.1 = (f32[8,64,128]{2,1,0:T(8,128)S(1)}, f32[2,64,128]{2,1,0:T(8,128)S(1)}, f32[32,128]{1,0:T(8,128)S(1)}, f32[40,128]{1,0:T(8,128)S(1)}, f32[48,128]{1,0:T(8,128)S(1)}) custom-call(f32[2,2,64,128]{3,2,1,0:T(8,128)S(1)} %get-tuple-element.40.refs_0_, f32[2,2,64,128]{3,2,1,0:T(8,128)S(1)} %collective-permute-done.refs_1_, ...), custom_call_target="tpu_custom_call" | custom-call | tf_op jit(solution)/shard_map/first_chain/pallas_call | solution.py:511
  19.0 3.7 %collective-permute-start.7 = (f32[48,128]{1,0:T(8,128)S(1)}, f32[48,128]{1,0:T(8,128)S(1)}, u32[]{:S(2)}, u32[]{:S(2)}) collective-permute-start(f32[48,128]{1,0:T(8,128)S(1)} %get-tuple-element.49), channel_id=1, source_target_pairs={{0,3},{1,2},{2,1},{3,0},{4,7},{5,6},{6,5},{7,4},{8,11},{9,10},{10,... | collective-permute-start | bytes 73736 | tf_op jit(solution)/shard_map/ppermute | solution.py:531
  22.7 0.8 %collective-permute-start.5 = (f32[32,128]{1,0:T(8,128)S(1)}, f32[32,128]{1,0:T(8,128)S(1)}, u32[]{:S(2)}, u32[]{:S(2)}) collective-permute-start(f32[32,128]{1,0:T(8,128)S(1)} %get-tuple-element.47.refs_0_), channel_id=1, source_target_pairs={{0,1},{1,0},{2,3},{3,2},{4,5},{5,4},{6,7},{7,6},{8,9},{9,8},{10,11... | collective-permute-start | bytes 49160 | tf_op jit(solution)/shard_map/ppermute | solution.py:531
  23.5 3.0 %collective-permute-done.5.refs_1_ = f32[32,128]{1,0:T(8,128)S(1)} collective-permute-done((f32[32,128]{1,0:T(8,128)S(1)}, f32[32,128]{1,0:T(8,128)S(1)}, u32[]{:S(2)}, u32[]{:S(2)}) %collective-permute-start.5) | collective-permute-done | bytes 16416 | tf_op jit(solution)/shard_map/ppermute | solution.py:531
  26.5 0.9 %collective-permute-done.6.refs_2_ = f32[40,128]{1,0:T(8,128)S(1)} collective-permute-done((f32[40,128]{1,0:T(8,128)S(1)}, f32[40,128]{1,0:T(8,128)S(1)}, u32[]{:S(2)}, u32[]{:S(2)}) %collective-permute-start.6) | collective-permute-done | bytes 20512 | tf_op jit(solution)/shard_map/ppermute | solution.py:531
  27.4 2.3 %next_chain.4 = (f32[8,64,128]{2,1,0:T(8,128)S(1)}, f32[8,64,128]{2,1,0:T(8,128)S(1)}, f32[64,128]{1,0:T(8,128)S(1)}, f32[2,64,128]{2,1,0:T(8,128)S(1)}, f32[8,1...) custom-call(f32[32,128]{1,0:T(8,128)S(1)} %get-tuple-element.47.refs, ...), custom_call_target="tpu_custom_call", output_to_operand_aliasing={{0}: (6, {})} | custom-call | tf_op jit(solution)/shard_map/next_chain/pallas_call | solution.py:511
  29.7 1.5 %collective-permute-start.10 = (f32[24,128]{1,0:T(8,128)S(1)}, f32[24,128]{1,0:T(8,128)S(1)}, u32[]{:S(2)}, u32[]{:S(2)}) collective-permute-start(f32[24,128]{1,0:T(8,128)S(1)} %get-tuple-element.55), channel_id=1, source_target_pairs={{0,3},{1,2},{2,1},{3,0},{4,7},{5,6},{6,5},{7,4},{8,11},{9,10},{10,... | collective-permute-start | bytes 36872 | tf_op jit(solution)/shard_map/ppermute | solution.py:531
  31.9 2.3 %collective-permute-start.8 = (f32[8,128]{1,0:T(8,128)S(1)}, f32[8,128]{1,0:T(8,128)S(1)}, u32[]{:S(2)}, u32[]{:S(2)}) collective-permute-start(f32[8,128]{1,0:T(8,128)S(1)} %get-tuple-element.53.refs_0_), channel_id=1, source_target_pairs={{0,1},{1,0},{2,3},{3,2},{4,5},{5,4},{6,7},{7,6},{8,9},{9,8},{10,11... | collective-permute-start | bytes 12296 | tf_op jit(solution)/shard_map/ppermute | solution.py:531
  34.2 1.6 %collective-permute-done.8.refs_1_ = f32[8,128]{1,0:T(8,128)S(1)} collective-permute-done((f32[8,128]{1,0:T(8,128)S(1)}, f32[8,128]{1,0:T(8,128)S(1)}, u32[]{:S(2)}, u32[]{:S(2)}) %collective-permute-start.8) | collective-permute-done | bytes 4128 | tf_op jit(solution)/shard_map/ppermute | solution.py:531
  35.8 2.7 %next_chain.5 = (f32[8,64,128]{2,1,0:T(8,128)S(1)}, f32[8,64,128]{2,1,0:T(8,128)S(1)}, f32[64,128]{1,0:T(8,128)S(1)}, f32[2,64,128]{2,1,0:T(8,128)S(1)}, f32[8,1...) custom-call(f32[8,128]{1,0:T(8,128)S(1)} %get-tuple-element.53.refs_, ...), custom_call_target="tpu_custom_call", output_to_operand_aliasing={{0}: (6, {}), {1}: (9, {})} | custom-call | tf_op jit(solution)/shard_map/next_chain/pallas_call | solution.py:511
  38.5 2.6 %collective-permute-start.13 = (f32[24,128]{1,0:T(8,128)S(1)}, f32[24,128]{1,0:T(8,128)S(1)}, u32[]{:S(2)}, u32[]{:S(2)}) collective-permute-start(f32[24,128]{1,0:T(8,128)S(1)} %get-tuple-element.63), channel_id=1, source_target_pairs={{0,3},{1,2},{2,1},{3,0},{4,7},{5,6},{6,5},{7,4},{8,11},{9,10},{10,... | collective-permute-start | bytes 36872 | tf_op jit(solution)/shard_map/ppermute | solution.py:531
  41.1 0.9 %collective-permute-start.12 = (f32[16,128]{1,0:T(8,128)S(1)}, f32[16,128]{1,0:T(8,128)S(1)}, u32[]{:S(2)}, u32[]{:S(2)}) collective-permute-start(f32[16,128]{1,0:T(8,128)S(1)} %get-tuple-element.62), channel_id=1, source_target_pairs={{0,2},{1,3},{2,0},{3,1},{4,6},{5,7},{6,4},{7,5},{8,10},{9,11},{10,... | collective-permute-start | bytes 24584 | tf_op jit(solution)/shard_map/ppermute | solution.py:531
  42.0 1.0 %collective-permute-start.11 = (f32[8,128]{1,0:T(8,128)S(1)}, f32[8,128]{1,0:T(8,128)S(1)}, u32[]{:S(2)}, u32[]{:S(2)}) collective-permute-start(f32[8,128]{1,0:T(8,128)S(1)} %get-tuple-element.61.refs_0_), channel_id=1, source_target_pairs={{0,1},{1,0},{2,3},{3,2},{4,5},{5,4},{6,7},{7,6},{8,9},{9,8},{10,11... | collective-permute-start | bytes 12296 | tf_op jit(solution)/shard_map/ppermute | solution.py:531
  43.0 2.7 %collective-permute-done.11.refs_1_ = f32[8,128]{1,0:T(8,128)S(1)} collective-permute-done((f32[8,128]{1,0:T(8,128)S(1)}, f32[8,128]{1,0:T(8,128)S(1)}, u32[]{:S(2)}, u32[]{:S(2)}) %collective-permute-start.11) | collective-permute-done | bytes 4128 | tf_op jit(solution)/shard_map/ppermute | solution.py:531
  45.7 2.3 %next_chain.6 = (f32[8,64,128]{2,1,0:T(8,128)S(1)}, f32[8,64,128]{2,1,0:T(8,128)S(1)}, f32[64,128]{1,0:T(8,128)S(1)}, f32[2,64,128]{2,1,0:T(8,128)S(1)}, f32[8,1...) custom-call(f32[8,128]{1,0:T(8,128)S(1)} %get-tuple-element.61.refs_, ...), custom_call_target="tpu_custom_call", output_to_operand_aliasing={{0}: (6, {}), {1}: (9, {})} | custom-call | tf_op jit(solution)/shard_map/next_chain/pallas_call | solution.py:511
  48.0 1.5 %collective-permute-start.16 = (f32[24,128]{1,0:T(8,128)S(1)}, f32[24,128]{1,0:T(8,128)S(1)}, u32[]{:S(2)}, u32[]{:S(2)}) collective-permute-start(f32[24,128]{1,0:T(8,128)S(1)} %get-tuple-element.70), channel_id=1, source_target_pairs={{0,3},{1,2},{2,1},{3,0},{4,7},{5,6},{6,5},{7,4},{8,11},{9,10},{10,... | collective-permute-start | bytes 36872 | tf_op jit(solution)/shard_map/ppermute | solution.py:531
  49.5 1.0 %collective-permute-start.15 = (f32[16,128]{1,0:T(8,128)S(1)}, f32[16,128]{1,0:T(8,128)S(1)}, u32[]{:S(2)}, u32[]{:S(2)}) collective-permute-start(f32[16,128]{1,0:T(8,128)S(1)} %get-tuple-element.69), channel_id=1, source_target_pairs={{0,2},{1,3},{2,0},{3,1},{4,6},{5,7},{6,4},{7,5},{8,10},{9,11},{10,... | collective-permute-start | bytes 24584 | tf_op jit(solution)/shard_map/ppermute | solution.py:531
  50.4 2.0 %collective-permute-start.14 = (f32[8,128]{1,0:T(8,128)S(1)}, f32[8,128]{1,0:T(8,128)S(1)}, u32[]{:S(2)}, u32[]{:S(2)}) collective-permute-start(f32[8,128]{1,0:T(8,128)S(1)} %get-tuple-element.68.refs_0_), channel_id=1, source_target_pairs={{0,1},{1,0},{2,3},{3,2},{4,5},{5,4},{6,7},{7,6},{8,9},{9,8},{10,11... | collective-permute-start | bytes 12296 | tf_op jit(solution)/shard_map/ppermute | solution.py:531
  52.5 1.6 %collective-permute-done.14.refs_1_ = f32[8,128]{1,0:T(8,128)S(1)} collective-permute-done((f32[8,128]{1,0:T(8,128)S(1)}, f32[8,128]{1,0:T(8,128)S(1)}, u32[]{:S(2)}, u32[]{:S(2)}) %collective-permute-start.14) | collective-permute-done | bytes 4128 | tf_op jit(solution)/shard_map/ppermute | solution.py:531
  54.1 3.1 %next_chain.7 = f32[8,32,128]{2,1,0:T(8,128)S(1)} custom-call(f32[8,128]{1,0:T(8,128)S(1)} %get-tuple-element.68.refs_0_, f32[8,128]{1,0:T(8,128)S(1)} %collective-permute-done.14.refs_1_, f32[16,128]{1,0:T(8,128)S(1)} %collective-permute-done.15.refs_2_, f32[24,128]{1,0:T(8,128)S(1)} %collective-permute-done.16.refs_3_, f32[8192,128]{1,0:T(8,128)} %copy-done, ...), custom_call_target="tpu_custom_call" | custom-call | tf_op jit(solution)/shard_map/next_chain/pallas_call | solution.py:511
  57.3 0.8 %collective-permute-start.18 = (f32[2,32,128]{2,1,0:T(8,128)S(1)}, f32[2,32,128]{2,1,0:T(8,128)S(1)}, u32[]{:S(2)}, u32[]{:S(2)}) collective-permute-start(f32[2,32,128]{2,1,0:T(8,128)S(1)} %get-tuple-element.76), channel_id=1, source_target_pairs={{0,16},{8,24},{16,0},{24,8},{1,17},{9,25},{17,1},{25,9},{2,18},{10... | collective-permute-start | bytes 98312 | tf_op jit(solution)/shard_map/ppermute | solution.py:531
  58.0 1.1 %collective-permute-start.19 = (f32[2,32,128]{2,1,0:T(8,128)S(1)}, f32[2,32,128]{2,1,0:T(8,128)S(1)}, u32[]{:S(2)}, u32[]{:S(2)}) collective-permute-start(f32[2,32,128]{2,1,0:T(8,128)S(1)} %get-tuple-element.75), channel_id=1, source_target_pairs={{0,24},{8,16},{16,8},{24,0},{1,25},{9,17},{17,9},{25,1},{2,26},{10... | collective-permute-start | bytes 98312 | tf_op jit(solution)/shard_map/ppermute | solution.py:531
  59.1 2.3 %collective-permute-done.18.refs_2_ = f32[2,32,128]{2,1,0:T(8,128)S(1)} collective-permute-done((f32[2,32,128]{2,1,0:T(8,128)S(1)}, f32[2,32,128]{2,1,0:T(8,128)S(1)}, u32[]{:S(2)}, u32[]{:S(2)}) %collective-permute-start.18) | collective-permute-done | bytes 32800 | tf_op jit(solution)/shard_map/ppermute | solution.py:531
  61.7 0.7 %finish.1 = f32[2,128,128]{2,1,0:T(8,128)} custom-call(f32[2,128,128]{2,1,0:T(8,128)S(1)} %copy-done.1, f32[2,32,128]{2,1,0:T(8,128)S(1)} %get-tuple-element.78.refs_0_, f32[2,32,128]{2,1,0:T(8,128)S(1)} %collective-permute-done.17.refs_1_, f32[2,32,128]{2,1,0:T(8,128)S(1)} %collective-permute-done.18.refs_2_, f32[2,32,128]{2,1,0:T(8,128)S(1)} %collective-permute-done.19.refs_3_), custom_call_target="tpu_custom_call" | custom-call | tf_op jit(solution)/shard_map/finish/pallas_call | solution.py:511
  (25 shorter events, 1.8 us)
Async XLA Ops:
  1.2 13.9 %collective-permute-start.4 = (f32[16,128,128]{2,1,0:T(8,128)S(1)}, f32[16,128,128]{2,1,0:T(8,128)S(1)}, u32[]{:S(2)}, u32[]{:S(2)}) collective-permute-start(f32[16,128,128]{2,1,0:T(8,128)S(1)} %tail.1), channel_id=1, source_target_pairs={{8,12},{28,24},{9,13},{29,25},{10,14},{30,26},{11,15},{31,27}} | collective-permute-start | bytes 3145736 | tf_op jit(solution)/shard_map/ppermute | solution.py:566
  3.3 10.3 %collective-permute-start = (f32[2,2,64,128]{3,2,1,0:T(8,128)S(1)}, f32[2,2,64,128]{3,2,1,0:T(8,128)S(1)}, u32[]{:S(2)}, u32[]{:S(2)}) collective-permute-start(f32[2,2,64,128]{3,2,1,0:T(8,128)S(1)} %get-tuple-element.41), channel_id=1, source_target_pairs={{0,8},{8,0},{16,24},{24,16},{1,9},{9,1},{17,25},{25,17},{2,10},{10... | collective-permute-start | bytes 393224 | tf_op jit(solution)/shard_map/ppermute | solution.py:531
  7.1 6.5 %collective-permute-start.1 = (f32[2,2,64,128]{3,2,1,0:T(8,128)S(1)}, f32[2,2,64,128]{3,2,1,0:T(8,128)S(1)}, u32[]{:S(2)}, u32[]{:S(2)}) collective-permute-start(f32[2,2,64,128]{3,2,1,0:T(8,128)S(1)} %get-tuple-element.42), channel_id=1, source_target_pairs={{0,16},{8,24},{16,0},{24,8},{1,17},{9,25},{17,1},{25,9},{2,18},{10... | collective-permute-start | bytes 393224 | tf_op jit(solution)/shard_map/ppermute | solution.py:531
  7.1 7.4 %collective-permute-start.2 = (f32[2,2,64,128]{3,2,1,0:T(8,128)S(1)}, f32[2,2,64,128]{3,2,1,0:T(8,128)S(1)}, u32[]{:S(2)}, u32[]{:S(2)}) collective-permute-start(f32[2,2,64,128]{3,2,1,0:T(8,128)S(1)} %get-tuple-element.43), channel_id=1, source_target_pairs={{0,24},{8,16},{16,8},{24,0},{1,25},{9,17},{17,9},{25,1},{2,26},{10... | collective-permute-start | bytes 393224 | tf_op jit(solution)/shard_map/ppermute | solution.py:531
  14.5 3.0 %collective-permute-start.3 = (f32[4,2,2,16,128]{4,3,2,1,0:T(8,128)S(1)}, f32[4,2,2,16,128]{4,3,2,1,0:T(8,128)S(1)}, u32[]{:S(2)}, u32[]{:S(2)}) collective-permute-start(f32[4,2,2,16,128]{4,3,2,1,0:T(8,128)S(1)} %ghost_pack.1), channel_id=1, source_target_pairs={{24,12},{12,24},{25,13},{13,25},{26,14},{14,26},{27,15},{15,27}} | collective-permute-start | bytes 393224 | tf_op jit(solution)/shard_map/ppermute | solution.py:582
  15.2 30.5 %copy-start = (f32[8192,128]{1,0:T(8,128)}, f32[8192,128]{1,0:T(8,128)S(1)}, u32[]{:S(2)}) copy-start(f32[8192,128]{1,0:T(8,128)S(1)} %patch.1.b_ref.refs_5_.refs_4_) | copy-start | bytes 12582916
  19.0 8.4 %collective-permute-start.7 = (f32[48,128]{1,0:T(8,128)S(1)}, f32[48,128]{1,0:T(8,128)S(1)}, u32[]{:S(2)}, u32[]{:S(2)}) collective-permute-start(f32[48,128]{1,0:T(8,128)S(1)} %get-tuple-element.49), channel_id=1, source_target_pairs={{0,3},{1,2},{2,1},{3,0},{4,7},{5,6},{6,5},{7,4},{8,11},{9,10},{10,... | collective-permute-start | bytes 73736 | tf_op jit(solution)/shard_map/ppermute | solution.py:531
  22.7 4.7 %collective-permute-start.6 = (f32[40,128]{1,0:T(8,128)S(1)}, f32[40,128]{1,0:T(8,128)S(1)}, u32[]{:S(2)}, u32[]{:S(2)}) collective-permute-start(f32[40,128]{1,0:T(8,128)S(1)} %get-tuple-element.48), channel_id=1, source_target_pairs={{0,2},{1,3},{2,0},{3,1},{4,6},{5,7},{6,4},{7,5},{8,10},{9,11},{10,... | collective-permute-start | bytes 61448 | tf_op jit(solution)/shard_map/ppermute | solution.py:531
  22.7 3.7 %collective-permute-start.5 = (f32[32,128]{1,0:T(8,128)S(1)}, f32[32,128]{1,0:T(8,128)S(1)}, u32[]{:S(2)}, u32[]{:S(2)}) collective-permute-start(f32[32,128]{1,0:T(8,128)S(1)} %get-tuple-element.47.refs_0_), channel_id=1, source_target_pairs={{0,1},{1,0},{2,3},{3,2},{4,5},{5,4},{6,7},{7,6},{8,9},{9,8},{10,11... | collective-permute-start | bytes 49160 | tf_op jit(solution)/shard_map/ppermute | solution.py:531
  29.7 6.1 %collective-permute-start.10 = (f32[24,128]{1,0:T(8,128)S(1)}, f32[24,128]{1,0:T(8,128)S(1)}, u32[]{:S(2)}, u32[]{:S(2)}) collective-permute-start(f32[24,128]{1,0:T(8,128)S(1)} %get-tuple-element.55), channel_id=1, source_target_pairs={{0,3},{1,2},{2,1},{3,0},{4,7},{5,6},{6,5},{7,4},{8,11},{9,10},{10,... | collective-permute-start | bytes 36872 | tf_op jit(solution)/shard_map/ppermute | solution.py:531
  31.2 4.6 %collective-permute-start.9 = (f32[16,128]{1,0:T(8,128)S(1)}, f32[16,128]{1,0:T(8,128)S(1)}, u32[]{:S(2)}, u32[]{:S(2)}) collective-permute-start(f32[16,128]{1,0:T(8,128)S(1)} %get-tuple-element.54), channel_id=1, source_target_pairs={{0,2},{1,3},{2,0},{3,1},{4,6},{5,7},{6,4},{7,5},{8,10},{9,11},{10,... | collective-permute-start | bytes 24584 | tf_op jit(solution)/shard_map/ppermute | solution.py:531
  31.9 3.9 %collective-permute-start.8 = (f32[8,128]{1,0:T(8,128)S(1)}, f32[8,128]{1,0:T(8,128)S(1)}, u32[]{:S(2)}, u32[]{:S(2)}) collective-permute-start(f32[8,128]{1,0:T(8,128)S(1)} %get-tuple-element.53.refs_0_), channel_id=1, source_target_pairs={{0,1},{1,0},{2,3},{3,2},{4,5},{5,4},{6,7},{7,6},{8,9},{9,8},{10,11... | collective-permute-start | bytes 12296 | tf_op jit(solution)/shard_map/ppermute | solution.py:531
  38.5 7.2 %collective-permute-start.13 = (f32[24,128]{1,0:T(8,128)S(1)}, f32[24,128]{1,0:T(8,128)S(1)}, u32[]{:S(2)}, u32[]{:S(2)}) collective-permute-start(f32[24,128]{1,0:T(8,128)S(1)} %get-tuple-element.63), channel_id=1, source_target_pairs={{0,3},{1,2},{2,1},{3,0},{4,7},{5,6},{6,5},{7,4},{8,11},{9,10},{10,... | collective-permute-start | bytes 36872 | tf_op jit(solution)/shard_map/ppermute | solution.py:531
  41.1 4.6 %collective-permute-start.12 = (f32[16,128]{1,0:T(8,128)S(1)}, f32[16,128]{1,0:T(8,128)S(1)}, u32[]{:S(2)}, u32[]{:S(2)}) collective-permute-start(f32[16,128]{1,0:T(8,128)S(1)} %get-tuple-element.62), channel_id=1, source_target_pairs={{0,2},{1,3},{2,0},{3,1},{4,6},{5,7},{6,4},{7,5},{8,10},{9,11},{10,... | collective-permute-start | bytes 24584 | tf_op jit(solution)/shard_map/ppermute | solution.py:531
  42.0 3.7 %collective-permute-start.11 = (f32[8,128]{1,0:T(8,128)S(1)}, f32[8,128]{1,0:T(8,128)S(1)}, u32[]{:S(2)}, u32[]{:S(2)}) collective-permute-start(f32[8,128]{1,0:T(8,128)S(1)} %get-tuple-element.61.refs_0_), channel_id=1, source_target_pairs={{0,1},{1,0},{2,3},{3,2},{4,5},{5,4},{6,7},{7,6},{8,9},{9,8},{10,11... | collective-permute-start | bytes 12296 | tf_op jit(solution)/shard_map/ppermute | solution.py:531
  45.7 16.0 %copy-start.1 = (f32[2,128,128]{2,1,0:T(8,128)S(1)}, f32[2,128,128]{2,1,0:T(8,128)}, u32[]{:S(2)}) copy-start(f32[2,128,128]{2,1,0:T(8,128)} %v_ref.3) | copy-start | bytes 393220
  48.0 6.1 %collective-permute-start.16 = (f32[24,128]{1,0:T(8,128)S(1)}, f32[24,128]{1,0:T(8,128)S(1)}, u32[]{:S(2)}, u32[]{:S(2)}) collective-permute-start(f32[24,128]{1,0:T(8,128)S(1)} %get-tuple-element.70), channel_id=1, source_target_pairs={{0,3},{1,2},{2,1},{3,0},{4,7},{5,6},{6,5},{7,4},{8,11},{9,10},{10,... | collective-permute-start | bytes 36872 | tf_op jit(solution)/shard_map/ppermute | solution.py:531
  49.5 4.6 %collective-permute-start.15 = (f32[16,128]{1,0:T(8,128)S(1)}, f32[16,128]{1,0:T(8,128)S(1)}, u32[]{:S(2)}, u32[]{:S(2)}) collective-permute-start(f32[16,128]{1,0:T(8,128)S(1)} %get-tuple-element.69), channel_id=1, source_target_pairs={{0,2},{1,3},{2,0},{3,1},{4,6},{5,7},{6,4},{7,5},{8,10},{9,11},{10,... | collective-permute-start | bytes 24584 | tf_op jit(solution)/shard_map/ppermute | solution.py:531
  50.4 3.6 %collective-permute-start.14 = (f32[8,128]{1,0:T(8,128)S(1)}, f32[8,128]{1,0:T(8,128)S(1)}, u32[]{:S(2)}, u32[]{:S(2)}) collective-permute-start(f32[8,128]{1,0:T(8,128)S(1)} %get-tuple-element.68.refs_0_), channel_id=1, source_target_pairs={{0,1},{1,0},{2,3},{3,2},{4,5},{5,4},{6,7},{7,6},{8,9},{9,8},{10,11... | collective-permute-start | bytes 12296 | tf_op jit(solution)/shard_map/ppermute | solution.py:531
  57.2 1.9 %collective-permute-start.17 = (f32[2,32,128]{2,1,0:T(8,128)S(1)}, f32[2,32,128]{2,1,0:T(8,128)S(1)}, u32[]{:S(2)}, u32[]{:S(2)}) collective-permute-start(f32[2,32,128]{2,1,0:T(8,128)S(1)} %get-tuple-element.77), channel_id=1, source_target_pairs={{0,8},{8,0},{16,24},{24,16},{1,9},{9,1},{17,25},{25,17},{2,10},{10... | collective-permute-start | bytes 98312 | tf_op jit(solution)/shard_map/ppermute | solution.py:531
  57.3 4.2 %collective-permute-start.18 = (f32[2,32,128]{2,1,0:T(8,128)S(1)}, f32[2,32,128]{2,1,0:T(8,128)S(1)}, u32[]{:S(2)}, u32[]{:S(2)}) collective-permute-start(f32[2,32,128]{2,1,0:T(8,128)S(1)} %get-tuple-element.76), channel_id=1, source_target_pairs={{0,16},{8,24},{16,0},{24,8},{1,17},{9,25},{17,1},{25,9},{2,18},{10... | collective-permute-start | bytes 98312 | tf_op jit(solution)/shard_map/ppermute | solution.py:531
  58.0 3.7 %collective-permute-start.19 = (f32[2,32,128]{2,1,0:T(8,128)S(1)}, f32[2,32,128]{2,1,0:T(8,128)S(1)}, u32[]{:S(2)}, u32[]{:S(2)}) collective-permute-start(f32[2,32,128]{2,1,0:T(8,128)S(1)} %get-tuple-element.75), channel_id=1, source_target_pairs={{0,24},{8,16},{16,8},{24,0},{1,25},{9,17},{17,9},{25,1},{2,26},{10... | collective-permute-start | bytes 98312 | tf_op jit(solution)/shard_map/ppermute | solution.py:531

commit v5 on v4

--- a/solution.py
+++ b/solution.py
@@ -110,8 +110,7 @@
 
 
 def layout_kernel(own, ghost, axis, b_ref, *refs):
-    *ghost_refs, out_ref, ready_ref, window, sems = refs
-    ready_ref[...] = jnp.zeros(ready_ref.shape, jnp.float32)
+    *ghost_refs, out_ref, window, sems = refs
     ghost_ref = ghost_refs[0] if ghost_refs else b_ref
     count = b_ref.shape[0] // LANES
     position = window_of(lax.axis_index(axis))
@@ -137,16 +136,44 @@
     for copy in copies:
         copy.wait()
 
-    def one(outer, carry):
-        for u in range(8):
-            i = outer * 8 + u
-            top = window[pl.ds(i, HALF, stride=LANES), :]
-            bottom = window[pl.ds(i + HALF, HALF, stride=LANES), :]
-            at = pl.multiple_of(i * LANES, LANES)
-            out_ref[pl.ds(at, LANES), :] = jnp.concatenate([top, bottom], axis=0).T
-        return carry
-
-    lax.fori_loop(0, HALF // 8, one, 0)
+    lax.fori_loop(0, HALF // 8, functools.partial(turn_rows, window, out_ref), 0)
+
+
+def turn_rows(window, out_ref, outer, carry):
+    for u in range(8):
+        i = outer * 8 + u
+        top = window[pl.ds(i, HALF, stride=LANES), :]
+        bottom = window[pl.ds(i + HALF, HALF, stride=LANES), :]
+        at = pl.multiple_of(i * LANES, LANES)
+        out_ref[pl.ds(at, LANES), :] = jnp.concatenate([top, bottom], axis=0).T
+    return carry
+
+
+def strip_kernel(own, ghost, axis, b_ref, out_ref, window, sems):
+    position = window_of(lax.axis_index(axis))
+    parts = sems.shape[0]
+    size = HALF // parts
+    copies = [[] for _ in range(parts)]
+    for n in range(parts):
+        for half in range(2):
+            rows = pl.ds(half * HALF + n * size, size)
+            for c in range(HALF // ghost):
+                at = jnp.clip(position * own - ghost + c * ghost, 0, b_ref.shape[0] - ghost)
+                copies[n].append(
+                    pltpu.make_async_copy(
+                        b_ref.at[pl.ds(at, ghost), rows, :],
+                        window.at[pl.ds(c * ghost, ghost), rows, :],
+                        sems.at[n, half, c],
+                    )
+                )
+    for copy in sum(copies, []):
+        copy.start()
+    flat = window.reshape(HALF * LANES, LANES)
+    for n in range(parts):
+        for copy in copies[n]:
+            copy.wait()
+        turn = functools.partial(turn_rows, flat, out_ref)
+        lax.fori_loop(n * size // 8, (n + 1) * size // 8, turn, 0)
 
 
 def tail_kernel(axis, groups, b_ref, tail_ref, sems):
@@ -188,7 +215,7 @@
         copy.wait()
 
 
-def patch_kernel(axis, groups, b_in, beyond, out_ref):
+def patch_kernel(axis, groups, b_in, beyond, early_ref, out_ref):
     ghost = beyond.shape[0] // LANES
     per_turn = HALF // ghost
     unroll = 4
@@ -221,7 +248,20 @@
             lax.fori_loop(0, HALF // per_turn // unroll, one, 0)
 
 
-def responses_kernel(b_ref, pack_ref, plane_ref, r_ref, many_ref):
+def responses_kernel(groups, at_end, b_ref, *refs):
+    pack_ref, plane_ref, r_ref, many_ref = refs[-4:]
+    if at_end is None:
+        responses(b_ref, pack_ref, plane_ref, r_ref, many_ref)
+        return
+    window = window_of(lax.axis_index("gz"))
+    ends = jnp.logical_or(window == 0, window == groups - 1)
+
+    @pl.when(ends if at_end else jnp.logical_not(ends))
+    def _():
+        responses(b_ref, pack_ref, plane_ref, r_ref, many_ref)
+
+
+def responses(b_ref, pack_ref, plane_ref, r_ref, many_ref):
     pack_ref[...] = jnp.zeros(pack_ref.shape, jnp.float32)
     firsts = [block_column(b_ref, 0), block_column(b_ref, LANES - 1)]
     for side, first in enumerate(firsts):
@@ -637,42 +677,53 @@
         ]
     beyond = block_ghosts(tail, own).reshape(ghost * LANES, LANES)
     turned = LANES * HALF * LANES * 4
-    blocks, ready = pl.pallas_call(
-        functools.partial(layout_kernel, own, ghost, "gz"),
-        out_shape=[f32(LANES * HALF, LANES), f32(8, LANES)],
-        in_specs=[HBM] * (1 if late else 2),
-        out_specs=[VMEM, VMEM],
-        scratch_shapes=[
-            pltpu.VMEM((HALF * LANES, LANES), jnp.float32),
-            pltpu.SemaphoreType.DMA((HALF // math.gcd(own, ghost),)),
-        ],
+    if late:
+        turn, sources = strip_kernel, [block_inverse]
+        window, sems = (HALF, LANES, LANES), (4, 2, HALF // ghost)
+    else:
+        turn, sources = layout_kernel, [rows, beyond]
+        window, sems = (HALF * LANES, LANES), (HALF // math.gcd(own, ghost),)
+    blocks = pl.pallas_call(
+        functools.partial(turn, own, ghost, "gz"),
+        out_shape=f32(LANES * HALF, LANES),
+        in_specs=[HBM] * len(sources),
+        out_specs=VMEM,
+        scratch_shapes=[pltpu.VMEM(window, jnp.float32), pltpu.SemaphoreType.DMA(sems)],
         compiler_params=PARAMS,
         cost_estimate=pl.CostEstimate(flops=0, bytes_accessed=4 * turned, transcendentals=0),
         name="layout",
-    )(*[in_hbm(a) for a in ([rows] if late else [rows, beyond])])
+    )(*[in_hbm(a) for a in sources])
     fields_here = to_peers(windows, "gz")
     ghosts_here = []
+    plane = pltpu.VMEM((HALF, LANES), jnp.float32)
+
+    def respond(at_end, ins, aliases=None):
+        return call(
+            functools.partial(responses_kernel, groups, at_end),
+            ins,
+            [f32(PACK_ROWS, LANES), f32(PLANES, HALF, LANES)],
+            [plane, pltpu.VMEM((PLANES, HALF, LANES), jnp.float32)],
+            "responses",
+            aliases,
+        )
+
     if late:
-        ghosts_here = [window_ghosts(fields_here, ready, own, ghost)]
+        early = respond(False, [blocks])
+        ghosts_here = [window_ghosts(fields_here, early[0], own, ghost)]
         blocks = pl.pallas_call(
             functools.partial(patch_kernel, "gz", groups),
             out_shape=f32(LANES * HALF, LANES),
-            in_specs=[VMEM, VMEM],
+            in_specs=[VMEM] * 3,
             out_specs=VMEM,
             input_output_aliases={0: 0},
             compiler_params=PARAMS,
             name="patch",
-        )(blocks, beyond)
-
-
-    plane = pltpu.VMEM((HALF, LANES), jnp.float32)
-    answers, effects = call(
-        responses_kernel,
-        [blocks],
-        [f32(PACK_ROWS, LANES), f32(PLANES, HALF, LANES)],
-        [plane, pltpu.VMEM((PLANES, HALF, LANES), jnp.float32)],
-        "responses",
-    )
+        )(blocks, beyond, early[0])
+
+    if late:
+        answers, effects = respond(True, [blocks, *early], {1: 0, 2: 1})
+    else:
+        answers, effects = respond(None, [blocks])
     first_rows = PACK_ROWS + 8 * (-(-nz // 8))
     rhs, loc, *packs = call(
         functools.partial(first_kernel, "gz", groups, late),

time: 62.6 us -> 62.1 us (level)
    pallas_call x8 -> x9, Pallas kernels: 14.8 us -> 15.1 us  [call(): pl.pallas_call(kernel, out_shape=outs, in_specs=[HBM if n in hbm else VME...]
  transfers between devices with their start and end apart: 20 -> 20, of which waited for: 8 -> 7; matrix products, arithmetic and copies ran while one was open for 0% -> 0% of each run, Pallas kernels for 14% -> 13%
where the time goes in v5:
time: 62.1 us; the launch traced here: 61.9 us
  starting transfers between devices  26.4 us (43%)
  Pallas kernels  22.1 us (36%)
  waiting for transfers between devices  13.2 us (21%)
    ppermute x18, starting transfers between devices, to_peers(): got[k] = lax.ppermute(pieces[k], axis, [(i, i ^ k) for i in range(count)])  25 us
    pallas_call x9, Pallas kernels, call(): pl.pallas_call(kernel, out_shape=outs, in_specs=[HBM if n in hbm else VME...  15.1 us
    ppermute x18, waiting for transfers between devices, to_peers(): got[k] = lax.ppermute(pieces[k], axis, [(i, i ^ k) for i in range(count)])  13.2 us
    pallas_call x1, Pallas kernels, body(): pl.pallas_call(functools.partial(turn, own, ghost, 'gz'), out_shape=f32(L...  4.45 us
    pallas_call x1, Pallas kernels, body(): pl.pallas_call(functools.partial(pack_kernel, 'gz', own, ghost), out_shap...  1.3 us
  transfers between devices with their start and end apart: 20, of which 7 were waited for; matrix products, arithmetic and copies ran while one was open for 0% of the time, Pallas kernels for 13%

profile of v5, /device:TPU:0, one launch (start us, length us, event | category | flops | bytes accessed | tf_op | source)
XLA Modules:
  0.0 61.9 jit_solution(8579033459157935195)
XLA Ops:
  0.0 1.2 %tail.1 = f32[16,128,128]{2,1,0:T(8,128)S(1)} custom-call(f32[128,128,128]{2,1,0:T(8,128)} %b_ref.3), custom_call_target="tpu_custom_call" | custom-call | tf_op jit(solution)/shard_map/tail/pallas_call | solution.py:651
  1.2 0.7 %collective-permute-start.4 = (f32[16,128,128]{2,1,0:T(8,128)S(1)}, f32[16,128,128]{2,1,0:T(8,128)S(1)}, u32[]{:S(2)}, u32[]{:S(2)}) collective-permute-start(f32[16,128,128]{2,1,0:T(8,128)S(1)} %tail.1), channel_id=1, source_target_pairs={{8,12},{28,24},{9,13},{29,25},{10,14},{30,26},{11,15},{31,27}} | collective-permute-start | bytes 3145736 | tf_op jit(solution)/shard_map/ppermute | solution.py:606
  2.0 1.3 %pack.1 = (f32[2,2,64,128]{3,2,1,0:T(8,128)S(1)}, f32[2,2,64,128]{3,2,1,0:T(8,128)S(1)}, f32[2,2,64,128]{3,2,1,0:T(8,128)S(1)}, f32[2,2,64,128]{3,2,1,0:T(8,128)S(1)}) custom-call(f32[2,128,128]{2,1,0:T(8,128)} %v_ref.3, f32[2,128,128]{2,1,0:T(8,128)} %s_ref.1), custom_call_target="tpu_custom_call" | custom-call | tf_op jit(solution)/shard_map/pack/pallas_call | solution.py:660
  3.3 3.8 %collective-permute-start = (f32[2,2,64,128]{3,2,1,0:T(8,128)S(1)}, f32[2,2,64,128]{3,2,1,0:T(8,128)S(1)}, u32[]{:S(2)}, u32[]{:S(2)}) collective-permute-start(f32[2,2,64,128]{3,2,1,0:T(8,128)S(1)} %get-tuple-element.41), channel_id=1, source_target_pairs={{0,8},{8,0},{16,24},{24,16},{1,9},{9,1},{17,25},{25,17},{2,10},{10... | collective-permute-start | bytes 393224 | tf_op jit(solution)/shard_map/ppermute | solution.py:571
  7.1 1.4 %collective-permute-start.2 = (f32[2,2,64,128]{3,2,1,0:T(8,128)S(1)}, f32[2,2,64,128]{3,2,1,0:T(8,128)S(1)}, u32[]{:S(2)}, u32[]{:S(2)}) collective-permute-start(f32[2,2,64,128]{3,2,1,0:T(8,128)S(1)} %get-tuple-element.43), channel_id=1, source_target_pairs={{0,24},{8,16},{16,8},{24,0},{1,25},{9,17},{17,9},{25,1},{2,26},{10... | collective-permute-start | bytes 393224 | tf_op jit(solution)/shard_map/ppermute | solution.py:571
  8.5 4.4 %layout.1.b_ref.b_in = f32[8192,128]{1,0:T(8,128)S(1)} custom-call(f32[128,128,128]{2,1,0:T(8,128)} %b_ref.3), custom_call_target="tpu_custom_call" | custom-call | bytes 16777216 | tf_op jit(solution)/shard_map/layout/pallas_call | solution.py:686
  13.0 2.3 %responses.2 = (f32[24,128]{1,0:T(8,128)S(1)}, f32[8,64,128]{2,1,0:T(8,128)S(1)}) custom-call(f32[8192,128]{1,0:T(8,128)S(1)} %layout.1.b_ref.b_in), custom_call_target="tpu_custom_call" | custom-call | tf_op jit(solution)/shard_map/responses/pallas_call | solution.py:551
  15.3 0.7 %collective-permute-start.3 = (f32[4,2,2,16,128]{4,3,2,1,0:T(8,128)S(1)}, f32[4,2,2,16,128]{4,3,2,1,0:T(8,128)S(1)}, u32[]{:S(2)}, u32[]{:S(2)}) collective-permute-start(f32[4,2,2,16,128]{4,3,2,1,0:T(8,128)S(1)} %ghost_pack.1), channel_id=1, source_target_pairs={{24,12},{12,24},{25,13},{13,25},{26,14},{14,26},{27,15},{15,27}} | collective-permute-start | bytes 393224 | tf_op jit(solution)/shard_map/ppermute | solution.py:622
  16.3 1.5 %first_chain.1 = (f32[8,64,128]{2,1,0:T(8,128)S(1)}, f32[2,64,128]{2,1,0:T(8,128)S(1)}, f32[32,128]{1,0:T(8,128)S(1)}, f32[40,128]{1,0:T(8,128)S(1)}, f32[48,128]{1,0:T(8,128)S(1)}) custom-call(f32[2,2,64,128]{3,2,1,0:T(8,128)S(1)} %get-tuple-element.40.refs_0_, f32[2,2,64,128]{3,2,1,0:T(8,128)S(1)} %collective-permute-done.refs_1_, ...), custom_call_target="tpu_custom_call" | custom-call | tf_op jit(solution)/shard_map/first_chain/pallas_call | solution.py:551
  17.8 3.7 %collective-permute-start.7 = (f32[48,128]{1,0:T(8,128)S(1)}, f32[48,128]{1,0:T(8,128)S(1)}, u32[]{:S(2)}, u32[]{:S(2)}) collective-permute-start(f32[48,128]{1,0:T(8,128)S(1)} %get-tuple-element.49), channel_id=1, source_target_pairs={{0,3},{1,2},{2,1},{3,0},{4,7},{5,6},{6,5},{7,4},{8,11},{9,10},{10,... | collective-permute-start | bytes 73736 | tf_op jit(solution)/shard_map/ppermute | solution.py:571
  21.5 0.8 %collective-permute-start.5 = (f32[32,128]{1,0:T(8,128)S(1)}, f32[32,128]{1,0:T(8,128)S(1)}, u32[]{:S(2)}, u32[]{:S(2)}) collective-permute-start(f32[32,128]{1,0:T(8,128)S(1)} %get-tuple-element.47.refs_0_), channel_id=1, source_target_pairs={{0,1},{1,0},{2,3},{3,2},{4,5},{5,4},{6,7},{7,6},{8,9},{9,8},{10,11... | collective-permute-start | bytes 49160 | tf_op jit(solution)/shard_map/ppermute | solution.py:571
  22.2 3.0 %collective-permute-done.5.refs_1_ = f32[32,128]{1,0:T(8,128)S(1)} collective-permute-done((f32[32,128]{1,0:T(8,128)S(1)}, f32[32,128]{1,0:T(8,128)S(1)}, u32[]{:S(2)}, u32[]{:S(2)}) %collective-permute-start.5) | collective-permute-done | bytes 16416 | tf_op jit(solution)/shard_map/ppermute | solution.py:571
  25.2 0.9 %collective-permute-done.6.refs_2_ = f32[40,128]{1,0:T(8,128)S(1)} collective-permute-done((f32[40,128]{1,0:T(8,128)S(1)}, f32[40,128]{1,0:T(8,128)S(1)}, u32[]{:S(2)}, u32[]{:S(2)}) %collective-permute-start.6) | collective-permute-done | bytes 20512 | tf_op jit(solution)/shard_map/ppermute | solution.py:571
  26.1 2.3 %next_chain.4 = (f32[8,64,128]{2,1,0:T(8,128)S(1)}, f32[8,64,128]{2,1,0:T(8,128)S(1)}, f32[64,128]{1,0:T(8,128)S(1)}, f32[2,64,128]{2,1,0:T(8,128)S(1)}, f32[8,1...) custom-call(f32[32,128]{1,0:T(8,128)S(1)} %get-tuple-element.47.refs, ...), custom_call_target="tpu_custom_call", output_to_operand_aliasing={{0}: (6, {})} | custom-call | tf_op jit(solution)/shard_map/next_chain/pallas_call | solution.py:551
  28.5 1.5 %collective-permute-start.10 = (f32[24,128]{1,0:T(8,128)S(1)}, f32[24,128]{1,0:T(8,128)S(1)}, u32[]{:S(2)}, u32[]{:S(2)}) collective-permute-start(f32[24,128]{1,0:T(8,128)S(1)} %get-tuple-element.55), channel_id=1, source_target_pairs={{0,3},{1,2},{2,1},{3,0},{4,7},{5,6},{6,5},{7,4},{8,11},{9,10},{10,... | collective-permute-start | bytes 36872 | tf_op jit(solution)/shard_map/ppermute | solution.py:571
  30.6 2.3 %collective-permute-start.8 = (f32[8,128]{1,0:T(8,128)S(1)}, f32[8,128]{1,0:T(8,128)S(1)}, u32[]{:S(2)}, u32[]{:S(2)}) collective-permute-start(f32[8,128]{1,0:T(8,128)S(1)} %get-tuple-element.53.refs_0_), channel_id=1, source_target_pairs={{0,1},{1,0},{2,3},{3,2},{4,5},{5,4},{6,7},{7,6},{8,9},{9,8},{10,11... | collective-permute-start | bytes 12296 | tf_op jit(solution)/shard_map/ppermute | solution.py:571
  32.9 1.6 %collective-permute-done.8.refs_1_ = f32[8,128]{1,0:T(8,128)S(1)} collective-permute-done((f32[8,128]{1,0:T(8,128)S(1)}, f32[8,128]{1,0:T(8,128)S(1)}, u32[]{:S(2)}, u32[]{:S(2)}) %collective-permute-start.8) | collective-permute-done | bytes 4128 | tf_op jit(solution)/shard_map/ppermute | solution.py:571
  34.5 2.7 %next_chain.5 = (f32[8,64,128]{2,1,0:T(8,128)S(1)}, f32[8,64,128]{2,1,0:T(8,128)S(1)}, f32[64,128]{1,0:T(8,128)S(1)}, f32[2,64,128]{2,1,0:T(8,128)S(1)}, f32[8,1...) custom-call(f32[8,128]{1,0:T(8,128)S(1)} %get-tuple-element.53.refs_, ...), custom_call_target="tpu_custom_call", output_to_operand_aliasing={{0}: (6, {}), {1}: (9, {})} | custom-call | tf_op jit(solution)/shard_map/next_chain/pallas_call | solution.py:551
  37.3 2.6 %collective-permute-start.13 = (f32[24,128]{1,0:T(8,128)S(1)}, f32[24,128]{1,0:T(8,128)S(1)}, u32[]{:S(2)}, u32[]{:S(2)}) collective-permute-start(f32[24,128]{1,0:T(8,128)S(1)} %get-tuple-element.63), channel_id=1, source_target_pairs={{0,3},{1,2},{2,1},{3,0},{4,7},{5,6},{6,5},{7,4},{8,11},{9,10},{10,... | collective-permute-start | bytes 36872 | tf_op jit(solution)/shard_map/ppermute | solution.py:571
  39.8 1.0 %collective-permute-start.12 = (f32[16,128]{1,0:T(8,128)S(1)}, f32[16,128]{1,0:T(8,128)S(1)}, u32[]{:S(2)}, u32[]{:S(2)}) collective-permute-start(f32[16,128]{1,0:T(8,128)S(1)} %get-tuple-element.62), channel_id=1, source_target_pairs={{0,2},{1,3},{2,0},{3,1},{4,6},{5,7},{6,4},{7,5},{8,10},{9,11},{10,... | collective-permute-start | bytes 24584 | tf_op jit(solution)/shard_map/ppermute | solution.py:571
  40.8 0.9 %collective-permute-start.11 = (f32[8,128]{1,0:T(8,128)S(1)}, f32[8,128]{1,0:T(8,128)S(1)}, u32[]{:S(2)}, u32[]{:S(2)}) collective-permute-start(f32[8,128]{1,0:T(8,128)S(1)} %get-tuple-element.61.refs_0_), channel_id=1, source_target_pairs={{0,1},{1,0},{2,3},{3,2},{4,5},{5,4},{6,7},{7,6},{8,9},{9,8},{10,11... | collective-permute-start | bytes 12296 | tf_op jit(solution)/shard_map/ppermute | solution.py:571
  41.7 2.7 %collective-permute-done.11.refs_1_ = f32[8,128]{1,0:T(8,128)S(1)} collective-permute-done((f32[8,128]{1,0:T(8,128)S(1)}, f32[8,128]{1,0:T(8,128)S(1)}, u32[]{:S(2)}, u32[]{:S(2)}) %collective-permute-start.11) | collective-permute-done | bytes 4128 | tf_op jit(solution)/shard_map/ppermute | solution.py:571
  44.5 2.3 %next_chain.6 = (f32[8,64,128]{2,1,0:T(8,128)S(1)}, f32[8,64,128]{2,1,0:T(8,128)S(1)}, f32[64,128]{1,0:T(8,128)S(1)}, f32[2,64,128]{2,1,0:T(8,128)S(1)}, f32[8,1...) custom-call(f32[8,128]{1,0:T(8,128)S(1)} %get-tuple-element.61.refs_, ...), custom_call_target="tpu_custom_call", output_to_operand_aliasing={{0}: (6, {}), {1}: (9, {})} | custom-call | tf_op jit(solution)/shard_map/next_chain/pallas_call | solution.py:551
  46.8 1.4 %collective-permute-start.16 = (f32[24,128]{1,0:T(8,128)S(1)}, f32[24,128]{1,0:T(8,128)S(1)}, u32[]{:S(2)}, u32[]{:S(2)}) collective-permute-start(f32[24,128]{1,0:T(8,128)S(1)} %get-tuple-element.70), channel_id=1, source_target_pairs={{0,3},{1,2},{2,1},{3,0},{4,7},{5,6},{6,5},{7,4},{8,11},{9,10},{10,... | collective-permute-start | bytes 36872 | tf_op jit(solution)/shard_map/ppermute | solution.py:571
  48.2 1.0 %collective-permute-start.15 = (f32[16,128]{1,0:T(8,128)S(1)}, f32[16,128]{1,0:T(8,128)S(1)}, u32[]{:S(2)}, u32[]{:S(2)}) collective-permute-start(f32[16,128]{1,0:T(8,128)S(1)} %get-tuple-element.69), channel_id=1, source_target_pairs={{0,2},{1,3},{2,0},{3,1},{4,6},{5,7},{6,4},{7,5},{8,10},{9,11},{10,... | collective-permute-start | bytes 24584 | tf_op jit(solution)/shard_map/ppermute | solution.py:571
  49.2 2.0 %collective-permute-start.14 = (f32[8,128]{1,0:T(8,128)S(1)}, f32[8,128]{1,0:T(8,128)S(1)}, u32[]{:S(2)}, u32[]{:S(2)}) collective-permute-start(f32[8,128]{1,0:T(8,128)S(1)} %get-tuple-element.68.refs_0_), channel_id=1, source_target_pairs={{0,1},{1,0},{2,3},{3,2},{4,5},{5,4},{6,7},{7,6},{8,9},{9,8},{10,11... | collective-permute-start | bytes 12296 | tf_op jit(solution)/shard_map/ppermute | solution.py:571
  51.2 1.6 %collective-permute-done.14.refs_1_ = f32[8,128]{1,0:T(8,128)S(1)} collective-permute-done((f32[8,128]{1,0:T(8,128)S(1)}, f32[8,128]{1,0:T(8,128)S(1)}, u32[]{:S(2)}, u32[]{:S(2)}) %collective-permute-start.14) | collective-permute-done | bytes 4128 | tf_op jit(solution)/shard_map/ppermute | solution.py:571
  52.8 3.1 %next_chain.7 = f32[8,32,128]{2,1,0:T(8,128)S(1)} custom-call(f32[8,128]{1,0:T(8,128)S(1)} %get-tuple-element.68.refs_0_, f32[8,128]{1,0:T(8,128)S(1)} %collective-permute-done.14.refs_1_, f32[16,128]{1,0:T(8,128)S(1)} %collective-permute-done.15.refs_2_, f32[24,128]{1,0:T(8,128)S(1)} %collective-permute-done.16.refs_3_, f32[8192,128]{1,0:T(8,128)} %copy-done, ...), custom_call_target="tpu_custom_call" | custom-call | tf_op jit(solution)/shard_map/next_chain/pallas_call | solution.py:551
  55.9 1.4 %collective-permute-start.19 = (f32[2,32,128]{2,1,0:T(8,128)S(1)}, f32[2,32,128]{2,1,0:T(8,128)S(1)}, u32[]{:S(2)}, u32[]{:S(2)}) collective-permute-start(f32[2,32,128]{2,1,0:T(8,128)S(1)} %get-tuple-element.75), channel_id=1, source_target_pairs={{0,24},{8,16},{16,8},{24,0},{1,25},{9,17},{17,9},{25,1},{2,26},{10... | collective-permute-start | bytes 98312 | tf_op jit(solution)/shard_map/ppermute | solution.py:571
  57.9 1.8 %collective-permute-done.19.refs_3_ = f32[2,32,128]{2,1,0:T(8,128)S(1)} collective-permute-done((f32[2,32,128]{2,1,0:T(8,128)S(1)}, f32[2,32,128]{2,1,0:T(8,128)S(1)}, u32[]{:S(2)}, u32[]{:S(2)}) %collective-permute-start.19) | collective-permute-done | bytes 32800 | tf_op jit(solution)/shard_map/ppermute | solution.py:571
  59.6 1.6 %collective-permute-done.18.refs_2_ = f32[2,32,128]{2,1,0:T(8,128)S(1)} collective-permute-done((f32[2,32,128]{2,1,0:T(8,128)S(1)}, f32[2,32,128]{2,1,0:T(8,128)S(1)}, u32[]{:S(2)}, u32[]{:S(2)}) %collective-permute-start.18) | collective-permute-done | bytes 32800 | tf_op jit(solution)/shard_map/ppermute | solution.py:571
  61.2 0.7 %finish.1 = f32[2,128,128]{2,1,0:T(8,128)} custom-call(f32[2,128,128]{2,1,0:T(8,128)S(1)} %copy-done.1, f32[2,32,128]{2,1,0:T(8,128)S(1)} %get-tuple-element.78.refs_0_, f32[2,32,128]{2,1,0:T(8,128)S(1)} %collective-permute-done.17.refs_1_, f32[2,32,128]{2,1,0:T(8,128)S(1)} %collective-permute-done.18.refs_2_, f32[2,32,128]{2,1,0:T(8,128)S(1)} %collective-permute-done.19.refs_3_), custom_call_target="tpu_custom_call" | custom-call | tf_op jit(solution)/shard_map/finish/pallas_call | solution.py:551
  (26 shorter events, 1.5 us)
Async XLA Ops:
  1.2 14.8 %collective-permute-start.4 = (f32[16,128,128]{2,1,0:T(8,128)S(1)}, f32[16,128,128]{2,1,0:T(8,128)S(1)}, u32[]{:S(2)}, u32[]{:S(2)}) collective-permute-start(f32[16,128,128]{2,1,0:T(8,128)S(1)} %tail.1), channel_id=1, source_target_pairs={{8,12},{28,24},{9,13},{29,25},{10,14},{30,26},{11,15},{31,27}} | collective-permute-start | bytes 3145736 | tf_op jit(solution)/shard_map/ppermute | solution.py:606
  3.3 12.0 %collective-permute-start = (f32[2,2,64,128]{3,2,1,0:T(8,128)S(1)}, f32[2,2,64,128]{3,2,1,0:T(8,128)S(1)}, u32[]{:S(2)}, u32[]{:S(2)}) collective-permute-start(f32[2,2,64,128]{3,2,1,0:T(8,128)S(1)} %get-tuple-element.41), channel_id=1, source_target_pairs={{0,8},{8,0},{16,24},{24,16},{1,9},{9,1},{17,25},{25,17},{2,10},{10... | collective-permute-start | bytes 393224 | tf_op jit(solution)/shard_map/ppermute | solution.py:571
  7.1 8.2 %collective-permute-start.1 = (f32[2,2,64,128]{3,2,1,0:T(8,128)S(1)}, f32[2,2,64,128]{3,2,1,0:T(8,128)S(1)}, u32[]{:S(2)}, u32[]{:S(2)}) collective-permute-start(f32[2,2,64,128]{3,2,1,0:T(8,128)S(1)} %get-tuple-element.42), channel_id=1, source_target_pairs={{0,16},{8,24},{16,0},{24,8},{1,17},{9,25},{17,1},{25,9},{2,18},{10... | collective-permute-start | bytes 393224 | tf_op jit(solution)/shard_map/ppermute | solution.py:571
  7.1 8.2 %collective-permute-start.2 = (f32[2,2,64,128]{3,2,1,0:T(8,128)S(1)}, f32[2,2,64,128]{3,2,1,0:T(8,128)S(1)}, u32[]{:S(2)}, u32[]{:S(2)}) collective-permute-start(f32[2,2,64,128]{3,2,1,0:T(8,128)S(1)} %get-tuple-element.43), channel_id=1, source_target_pairs={{0,24},{8,16},{16,8},{24,0},{1,25},{9,17},{17,9},{25,1},{2,26},{10... | collective-permute-start | bytes 393224 | tf_op jit(solution)/shard_map/ppermute | solution.py:571
  15.3 0.9 %collective-permute-start.3 = (f32[4,2,2,16,128]{4,3,2,1,0:T(8,128)S(1)}, f32[4,2,2,16,128]{4,3,2,1,0:T(8,128)S(1)}, u32[]{:S(2)}, u32[]{:S(2)}) collective-permute-start(f32[4,2,2,16,128]{4,3,2,1,0:T(8,128)S(1)} %ghost_pack.1), channel_id=1, source_target_pairs={{24,12},{12,24},{25,13},{13,25},{26,14},{14,26},{27,15},{15,27}} | collective-permute-start | bytes 393224 | tf_op jit(solution)/shard_map/ppermute | solution.py:622
  16.0 28.4 %copy-start = (f32[8192,128]{1,0:T(8,128)}, f32[8192,128]{1,0:T(8,128)S(1)}, u32[]{:S(2)}) copy-start(f32[8192,128]{1,0:T(8,128)S(1)} %patch.1.b_ref.refs_5_.refs_4_) | copy-start | bytes 12582916
  17.8 8.4 %collective-permute-start.7 = (f32[48,128]{1,0:T(8,128)S(1)}, f32[48,128]{1,0:T(8,128)S(1)}, u32[]{:S(2)}, u32[]{:S(2)}) collective-permute-start(f32[48,128]{1,0:T(8,128)S(1)} %get-tuple-element.49), channel_id=1, source_target_pairs={{0,3},{1,2},{2,1},{3,0},{4,7},{5,6},{6,5},{7,4},{8,11},{9,10},{10,... | collective-permute-start | bytes 73736 | tf_op jit(solution)/shard_map/ppermute | solution.py:571
  21.5 4.7 %collective-permute-start.6 = (f32[40,128]{1,0:T(8,128)S(1)}, f32[40,128]{1,0:T(8,128)S(1)}, u32[]{:S(2)}, u32[]{:S(2)}) collective-permute-start(f32[40,128]{1,0:T(8,128)S(1)} %get-tuple-element.48), channel_id=1, source_target_pairs={{0,2},{1,3},{2,0},{3,1},{4,6},{5,7},{6,4},{7,5},{8,10},{9,11},{10,... | collective-permute-start | bytes 61448 | tf_op jit(solution)/shard_map/ppermute | solution.py:571
  21.5 3.7 %collective-permute-start.5 = (f32[32,128]{1,0:T(8,128)S(1)}, f32[32,128]{1,0:T(8,128)S(1)}, u32[]{:S(2)}, u32[]{:S(2)}) collective-permute-start(f32[32,128]{1,0:T(8,128)S(1)} %get-tuple-element.47.refs_0_), channel_id=1, source_target_pairs={{0,1},{1,0},{2,3},{3,2},{4,5},{5,4},{6,7},{7,6},{8,9},{9,8},{10,11... | collective-permute-start | bytes 49160 | tf_op jit(solution)/shard_map/ppermute | solution.py:571
  28.5 6.1 %collective-permute-start.10 = (f32[24,128]{1,0:T(8,128)S(1)}, f32[24,128]{1,0:T(8,128)S(1)}, u32[]{:S(2)}, u32[]{:S(2)}) collective-permute-start(f32[24,128]{1,0:T(8,128)S(1)} %get-tuple-element.55), channel_id=1, source_target_pairs={{0,3},{1,2},{2,1},{3,0},{4,7},{5,6},{6,5},{7,4},{8,11},{9,10},{10,... | collective-permute-start | bytes 36872 | tf_op jit(solution)/shard_map/ppermute | solution.py:571
  29.9 4.6 %collective-permute-start.9 = (f32[16,128]{1,0:T(8,128)S(1)}, f32[16,128]{1,0:T(8,128)S(1)}, u32[]{:S(2)}, u32[]{:S(2)}) collective-permute-start(f32[16,128]{1,0:T(8,128)S(1)} %get-tuple-element.54), channel_id=1, source_target_pairs={{0,2},{1,3},{2,0},{3,1},{4,6},{5,7},{6,4},{7,5},{8,10},{9,11},{10,... | collective-permute-start | bytes 24584 | tf_op jit(solution)/shard_map/ppermute | solution.py:571
  30.6 4.0 %collective-permute-start.8 = (f32[8,128]{1,0:T(8,128)S(1)}, f32[8,128]{1,0:T(8,128)S(1)}, u32[]{:S(2)}, u32[]{:S(2)}) collective-permute-start(f32[8,128]{1,0:T(8,128)S(1)} %get-tuple-element.53.refs_0_), channel_id=1, source_target_pairs={{0,1},{1,0},{2,3},{3,2},{4,5},{5,4},{6,7},{7,6},{8,9},{9,8},{10,11... | collective-permute-start | bytes 12296 | tf_op jit(solution)/shard_map/ppermute | solution.py:571
  37.3 7.2 %collective-permute-start.13 = (f32[24,128]{1,0:T(8,128)S(1)}, f32[24,128]{1,0:T(8,128)S(1)}, u32[]{:S(2)}, u32[]{:S(2)}) collective-permute-start(f32[24,128]{1,0:T(8,128)S(1)} %get-tuple-element.63), channel_id=1, source_target_pairs={{0,3},{1,2},{2,1},{3,0},{4,7},{5,6},{6,5},{7,4},{8,11},{9,10},{10,... | collective-permute-start | bytes 36872 | tf_op jit(solution)/shard_map/ppermute | solution.py:571
  39.8 4.6 %collective-permute-start.12 = (f32[16,128]{1,0:T(8,128)S(1)}, f32[16,128]{1,0:T(8,128)S(1)}, u32[]{:S(2)}, u32[]{:S(2)}) collective-permute-start(f32[16,128]{1,0:T(8,128)S(1)} %get-tuple-element.62), channel_id=1, source_target_pairs={{0,2},{1,3},{2,0},{3,1},{4,6},{5,7},{6,4},{7,5},{8,10},{9,11},{10,... | collective-permute-start | bytes 24584 | tf_op jit(solution)/shard_map/ppermute | solution.py:571
  40.8 3.6 %collective-permute-start.11 = (f32[8,128]{1,0:T(8,128)S(1)}, f32[8,128]{1,0:T(8,128)S(1)}, u32[]{:S(2)}, u32[]{:S(2)}) collective-permute-start(f32[8,128]{1,0:T(8,128)S(1)} %get-tuple-element.61.refs_0_), channel_id=1, source_target_pairs={{0,1},{1,0},{2,3},{3,2},{4,5},{5,4},{6,7},{7,6},{8,9},{9,8},{10,11... | collective-permute-start | bytes 12296 | tf_op jit(solution)/shard_map/ppermute | solution.py:571
  44.5 16.7 %copy-start.1 = (f32[2,128,128]{2,1,0:T(8,128)S(1)}, f32[2,128,128]{2,1,0:T(8,128)}, u32[]{:S(2)}) copy-start(f32[2,128,128]{2,1,0:T(8,128)} %v_ref.3) | copy-start | bytes 393220
  46.8 6.1 %collective-permute-start.16 = (f32[24,128]{1,0:T(8,128)S(1)}, f32[24,128]{1,0:T(8,128)S(1)}, u32[]{:S(2)}, u32[]{:S(2)}) collective-permute-start(f32[24,128]{1,0:T(8,128)S(1)} %get-tuple-element.70), channel_id=1, source_target_pairs={{0,3},{1,2},{2,1},{3,0},{4,7},{5,6},{6,5},{7,4},{8,11},{9,10},{10,... | collective-permute-start | bytes 36872 | tf_op jit(solution)/shard_map/ppermute | solution.py:571
  48.2 4.6 %collective-permute-start.15 = (f32[16,128]{1,0:T(8,128)S(1)}, f32[16,128]{1,0:T(8,128)S(1)}, u32[]{:S(2)}, u32[]{:S(2)}) collective-permute-start(f32[16,128]{1,0:T(8,128)S(1)} %get-tuple-element.69), channel_id=1, source_target_pairs={{0,2},{1,3},{2,0},{3,1},{4,6},{5,7},{6,4},{7,5},{8,10},{9,11},{10,... | collective-permute-start | bytes 24584 | tf_op jit(solution)/shard_map/ppermute | solution.py:571
  49.2 3.6 %collective-permute-start.14 = (f32[8,128]{1,0:T(8,128)S(1)}, f32[8,128]{1,0:T(8,128)S(1)}, u32[]{:S(2)}, u32[]{:S(2)}) collective-permute-start(f32[8,128]{1,0:T(8,128)S(1)} %get-tuple-element.68.refs_0_), channel_id=1, source_target_pairs={{0,1},{1,0},{2,3},{3,2},{4,5},{5,4},{6,7},{7,6},{8,9},{9,8},{10,11... | collective-permute-start | bytes 12296 | tf_op jit(solution)/shard_map/ppermute | solution.py:571
  55.9 3.7 %collective-permute-start.19 = (f32[2,32,128]{2,1,0:T(8,128)S(1)}, f32[2,32,128]{2,1,0:T(8,128)S(1)}, u32[]{:S(2)}, u32[]{:S(2)}) collective-permute-start(f32[2,32,128]{2,1,0:T(8,128)S(1)} %get-tuple-element.75), channel_id=1, source_target_pairs={{0,24},{8,16},{16,8},{24,0},{1,25},{9,17},{17,9},{25,1},{2,26},{10... | collective-permute-start | bytes 98312 | tf_op jit(solution)/shard_map/ppermute | solution.py:571
  57.3 3.9 %collective-permute-start.18 = (f32[2,32,128]{2,1,0:T(8,128)S(1)}, f32[2,32,128]{2,1,0:T(8,128)S(1)}, u32[]{:S(2)}, u32[]{:S(2)}) collective-permute-start(f32[2,32,128]{2,1,0:T(8,128)S(1)} %get-tuple-element.76), channel_id=1, source_target_pairs={{0,16},{8,24},{16,0},{24,8},{1,17},{9,25},{17,1},{25,9},{2,18},{10... | collective-permute-start | bytes 98312 | tf_op jit(solution)/shard_map/ppermute | solution.py:571
  57.4 3.8 %collective-permute-start.17 = (f32[2,32,128]{2,1,0:T(8,128)S(1)}, f32[2,32,128]{2,1,0:T(8,128)S(1)}, u32[]{:S(2)}, u32[]{:S(2)}) collective-permute-start(f32[2,32,128]{2,1,0:T(8,128)S(1)} %get-tuple-element.77), channel_id=1, source_target_pairs={{0,8},{8,0},{16,24},{24,16},{1,9},{9,1},{17,25},{25,17},{2,10},{10... | collective-permute-start | bytes 98312 | tf_op jit(solution)/shard_map/ppermute | solution.py:571

commit v6 on v5

--- a/solution.py
+++ b/solution.py
@@ -679,7 +679,7 @@
     turned = LANES * HALF * LANES * 4
     if late:
         turn, sources = strip_kernel, [block_inverse]
-        window, sems = (HALF, LANES, LANES), (4, 2, HALF // ghost)
+        window, sems = (HALF, LANES, LANES), (8, 2, HALF // ghost)
     else:
         turn, sources = layout_kernel, [rows, beyond]
         window, sems = (HALF * LANES, LANES), (HALF // math.gcd(own, ghost),)

time: 62.1 us -> 62.1 us (level)
  transfers between devices with their start and end apart: 20 -> 20, of which waited for: 7 -> 7; matrix products, arithmetic and copies ran while one was open for 0% -> 0% of each run, Pallas kernels for 13% -> 14%
where the time goes in v6:
time: 62.1 us; the launch traced here: 61.9 us
  starting transfers between devices  26.4 us (43%)
  Pallas kernels  22.2 us (36%)
  waiting for transfers between devices  13.1 us (21%)
    ppermute x18, starting transfers between devices, to_peers(): got[k] = lax.ppermute(pieces[k], axis, [(i, i ^ k) for i in range(count)])  25 us
    pallas_call x9, Pallas kernels, call(): pl.pallas_call(kernel, out_shape=outs, in_specs=[HBM if n in hbm else VME...  15.1 us
    ppermute x18, waiting for transfers between devices, to_peers(): got[k] = lax.ppermute(pieces[k], axis, [(i, i ^ k) for i in range(count)])  13.1 us
    pallas_call x1, Pallas kernels, body(): pl.pallas_call(functools.partial(turn, own, ghost, 'gz'), out_shape=f32(L...  4.56 us
    pallas_call x1, Pallas kernels, body(): pl.pallas_call(functools.partial(pack_kernel, 'gz', own, ghost), out_shap...  1.3 us
  transfers between devices with their start and end apart: 20, of which 7 were waited for; matrix products, arithmetic and copies ran while one was open for 0% of the time, Pallas kernels for 14%

profile of v6, /device:TPU:0, one launch (start us, length us, event | category | flops | bytes accessed | tf_op | source)
XLA Modules:
  0.0 61.9 jit_solution(4420986462515003054)
XLA Ops:
  0.0 1.2 %tail.1 = f32[16,128,128]{2,1,0:T(8,128)S(1)} custom-call(f32[128,128,128]{2,1,0:T(8,128)} %b_ref.3), custom_call_target="tpu_custom_call" | custom-call | tf_op jit(solution)/shard_map/tail/pallas_call | solution.py:651
  1.2 0.7 %collective-permute-start.4 = (f32[16,128,128]{2,1,0:T(8,128)S(1)}, f32[16,128,128]{2,1,0:T(8,128)S(1)}, u32[]{:S(2)}, u32[]{:S(2)}) collective-permute-start(f32[16,128,128]{2,1,0:T(8,128)S(1)} %tail.1), channel_id=1, source_target_pairs={{8,12},{28,24},{9,13},{29,25},{10,14},{30,26},{11,15},{31,27}} | collective-permute-start | bytes 3145736 | tf_op jit(solution)/shard_map/ppermute | solution.py:606
  2.0 1.3 %pack.1 = (f32[2,2,64,128]{3,2,1,0:T(8,128)S(1)}, f32[2,2,64,128]{3,2,1,0:T(8,128)S(1)}, f32[2,2,64,128]{3,2,1,0:T(8,128)S(1)}, f32[2,2,64,128]{3,2,1,0:T(8,128)S(1)}) custom-call(f32[2,128,128]{2,1,0:T(8,128)} %v_ref.3, f32[2,128,128]{2,1,0:T(8,128)} %s_ref.1), custom_call_target="tpu_custom_call" | custom-call | tf_op jit(solution)/shard_map/pack/pallas_call | solution.py:660
  3.3 3.8 %collective-permute-start = (f32[2,2,64,128]{3,2,1,0:T(8,128)S(1)}, f32[2,2,64,128]{3,2,1,0:T(8,128)S(1)}, u32[]{:S(2)}, u32[]{:S(2)}) collective-permute-start(f32[2,2,64,128]{3,2,1,0:T(8,128)S(1)} %get-tuple-element.41), channel_id=1, source_target_pairs={{0,8},{8,0},{16,24},{24,16},{1,9},{9,1},{17,25},{25,17},{2,10},{10... | collective-permute-start | bytes 393224 | tf_op jit(solution)/shard_map/ppermute | solution.py:571
  7.1 1.4 %collective-permute-start.2 = (f32[2,2,64,128]{3,2,1,0:T(8,128)S(1)}, f32[2,2,64,128]{3,2,1,0:T(8,128)S(1)}, u32[]{:S(2)}, u32[]{:S(2)}) collective-permute-start(f32[2,2,64,128]{3,2,1,0:T(8,128)S(1)} %get-tuple-element.43), channel_id=1, source_target_pairs={{0,24},{8,16},{16,8},{24,0},{1,25},{9,17},{17,9},{25,1},{2,26},{10... | collective-permute-start | bytes 393224 | tf_op jit(solution)/shard_map/ppermute | solution.py:571
  8.5 4.6 %layout.1.b_ref.b_in = f32[8192,128]{1,0:T(8,128)S(1)} custom-call(f32[128,128,128]{2,1,0:T(8,128)} %b_ref.3), custom_call_target="tpu_custom_call" | custom-call | bytes 16777216 | tf_op jit(solution)/shard_map/layout/pallas_call | solution.py:686
  13.1 2.3 %responses.2 = (f32[24,128]{1,0:T(8,128)S(1)}, f32[8,64,128]{2,1,0:T(8,128)S(1)}) custom-call(f32[8192,128]{1,0:T(8,128)S(1)} %layout.1.b_ref.b_in), custom_call_target="tpu_custom_call" | custom-call | tf_op jit(solution)/shard_map/responses/pallas_call | solution.py:551
  16.4 1.5 %first_chain.1 = (f32[8,64,128]{2,1,0:T(8,128)S(1)}, f32[2,64,128]{2,1,0:T(8,128)S(1)}, f32[32,128]{1,0:T(8,128)S(1)}, f32[40,128]{1,0:T(8,128)S(1)}, f32[48,128]{1,0:T(8,128)S(1)}) custom-call(f32[2,2,64,128]{3,2,1,0:T(8,128)S(1)} %get-tuple-element.40.refs_0_, f32[2,2,64,128]{3,2,1,0:T(8,128)S(1)} %collective-permute-done.refs_1_, ...), custom_call_target="tpu_custom_call" | custom-call | tf_op jit(solution)/shard_map/first_chain/pallas_call | solution.py:551
  17.9 3.7 %collective-permute-start.7 = (f32[48,128]{1,0:T(8,128)S(1)}, f32[48,128]{1,0:T(8,128)S(1)}, u32[]{:S(2)}, u32[]{:S(2)}) collective-permute-start(f32[48,128]{1,0:T(8,128)S(1)} %get-tuple-element.49), channel_id=1, source_target_pairs={{0,3},{1,2},{2,1},{3,0},{4,7},{5,6},{6,5},{7,4},{8,11},{9,10},{10,... | collective-permute-start | bytes 73736 | tf_op jit(solution)/shard_map/ppermute | solution.py:571
  21.6 0.8 %collective-permute-start.5 = (f32[32,128]{1,0:T(8,128)S(1)}, f32[32,128]{1,0:T(8,128)S(1)}, u32[]{:S(2)}, u32[]{:S(2)}) collective-permute-start(f32[32,128]{1,0:T(8,128)S(1)} %get-tuple-element.47.refs_0_), channel_id=1, source_target_pairs={{0,1},{1,0},{2,3},{3,2},{4,5},{5,4},{6,7},{7,6},{8,9},{9,8},{10,11... | collective-permute-start | bytes 49160 | tf_op jit(solution)/shard_map/ppermute | solution.py:571
  22.4 3.0 %collective-permute-done.5.refs_1_ = f32[32,128]{1,0:T(8,128)S(1)} collective-permute-done((f32[32,128]{1,0:T(8,128)S(1)}, f32[32,128]{1,0:T(8,128)S(1)}, u32[]{:S(2)}, u32[]{:S(2)}) %collective-permute-start.5) | collective-permute-done | bytes 16416 | tf_op jit(solution)/shard_map/ppermute | solution.py:571
  25.3 0.9 %collective-permute-done.6.refs_2_ = f32[40,128]{1,0:T(8,128)S(1)} collective-permute-done((f32[40,128]{1,0:T(8,128)S(1)}, f32[40,128]{1,0:T(8,128)S(1)}, u32[]{:S(2)}, u32[]{:S(2)}) %collective-permute-start.6) | collective-permute-done | bytes 20512 | tf_op jit(solution)/shard_map/ppermute | solution.py:571
  26.3 2.3 %next_chain.4 = (f32[8,64,128]{2,1,0:T(8,128)S(1)}, f32[8,64,128]{2,1,0:T(8,128)S(1)}, f32[64,128]{1,0:T(8,128)S(1)}, f32[2,64,128]{2,1,0:T(8,128)S(1)}, f32[8,1...) custom-call(f32[32,128]{1,0:T(8,128)S(1)} %get-tuple-element.47.refs, ...), custom_call_target="tpu_custom_call", output_to_operand_aliasing={{0}: (6, {})} | custom-call | tf_op jit(solution)/shard_map/next_chain/pallas_call | solution.py:551
  28.6 1.5 %collective-permute-start.10 = (f32[24,128]{1,0:T(8,128)S(1)}, f32[24,128]{1,0:T(8,128)S(1)}, u32[]{:S(2)}, u32[]{:S(2)}) collective-permute-start(f32[24,128]{1,0:T(8,128)S(1)} %get-tuple-element.55), channel_id=1, source_target_pairs={{0,3},{1,2},{2,1},{3,0},{4,7},{5,6},{6,5},{7,4},{8,11},{9,10},{10,... | collective-permute-start | bytes 36872 | tf_op jit(solution)/shard_map/ppermute | solution.py:571
  30.1 0.7 %collective-permute-start.9 = (f32[16,128]{1,0:T(8,128)S(1)}, f32[16,128]{1,0:T(8,128)S(1)}, u32[]{:S(2)}, u32[]{:S(2)}) collective-permute-start(f32[16,128]{1,0:T(8,128)S(1)} %get-tuple-element.54), channel_id=1, source_target_pairs={{0,2},{1,3},{2,0},{3,1},{4,6},{5,7},{6,4},{7,5},{8,10},{9,11},{10,... | collective-permute-start | bytes 24584 | tf_op jit(solution)/shard_map/ppermute | solution.py:571
  30.7 2.3 %collective-permute-start.8 = (f32[8,128]{1,0:T(8,128)S(1)}, f32[8,128]{1,0:T(8,128)S(1)}, u32[]{:S(2)}, u32[]{:S(2)}) collective-permute-start(f32[8,128]{1,0:T(8,128)S(1)} %get-tuple-element.53.refs_0_), channel_id=1, source_target_pairs={{0,1},{1,0},{2,3},{3,2},{4,5},{5,4},{6,7},{7,6},{8,9},{9,8},{10,11... | collective-permute-start | bytes 12296 | tf_op jit(solution)/shard_map/ppermute | solution.py:571
  33.0 1.6 %collective-permute-done.8.refs_1_ = f32[8,128]{1,0:T(8,128)S(1)} collective-permute-done((f32[8,128]{1,0:T(8,128)S(1)}, f32[8,128]{1,0:T(8,128)S(1)}, u32[]{:S(2)}, u32[]{:S(2)}) %collective-permute-start.8) | collective-permute-done | bytes 4128 | tf_op jit(solution)/shard_map/ppermute | solution.py:571
  34.7 2.7 %next_chain.5 = (f32[8,64,128]{2,1,0:T(8,128)S(1)}, f32[8,64,128]{2,1,0:T(8,128)S(1)}, f32[64,128]{1,0:T(8,128)S(1)}, f32[2,64,128]{2,1,0:T(8,128)S(1)}, f32[8,1...) custom-call(f32[8,128]{1,0:T(8,128)S(1)} %get-tuple-element.53.refs_, ...), custom_call_target="tpu_custom_call", output_to_operand_aliasing={{0}: (6, {}), {1}: (9, {})} | custom-call | tf_op jit(solution)/shard_map/next_chain/pallas_call | solution.py:551
  37.4 2.6 %collective-permute-start.13 = (f32[24,128]{1,0:T(8,128)S(1)}, f32[24,128]{1,0:T(8,128)S(1)}, u32[]{:S(2)}, u32[]{:S(2)}) collective-permute-start(f32[24,128]{1,0:T(8,128)S(1)} %get-tuple-element.63), channel_id=1, source_target_pairs={{0,3},{1,2},{2,1},{3,0},{4,7},{5,6},{6,5},{7,4},{8,11},{9,10},{10,... | collective-permute-start | bytes 36872 | tf_op jit(solution)/shard_map/ppermute | solution.py:571
  40.0 0.9 %collective-permute-start.12 = (f32[16,128]{1,0:T(8,128)S(1)}, f32[16,128]{1,0:T(8,128)S(1)}, u32[]{:S(2)}, u32[]{:S(2)}) collective-permute-start(f32[16,128]{1,0:T(8,128)S(1)} %get-tuple-element.62), channel_id=1, source_target_pairs={{0,2},{1,3},{2,0},{3,1},{4,6},{5,7},{6,4},{7,5},{8,10},{9,11},{10,... | collective-permute-start | bytes 24584 | tf_op jit(solution)/shard_map/ppermute | solution.py:571
  40.9 1.0 %collective-permute-start.11 = (f32[8,128]{1,0:T(8,128)S(1)}, f32[8,128]{1,0:T(8,128)S(1)}, u32[]{:S(2)}, u32[]{:S(2)}) collective-permute-start(f32[8,128]{1,0:T(8,128)S(1)} %get-tuple-element.61.refs_0_), channel_id=1, source_target_pairs={{0,1},{1,0},{2,3},{3,2},{4,5},{5,4},{6,7},{7,6},{8,9},{9,8},{10,11... | collective-permute-start | bytes 12296 | tf_op jit(solution)/shard_map/ppermute | solution.py:571
  41.8 2.7 %collective-permute-done.11.refs_1_ = f32[8,128]{1,0:T(8,128)S(1)} collective-permute-done((f32[8,128]{1,0:T(8,128)S(1)}, f32[8,128]{1,0:T(8,128)S(1)}, u32[]{:S(2)}, u32[]{:S(2)}) %collective-permute-start.11) | collective-permute-done | bytes 4128 | tf_op jit(solution)/shard_map/ppermute | solution.py:571
  44.6 2.3 %next_chain.6 = (f32[8,64,128]{2,1,0:T(8,128)S(1)}, f32[8,64,128]{2,1,0:T(8,128)S(1)}, f32[64,128]{1,0:T(8,128)S(1)}, f32[2,64,128]{2,1,0:T(8,128)S(1)}, f32[8,1...) custom-call(f32[8,128]{1,0:T(8,128)S(1)} %get-tuple-element.61.refs_, ...), custom_call_target="tpu_custom_call", output_to_operand_aliasing={{0}: (6, {}), {1}: (9, {})} | custom-call | tf_op jit(solution)/shard_map/next_chain/pallas_call | solution.py:551
  46.9 1.4 %collective-permute-start.16 = (f32[24,128]{1,0:T(8,128)S(1)}, f32[24,128]{1,0:T(8,128)S(1)}, u32[]{:S(2)}, u32[]{:S(2)}) collective-permute-start(f32[24,128]{1,0:T(8,128)S(1)} %get-tuple-element.70), channel_id=1, source_target_pairs={{0,3},{1,2},{2,1},{3,0},{4,7},{5,6},{6,5},{7,4},{8,11},{9,10},{10,... | collective-permute-start | bytes 36872 | tf_op jit(solution)/shard_map/ppermute | solution.py:571
  48.3 1.0 %collective-permute-start.15 = (f32[16,128]{1,0:T(8,128)S(1)}, f32[16,128]{1,0:T(8,128)S(1)}, u32[]{:S(2)}, u32[]{:S(2)}) collective-permute-start(f32[16,128]{1,0:T(8,128)S(1)} %get-tuple-element.69), channel_id=1, source_target_pairs={{0,2},{1,3},{2,0},{3,1},{4,6},{5,7},{6,4},{7,5},{8,10},{9,11},{10,... | collective-permute-start | bytes 24584 | tf_op jit(solution)/shard_map/ppermute | solution.py:571
  49.3 2.0 %collective-permute-start.14 = (f32[8,128]{1,0:T(8,128)S(1)}, f32[8,128]{1,0:T(8,128)S(1)}, u32[]{:S(2)}, u32[]{:S(2)}) collective-permute-start(f32[8,128]{1,0:T(8,128)S(1)} %get-tuple-element.68.refs_0_), channel_id=1, source_target_pairs={{0,1},{1,0},{2,3},{3,2},{4,5},{5,4},{6,7},{7,6},{8,9},{9,8},{10,11... | collective-permute-start | bytes 12296 | tf_op jit(solution)/shard_map/ppermute | solution.py:571
  51.3 1.6 %collective-permute-done.14.refs_1_ = f32[8,128]{1,0:T(8,128)S(1)} collective-permute-done((f32[8,128]{1,0:T(8,128)S(1)}, f32[8,128]{1,0:T(8,128)S(1)}, u32[]{:S(2)}, u32[]{:S(2)}) %collective-permute-start.14) | collective-permute-done | bytes 4128 | tf_op jit(solution)/shard_map/ppermute | solution.py:571
  52.9 3.1 %next_chain.7 = f32[8,32,128]{2,1,0:T(8,128)S(1)} custom-call(f32[8,128]{1,0:T(8,128)S(1)} %get-tuple-element.68.refs_0_, f32[8,128]{1,0:T(8,128)S(1)} %collective-permute-done.14.refs_1_, f32[16,128]{1,0:T(8,128)S(1)} %collective-permute-done.15.refs_2_, f32[24,128]{1,0:T(8,128)S(1)} %collective-permute-done.16.refs_3_, f32[8192,128]{1,0:T(8,128)} %copy-done, ...), custom_call_target="tpu_custom_call" | custom-call | tf_op jit(solution)/shard_map/next_chain/pallas_call | solution.py:551
  56.0 1.3 %collective-permute-start.19 = (f32[2,32,128]{2,1,0:T(8,128)S(1)}, f32[2,32,128]{2,1,0:T(8,128)S(1)}, u32[]{:S(2)}, u32[]{:S(2)}) collective-permute-start(f32[2,32,128]{2,1,0:T(8,128)S(1)} %get-tuple-element.75), channel_id=1, source_target_pairs={{0,24},{8,16},{16,8},{24,0},{1,25},{9,17},{17,9},{25,1},{2,26},{10... | collective-permute-start | bytes 98312 | tf_op jit(solution)/shard_map/ppermute | solution.py:571
  58.0 1.8 %collective-permute-done.19.refs_3_ = f32[2,32,128]{2,1,0:T(8,128)S(1)} collective-permute-done((f32[2,32,128]{2,1,0:T(8,128)S(1)}, f32[2,32,128]{2,1,0:T(8,128)S(1)}, u32[]{:S(2)}, u32[]{:S(2)}) %collective-permute-start.19) | collective-permute-done | bytes 32800 | tf_op jit(solution)/shard_map/ppermute | solution.py:571
  59.7 1.5 %collective-permute-done.18.refs_2_ = f32[2,32,128]{2,1,0:T(8,128)S(1)} collective-permute-done((f32[2,32,128]{2,1,0:T(8,128)S(1)}, f32[2,32,128]{2,1,0:T(8,128)S(1)}, u32[]{:S(2)}, u32[]{:S(2)}) %collective-permute-start.18) | collective-permute-done | bytes 32800 | tf_op jit(solution)/shard_map/ppermute | solution.py:571
  61.2 0.7 %finish.1 = f32[2,128,128]{2,1,0:T(8,128)} custom-call(f32[2,128,128]{2,1,0:T(8,128)S(1)} %copy-done.1, f32[2,32,128]{2,1,0:T(8,128)S(1)} %get-tuple-element.78.refs_0_, f32[2,32,128]{2,1,0:T(8,128)S(1)} %collective-permute-done.17.refs_1_, f32[2,32,128]{2,1,0:T(8,128)S(1)} %collective-permute-done.18.refs_2_, f32[2,32,128]{2,1,0:T(8,128)S(1)} %collective-permute-done.19.refs_3_), custom_call_target="tpu_custom_call" | custom-call | tf_op jit(solution)/shard_map/finish/pallas_call | solution.py:551
  (26 shorter events, 1.7 us)
Async XLA Ops:
  1.2 14.9 %collective-permute-start.4 = (f32[16,128,128]{2,1,0:T(8,128)S(1)}, f32[16,128,128]{2,1,0:T(8,128)S(1)}, u32[]{:S(2)}, u32[]{:S(2)}) collective-permute-start(f32[16,128,128]{2,1,0:T(8,128)S(1)} %tail.1), channel_id=1, source_target_pairs={{8,12},{28,24},{9,13},{29,25},{10,14},{30,26},{11,15},{31,27}} | collective-permute-start | bytes 3145736 | tf_op jit(solution)/shard_map/ppermute | solution.py:606
  3.3 12.1 %collective-permute-start = (f32[2,2,64,128]{3,2,1,0:T(8,128)S(1)}, f32[2,2,64,128]{3,2,1,0:T(8,128)S(1)}, u32[]{:S(2)}, u32[]{:S(2)}) collective-permute-start(f32[2,2,64,128]{3,2,1,0:T(8,128)S(1)} %get-tuple-element.41), channel_id=1, source_target_pairs={{0,8},{8,0},{16,24},{24,16},{1,9},{9,1},{17,25},{25,17},{2,10},{10... | collective-permute-start | bytes 393224 | tf_op jit(solution)/shard_map/ppermute | solution.py:571
  7.1 8.3 %collective-permute-start.1 = (f32[2,2,64,128]{3,2,1,0:T(8,128)S(1)}, f32[2,2,64,128]{3,2,1,0:T(8,128)S(1)}, u32[]{:S(2)}, u32[]{:S(2)}) collective-permute-start(f32[2,2,64,128]{3,2,1,0:T(8,128)S(1)} %get-tuple-element.42), channel_id=1, source_target_pairs={{0,16},{8,24},{16,0},{24,8},{1,17},{9,25},{17,1},{25,9},{2,18},{10... | collective-permute-start | bytes 393224 | tf_op jit(solution)/shard_map/ppermute | solution.py:571
  7.1 8.3 %collective-permute-start.2 = (f32[2,2,64,128]{3,2,1,0:T(8,128)S(1)}, f32[2,2,64,128]{3,2,1,0:T(8,128)S(1)}, u32[]{:S(2)}, u32[]{:S(2)}) collective-permute-start(f32[2,2,64,128]{3,2,1,0:T(8,128)S(1)} %get-tuple-element.43), channel_id=1, source_target_pairs={{0,24},{8,16},{16,8},{24,0},{1,25},{9,17},{17,9},{25,1},{2,26},{10... | collective-permute-start | bytes 393224 | tf_op jit(solution)/shard_map/ppermute | solution.py:571
  15.4 0.9 %collective-permute-start.3 = (f32[4,2,2,16,128]{4,3,2,1,0:T(8,128)S(1)}, f32[4,2,2,16,128]{4,3,2,1,0:T(8,128)S(1)}, u32[]{:S(2)}, u32[]{:S(2)}) collective-permute-start(f32[4,2,2,16,128]{4,3,2,1,0:T(8,128)S(1)} %ghost_pack.1), channel_id=1, source_target_pairs={{24,12},{12,24},{25,13},{13,25},{26,14},{14,26},{27,15},{15,27}} | collective-permute-start | bytes 393224 | tf_op jit(solution)/shard_map/ppermute | solution.py:622
  16.2 28.4 %copy-start = (f32[8192,128]{1,0:T(8,128)}, f32[8192,128]{1,0:T(8,128)S(1)}, u32[]{:S(2)}) copy-start(f32[8192,128]{1,0:T(8,128)S(1)} %patch.1.b_ref.refs_5_.refs_4_) | copy-start | bytes 12582916
  17.9 8.4 %collective-permute-start.7 = (f32[48,128]{1,0:T(8,128)S(1)}, f32[48,128]{1,0:T(8,128)S(1)}, u32[]{:S(2)}, u32[]{:S(2)}) collective-permute-start(f32[48,128]{1,0:T(8,128)S(1)} %get-tuple-element.49), channel_id=1, source_target_pairs={{0,3},{1,2},{2,1},{3,0},{4,7},{5,6},{6,5},{7,4},{8,11},{9,10},{10,... | collective-permute-start | bytes 73736 | tf_op jit(solution)/shard_map/ppermute | solution.py:571
  21.6 4.7 %collective-permute-start.6 = (f32[40,128]{1,0:T(8,128)S(1)}, f32[40,128]{1,0:T(8,128)S(1)}, u32[]{:S(2)}, u32[]{:S(2)}) collective-permute-start(f32[40,128]{1,0:T(8,128)S(1)} %get-tuple-element.48), channel_id=1, source_target_pairs={{0,2},{1,3},{2,0},{3,1},{4,6},{5,7},{6,4},{7,5},{8,10},{9,11},{10,... | collective-permute-start | bytes 61448 | tf_op jit(solution)/shard_map/ppermute | solution.py:571
  21.6 3.7 %collective-permute-start.5 = (f32[32,128]{1,0:T(8,128)S(1)}, f32[32,128]{1,0:T(8,128)S(1)}, u32[]{:S(2)}, u32[]{:S(2)}) collective-permute-start(f32[32,128]{1,0:T(8,128)S(1)} %get-tuple-element.47.refs_0_), channel_id=1, source_target_pairs={{0,1},{1,0},{2,3},{3,2},{4,5},{5,4},{6,7},{7,6},{8,9},{9,8},{10,11... | collective-permute-start | bytes 49160 | tf_op jit(solution)/shard_map/ppermute | solution.py:571
  28.6 6.1 %collective-permute-start.10 = (f32[24,128]{1,0:T(8,128)S(1)}, f32[24,128]{1,0:T(8,128)S(1)}, u32[]{:S(2)}, u32[]{:S(2)}) collective-permute-start(f32[24,128]{1,0:T(8,128)S(1)} %get-tuple-element.55), channel_id=1, source_target_pairs={{0,3},{1,2},{2,1},{3,0},{4,7},{5,6},{6,5},{7,4},{8,11},{9,10},{10,... | collective-permute-start | bytes 36872 | tf_op jit(solution)/shard_map/ppermute | solution.py:571
  30.1 4.6 %collective-permute-start.9 = (f32[16,128]{1,0:T(8,128)S(1)}, f32[16,128]{1,0:T(8,128)S(1)}, u32[]{:S(2)}, u32[]{:S(2)}) collective-permute-start(f32[16,128]{1,0:T(8,128)S(1)} %get-tuple-element.54), channel_id=1, source_target_pairs={{0,2},{1,3},{2,0},{3,1},{4,6},{5,7},{6,4},{7,5},{8,10},{9,11},{10,... | collective-permute-start | bytes 24584 | tf_op jit(solution)/shard_map/ppermute | solution.py:571
  30.7 3.9 %collective-permute-start.8 = (f32[8,128]{1,0:T(8,128)S(1)}, f32[8,128]{1,0:T(8,128)S(1)}, u32[]{:S(2)}, u32[]{:S(2)}) collective-permute-start(f32[8,128]{1,0:T(8,128)S(1)} %get-tuple-element.53.refs_0_), channel_id=1, source_target_pairs={{0,1},{1,0},{2,3},{3,2},{4,5},{5,4},{6,7},{7,6},{8,9},{9,8},{10,11... | collective-permute-start | bytes 12296 | tf_op jit(solution)/shard_map/ppermute | solution.py:571
  37.4 7.2 %collective-permute-start.13 = (f32[24,128]{1,0:T(8,128)S(1)}, f32[24,128]{1,0:T(8,128)S(1)}, u32[]{:S(2)}, u32[]{:S(2)}) collective-permute-start(f32[24,128]{1,0:T(8,128)S(1)} %get-tuple-element.63), channel_id=1, source_target_pairs={{0,3},{1,2},{2,1},{3,0},{4,7},{5,6},{6,5},{7,4},{8,11},{9,10},{10,... | collective-permute-start | bytes 36872 | tf_op jit(solution)/shard_map/ppermute | solution.py:571
  40.0 4.6 %collective-permute-start.12 = (f32[16,128]{1,0:T(8,128)S(1)}, f32[16,128]{1,0:T(8,128)S(1)}, u32[]{:S(2)}, u32[]{:S(2)}) collective-permute-start(f32[16,128]{1,0:T(8,128)S(1)} %get-tuple-element.62), channel_id=1, source_target_pairs={{0,2},{1,3},{2,0},{3,1},{4,6},{5,7},{6,4},{7,5},{8,10},{9,11},{10,... | collective-permute-start | bytes 24584 | tf_op jit(solution)/shard_map/ppermute | solution.py:571
  40.9 3.7 %collective-permute-start.11 = (f32[8,128]{1,0:T(8,128)S(1)}, f32[8,128]{1,0:T(8,128)S(1)}, u32[]{:S(2)}, u32[]{:S(2)}) collective-permute-start(f32[8,128]{1,0:T(8,128)S(1)} %get-tuple-element.61.refs_0_), channel_id=1, source_target_pairs={{0,1},{1,0},{2,3},{3,2},{4,5},{5,4},{6,7},{7,6},{8,9},{9,8},{10,11... | collective-permute-start | bytes 12296 | tf_op jit(solution)/shard_map/ppermute | solution.py:571
  44.6 16.6 %copy-start.1 = (f32[2,128,128]{2,1,0:T(8,128)S(1)}, f32[2,128,128]{2,1,0:T(8,128)}, u32[]{:S(2)}) copy-start(f32[2,128,128]{2,1,0:T(8,128)} %v_ref.3) | copy-start | bytes 393220
  46.9 6.0 %collective-permute-start.16 = (f32[24,128]{1,0:T(8,128)S(1)}, f32[24,128]{1,0:T(8,128)S(1)}, u32[]{:S(2)}, u32[]{:S(2)}) collective-permute-start(f32[24,128]{1,0:T(8,128)S(1)} %get-tuple-element.70), channel_id=1, source_target_pairs={{0,3},{1,2},{2,1},{3,0},{4,7},{5,6},{6,5},{7,4},{8,11},{9,10},{10,... | collective-permute-start | bytes 36872 | tf_op jit(solution)/shard_map/ppermute | solution.py:571
  48.3 4.6 %collective-permute-start.15 = (f32[16,128]{1,0:T(8,128)S(1)}, f32[16,128]{1,0:T(8,128)S(1)}, u32[]{:S(2)}, u32[]{:S(2)}) collective-permute-start(f32[16,128]{1,0:T(8,128)S(1)} %get-tuple-element.69), channel_id=1, source_target_pairs={{0,2},{1,3},{2,0},{3,1},{4,6},{5,7},{6,4},{7,5},{8,10},{9,11},{10,... | collective-permute-start | bytes 24584 | tf_op jit(solution)/shard_map/ppermute | solution.py:571
  49.3 3.6 %collective-permute-start.14 = (f32[8,128]{1,0:T(8,128)S(1)}, f32[8,128]{1,0:T(8,128)S(1)}, u32[]{:S(2)}, u32[]{:S(2)}) collective-permute-start(f32[8,128]{1,0:T(8,128)S(1)} %get-tuple-element.68.refs_0_), channel_id=1, source_target_pairs={{0,1},{1,0},{2,3},{3,2},{4,5},{5,4},{6,7},{7,6},{8,9},{9,8},{10,11... | collective-permute-start | bytes 12296 | tf_op jit(solution)/shard_map/ppermute | solution.py:571
  56.0 3.7 %collective-permute-start.19 = (f32[2,32,128]{2,1,0:T(8,128)S(1)}, f32[2,32,128]{2,1,0:T(8,128)S(1)}, u32[]{:S(2)}, u32[]{:S(2)}) collective-permute-start(f32[2,32,128]{2,1,0:T(8,128)S(1)} %get-tuple-element.75), channel_id=1, source_target_pairs={{0,24},{8,16},{16,8},{24,0},{1,25},{9,17},{17,9},{25,1},{2,26},{10... | collective-permute-start | bytes 98312 | tf_op jit(solution)/shard_map/ppermute | solution.py:571
  57.3 3.9 %collective-permute-start.18 = (f32[2,32,128]{2,1,0:T(8,128)S(1)}, f32[2,32,128]{2,1,0:T(8,128)S(1)}, u32[]{:S(2)}, u32[]{:S(2)}) collective-permute-start(f32[2,32,128]{2,1,0:T(8,128)S(1)} %get-tuple-element.76), channel_id=1, source_target_pairs={{0,16},{8,24},{16,0},{24,8},{1,17},{9,25},{17,1},{25,9},{2,18},{10... | collective-permute-start | bytes 98312 | tf_op jit(solution)/shard_map/ppermute | solution.py:571
  57.5 3.7 %collective-permute-start.17 = (f32[2,32,128]{2,1,0:T(8,128)S(1)}, f32[2,32,128]{2,1,0:T(8,128)S(1)}, u32[]{:S(2)}, u32[]{:S(2)}) collective-permute-start(f32[2,32,128]{2,1,0:T(8,128)S(1)} %get-tuple-element.77), channel_id=1, source_target_pairs={{0,8},{8,0},{16,24},{24,16},{1,9},{9,1},{17,25},{25,17},{2,10},{10... | collective-permute-start | bytes 98312 | tf_op jit(solution)/shard_map/ppermute | solution.py:571
